TPU v7x, 32 devices: a whole 2x2x4 slice. The times are simulated.
32 devices in a mesh: dp: 16 (over z, y, core), tensor: 2 (over x).
Axes of the slice: x: 2, y: 2, z: 4, core: 2. Of those that a mesh axis runs over, the one named last changes fastest.
Arguments:
- hidden_rows: bfloat16 [1024, 16384], P('dp', 'tensor')
- norm_gain: float32 [16384], P('tensor'), may hold values from 0.5 to 1.5
- key_weight: bfloat16 [512, 16384], P('dp', 'tensor'), may hold values from -0.046875 to 0.046875
- cotangent: bfloat16 [16, 128, 512], P('dp'), may hold values from -6 to 6
- accepted_counts: int32 [16], P('dp'), may hold values from 16 to 64, as said below
- destination: int32 [1024], P('dp'), may hold values from 0 to 15, as said below
Outputs:
- keys: bfloat16 [16, 128, 512], P('dp')
- key_weight_grad: float32 [512, 16384], P('dp', 'tensor')
- gain_grad: float32 [16384], P('tensor')
Inputs may be any that keep to these rules, and one draw needn't show every extreme that they name: `accepted_counts`: rows 0 to the count minus 1 of a replica are accepted; in every draw one replica accepts all its rows and another a quarter of them. `destination`: among one replica's 64 rows no shard is named more than 8 times; in every draw one shard is named exactly 8 times by every replica, all within the first quarter of that replica's rows.
All inputs are finite; a program needn't handle non-finite values.
Results may differ from a plain program's by a relative error of at most 0.0051.
Values may be sent and summed in bfloat16 or wider, within the bound.
No kernel may reach another device: no remote copies, remote signals or barrier semaphores. Data moves between devices by JAX's collectives and lax.ppermute only.
A program may use at most 64 MiB of HBM per device.

v0:
```python
import math

import jax
import jax.numpy as jnp
from jax import lax
from jax.sharding import PartitionSpec as P

D = 16384


EPSILON = 1e-05


def slot_layout(dest_rows, count, groups, capacity):
    row_total = dest_rows.shape[0]
    row_order = lax.broadcasted_iota(jnp.int32, (row_total,), 0)
    onehot = (dest_rows[:, None] == lax.broadcasted_iota(jnp.int32, (row_total, groups), 1)).astype(
        jnp.int32
    )
    before = jnp.cumsum(onehot, axis=0) - onehot
    slot_rank = jnp.sum(before * onehot, axis=1)
    accepted = row_order < count
    position = dest_rows * capacity + slot_rank
    filler = jnp.full((groups * capacity,), row_total, jnp.int32)
    filler = filler.at[jnp.where(accepted, position, groups * capacity)].set(row_order, mode="drop")
    return (accepted, position, filler)


def with_blank(source_table):
    return jnp.concatenate(
        [source_table, jnp.zeros((1, source_table.shape[1]), source_table.dtype)], axis=0
    )


def on_device(hidden_rows, norm_gain, key_weight, cotangent, accepted_counts, destination):
    replicas = lax.axis_size("dp")
    own_rows = hidden_rows.shape[0]
    capacity = 2 * own_rows // replicas
    accepted, position, filler = slot_layout(destination, accepted_counts[0], replicas, capacity)
    returned = lax.all_to_all(cotangent[0], "dp", split_axis=0, concat_axis=0, tiled=True)
    row_cot = returned[jnp.where(accepted, position, 0)]
    row_data = jnp.where(accepted[:, None], hidden_rows, jnp.zeros_like(hidden_rows))
    row_float = row_data.astype(jnp.float32)
    squares = lax.psum(jnp.sum(row_float * row_float, axis=1), "tensor")
    normed = (row_float * lax.rsqrt(squares / D + EPSILON)[:, None] * norm_gain[None, :]).astype(
        jnp.bfloat16
    )
    weights_whole = lax.all_gather(key_weight, "dp", axis=0, tiled=True)
    partial_value = lax.dot_general(
        normed, weights_whole, (((1,), (1,)), ((), ())), preferred_element_type=jnp.float32
    )
    backward = jnp.dot(row_cot, weights_whole, preferred_element_type=jnp.float32)
    row_keys = lax.psum(partial_value, "tensor").astype(jnp.bfloat16)
    key_out = lax.all_to_all(
        with_blank(row_keys)[filler], "dp", split_axis=0, concat_axis=0, tiled=True
    )
    factor = 1.0 / math.sqrt(own_rows * replicas)
    grad_weight = (
        lax.psum_scatter(
            lax.dot_general(
                row_cot, normed, (((0,), (0,)), ((), ())), preferred_element_type=jnp.float32
            ),
            "dp",
            scatter_dimension=0,
            tiled=True,
        )
        * factor
    )
    gain_term = jnp.sum(backward * normed.astype(jnp.float32), axis=0)
    grad_gain = lax.psum(gain_term, "dp") * factor / norm_gain
    return (key_out[None], grad_weight, grad_gain)


def solution(mesh):
    return jax.shard_map(
        on_device,
        mesh=mesh,
        in_specs=(
            P("dp", "tensor"),
            P("tensor"),
            P("dp", "tensor"),
            P("dp", None, None),
            P("dp"),
            P("dp"),
        ),
        out_specs=(P("dp", None, None), P("dp", "tensor"), P("tensor")),
        check_vma=False,
    )
```

profile of v0, /device:TPU:0, one launch (start us, length us, event | category | flops | bytes accessed | tf_op | source)
XLA Modules:
  0.0 278.3 jit_solution(14692922242966020250)
XLA Ops:
  7.2 0.0 copy-start
  7.2 0.0 copy-start.1
  7.2 0.0 all-gather.2.cloned.1.call-start
  7.2 0.7 all-gather.2.cloned.1.call-update
  7.9 7.4 %all-to-all-start.1 = ((bf16[16,8,512]{2,1,0:T(8,128)(2,1)}), bf16[16,8,512]{2,1,0:T(8,128)(2,1)S(1)}, u32[]{:S(2)}, u32[]{:S(2)}) async-start(bf16[16,8,512]{2,1,0:T(8,128)(2,1)} %bitcast.14), calls=%async_computation.1 | async-start | bytes 262144 | tf_op jit(solution)/shard_map/all_to_all | solution.py:40
  15.3 0.0 reduce-scatter.2.cloned.1.call-start
  16.0 0.7 fusion.4
  16.8 0.1 reduce_window_sum.11
  16.9 0.8 select_reduce_fusion
  17.7 1.7 fusion
  19.4 0.7 compare_select_fusion
  20.1 4.9 %psum.21 = f32[64]{0:T(128)S(1)} all-reduce(f32[64]{0:T(128)S(1)} %fusion), channel_id=1, replica_groups=mesh['dp'=16,'tensor'=2] {'tensor'}, use_global_device_ids=true, to_apply=%region_1.2 | all-reduce | flops 64 | bytes 512 | tf_op jit(solution)/shard_map/psum | solution.py:44
  25.0 0.0 all-to-all-done.1
  25.0 0.7 gather_fusion.1
  25.7 0.0 copy-done
  25.7 0.0 copy-done.1
  25.7 8.1 %fusion.7 = f32[512,8192]{1,0:T(8,128)} fusion(bf16[64,512]{1,0:T(8,128)(2,1)S(1)} %gather_fusion.1, f32[8192]{0:T(1024)S(1)} %copy-done.1, f32[64]{0:T(128)S(1)} %add_rsqrt_fusion, bf16[64,8192]{1,0:T(8,128)(2,1)S(1)} %copy-done, pred[64]{0:T(512)(128)(4,1)S(1)} %iota_compare_fusion.1), kind=kOutput, calls=%fused_computation.26 | convolution fusion | flops 539492352 | bytes 17924416 | tf_op jit(solution)/shard_map/dot_general | solution.py:60
  33.9 0.0 reduce-scatter.2.cloned.1.call-update
  33.9 0.8 scatter_custom_fusion
  34.7 53.1 %all-gather.2.cloned.1.call-done = bf16[512,8192]{1,0:T(8,128)(2,1)} async-done(((bf16[32,8192]{1,0:T(8,128)(2,1)}), bf16[512,8192]{1,0:T(8,128)(2,1)}) %all-gather.2.cloned.1.call-update) | async-done | bytes 8388624 | tf_op jit(solution)/shard_map/all_gather | solution.py:48
  87.8 6.1 %fusion.9 = f32[64,512]{1,0:T(8,128)S(1)} fusion(bf16[512,8192]{1,0:T(8,128)(2,1)} %all-gather.2.cloned.1.call-done, f32[8192]{0:T(1024)S(1)} %copy-done.1, f32[64]{0:T(128)S(1)} %add_rsqrt_fusion, bf16[64,8192]{1,0:T(8,128)(2,1)S(1)} %copy-done, pred[64]{0:T(512)(128)(4,1)S(1)} %iota_compare_fusion.1), kind=kOutput, calls=%fused_computation.27 | convolution fusion | flops 539492352 | bytes 9601344 | tf_op jit(solution)/shard_map/dot_general | solution.py:49
  93.9 9.7 %all-reduce.2 = bf16[64,512]{1,0:T(8,128)(2,1)S(1)} all-reduce(f32[64,512]{1,0:T(8,128)S(1)} %fusion.9), channel_id=1, replica_groups=mesh['dp'=16,'tensor'=2] {'tensor'}, use_global_device_ids=true, to_apply=%region_2.3 | all-reduce | flops 32768 | bytes 196608 | tf_op jit(solution)/shard_map/psum | solution.py:53
  103.6 1.5 gather_fusion
  105.1 3.5 %all-to-all-start = ((bf16[16,8,512]{2,1,0:T(8,128)(2,1)}), bf16[16,8,512]{2,1,0:T(8,128)(2,1)S(1)}, u32[]{:S(2)}, u32[]{:S(2)}) async-start(bf16[16,8,512]{2,1,0:T(8,128)(2,1)} %bitcast.1), calls=%async_computation | async-start | bytes 262144 | tf_op jit(solution)/shard_map/all_to_all | solution.py:54
  108.7 6.5 %fusion.3 = f32[8192]{0:T(1024)S(1)} fusion(bf16[64,512]{1,0:T(8,128)(2,1)S(1)} %gather_fusion.1, bf16[512,8192]{1,0:T(8,128)(2,1)} %all-gather.2.cloned.1.call-done, f32[8192]{0:T(1024)S(1)} %copy-done.1, f32[64]{0:T(128)S(1)} %add_rsqrt_fusion, bf16[64,8192]{1,0:T(8,128)(2,1)S(1)} %copy-done, pred[64]{0:T(512)(128)(4,1)S(1)} %iota_compare_fusion.1), kind=kOutput, calls=%fused_computation.9 | convolution fusion | flops 541057024 | bytes 9568576 | tf_op jit(solution)/shard_map/dot_general | solution.py:52
  115.2 65.5 %psum.23 = f32[8192]{0:T(1024)S(1)} all-reduce(f32[8192]{0:T(1024)S(1)} %fusion.3), channel_id=1, replica_groups=mesh['dp'=16,'tensor'=2] {'dp'}, use_global_device_ids=true, to_apply=%region_8.9 | all-reduce | flops 8192 | bytes 65536 | tf_op jit(solution)/shard_map/psum | solution.py:70
  180.7 0.6 multiply_divide_fusion
  181.3 0.0 all-to-all-done
  181.3 87.3 %reduce-scatter.2.cloned.1.call-done = f32[32,8192]{1,0:T(8,128)} async-done(((f32[512,8192]{1,0:T(8,128)}), f32[32,8192]{1,0:T(8,128)}) %reduce-scatter.2.cloned.1.call-update) | async-done | bytes 1048592 | tf_op jit(solution)/shard_map/reduce_scatter | solution.py:59
  268.6 2.3 broadcast_multiply_fusion
  270.9 0.7 copy.13
  (7 shorter events, 0.0 us)
Async XLA Ops:
  7.2 18.6 %copy-start = (bf16[64,8192]{1,0:T(8,128)(2,1)S(1)}, bf16[64,8192]{1,0:T(8,128)(2,1)}, u32[]{:S(2)}) copy-start(bf16[64,8192]{1,0:T(8,128)(2,1)} %param.6) | copy-start | bytes 3145732
  7.2 18.5 %copy-start.1 = (f32[8192]{0:T(1024)S(1)}, f32[8192]{0:T(1024)}, u32[]{:S(2)}) copy-start(f32[8192]{0:T(1024)} %param.7) | copy-start | bytes 98308
  7.2 80.7 %all-gather.2.cloned.1.call-start = ((), (), s32[]{:S(2)}) async-start(), calls=%async_computation.3 | async-start | bytes 8912896 | tf_op jit(solution)/shard_map/all_gather | solution.py:48
  7.9 17.1 %all-to-all-start.1 = ((bf16[16,8,512]{2,1,0:T(8,128)(2,1)}), bf16[16,8,512]{2,1,0:T(8,128)(2,1)S(1)}, u32[]{:S(2)}, u32[]{:S(2)}) async-start(bf16[16,8,512]{2,1,0:T(8,128)(2,1)} %bitcast.14), calls=%async_computation.1 | async-start | bytes 262144 | tf_op jit(solution)/shard_map/all_to_all | solution.py:40
  15.3 253.3 %reduce-scatter.2.cloned.1.call-start = ((), (), s32[]{:S(2)}) async-start(), calls=%async_computation.4 | async-start | bytes 17825792 | tf_op jit(solution)/shard_map/reduce_scatter | solution.py:59
  105.1 76.2 %all-to-all-start = ((bf16[16,8,512]{2,1,0:T(8,128)(2,1)}), bf16[16,8,512]{2,1,0:T(8,128)(2,1)S(1)}, u32[]{:S(2)}, u32[]{:S(2)}) async-start(bf16[16,8,512]{2,1,0:T(8,128)(2,1)} %bitcast.1), calls=%async_computation | async-start | bytes 262144 | tf_op jit(solution)/shard_map/all_to_all | solution.py:54
Sparse Core Ops, SparseCore 0:
  10.2 77.6 all-gather.1
  92.0 176.5 reduce-scatter.1
where the time goes:
time: 279 us; the launch traced here: 278 us
  waiting for transfers between devices  141 us (51%)
  blocking collectives  80.1 us (29%)
  matrix products  20.7 us (7%)
  between operations  14.8 us (5%)
  starting transfers between devices  11 us (4%)
  other arithmetic  6.93 us (2%)
  local copies, waits for them, and re-layouts  3.66 us (1%)
    reduce_scatter x1, waiting for transfers between devices, on_device(): lax.psum_scatter(lax.dot_general(row_cot, normed, (((0,), (0,)), ((), ())...  87.3 us
    psum x1, blocking collectives, on_device(): grad_gain = lax.psum(gain_term, 'dp') * factor / norm_gain  65.5 us
    all_gather x1, waiting for transfers between devices, on_device(): weights_whole = lax.all_gather(key_weight, 'dp', axis=0, tiled=True)  53.1 us
    psum x1, blocking collectives, on_device(): row_keys = lax.psum(partial_value, 'tensor').astype(jnp.bfloat16)  9.69 us
    dot_general x1, matrix products, on_device(): lax.dot_general(row_cot, normed, (((0,), (0,)), ((), ())), preferred_elem...  8.12 us
    all_to_all x1, starting transfers between devices, on_device(): lax.all_to_all(cotangent[0], 'dp', split_axis=0, concat_axis=0, tiled=True)  7.4 us
    dot_general x1, matrix products, on_device(): jnp.dot(row_cot, weights_whole, preferred_element_type=jnp.float32)  6.55 us
    dot_general x1, matrix products, on_device(): lax.dot_general(normed, weights_whole, (((1,), (1,)), ((), ())), preferre...  6.06 us
  transfers between devices with their start and end apart: 4, of which 2 were waited for; matrix products, arithmetic and copies ran while one was open for 10% of the time, Pallas kernels for 0%

commit v1 on v0

v1 whole, which is shorter than its diff:
```python
import math

import jax
import jax.numpy as jnp
from jax import lax
from jax.sharding import Mesh
from jax.sharding import PartitionSpec as P

EPSILON = 1e-05

DP = ("hi", "low")


def reduce_tensor(value):
    if lax.axis_size("tensor") == 2:
        return value + lax.ppermute(value, "tensor", [(0, 1), (1, 0)])
    return lax.psum(value, "tensor")


def slot_onehot(dest_rows, count, shards, capacity):
    rows = dest_rows.shape[0]
    order = lax.broadcasted_iota(jnp.int32, (rows, rows), 0)
    other = lax.broadcasted_iota(jnp.int32, (rows, rows), 1)
    same = (dest_rows[:, None] == dest_rows[None, :]) & (other < order)
    rank = jnp.sum(same.astype(jnp.int32), axis=1)
    accepted = lax.iota(jnp.int32, rows) < count
    position = jnp.where(accepted, dest_rows * capacity + rank, -1)
    slots = lax.broadcasted_iota(jnp.int32, (rows, shards * capacity), 1)
    return accepted, (position[:, None] == slots).astype(jnp.bfloat16)


def on_device(hidden_rows, norm_gain, key_weight, cotangent, accepted_counts, destination):
    halves, low = lax.axis_size("hi"), lax.axis_size("low")
    replicas = halves * low
    rows, width = hidden_rows.shape
    tensor = lax.axis_size("tensor")
    model_width = width * tensor
    owned, key_width = key_weight.shape[0], cotangent.shape[2]
    part = width // low
    slots = cotangent.shape[1]
    capacity = slots // replicas

    weight_parts = key_weight.reshape(owned, low, part).transpose(1, 0, 2)
    weight_parts = jnp.broadcast_to(weight_parts[None], (halves, low, owned, part))
    weights = lax.all_to_all(
        weight_parts.reshape(replicas, owned, part), DP, split_axis=0, concat_axis=0, tiled=True
    ).reshape(key_width, part)

    returned = lax.all_to_all(cotangent[0], DP, split_axis=0, concat_axis=0, tiled=True)
    accepted, onehot = slot_onehot(destination, accepted_counts[0], replicas, capacity)
    row_cot = jnp.dot(onehot, returned, preferred_element_type=jnp.float32).astype(jnp.bfloat16)

    row_float = hidden_rows.astype(jnp.float32)
    squares = reduce_tensor(jnp.sum(row_float * row_float, axis=1))
    scale = lax.rsqrt(squares / model_width + EPSILON)
    normed = jnp.where(
        accepted[:, None], row_float * scale[:, None] * norm_gain[None, :], jnp.float32(0.0)
    ).astype(jnp.bfloat16)

    sent = jnp.concatenate(
        [
            normed.reshape(rows, low, part).transpose(1, 0, 2),
            jnp.broadcast_to(row_cot[None], (low, rows, key_width)),
        ],
        axis=2,
    )
    got = lax.all_to_all(sent, "low", split_axis=0, concat_axis=0, tiled=True)
    half_normed = got[:, :, :part].reshape(low * rows, part)
    half_cot = got[:, :, part:].reshape(low * rows, key_width)

    grad_part = lax.dot_general(
        half_cot, half_normed, (((0,), (0,)), ((), ())), preferred_element_type=jnp.float32
    )
    key_part = lax.dot_general(
        half_normed, weights, (((1,), (1,)), ((), ())), preferred_element_type=jnp.float32
    )
    gain_part = jnp.sum(grad_part * weights.astype(jnp.float32), axis=0)

    factor = 1.0 / math.sqrt(rows * replicas)
    grad_terms = lax.all_to_all(
        grad_part.astype(jnp.bfloat16).reshape(replicas, owned, part),
        DP,
        split_axis=0,
        concat_axis=0,
        tiled=True,
    ).reshape(halves, low, owned, part)
    grad_weight = (
        jnp.sum(grad_terms.astype(jnp.float32), axis=0).transpose(1, 0, 2).reshape(owned, width)
        * factor
    )

    gain_terms = lax.all_to_all(
        jnp.broadcast_to(gain_part[None, None], (replicas, 1, part)),
        DP,
        split_axis=0,
        concat_axis=0,
        tiled=True,
    ).reshape(halves, width)
    grad_gain = jnp.sum(gain_terms, axis=0) * factor / norm_gain

    key_terms = lax.all_to_all(
        key_part.astype(jnp.bfloat16).reshape(low, rows, key_width),
        "low",
        split_axis=0,
        concat_axis=0,
        tiled=True,
    )
    row_keys = reduce_tensor(jnp.sum(key_terms.astype(jnp.float32), axis=0)).astype(jnp.bfloat16)
    key_slots = lax.dot_general(
        onehot, row_keys, (((0,), (0,)), ((), ())), preferred_element_type=jnp.float32
    ).astype(jnp.bfloat16)
    key_out = lax.all_to_all(key_slots, DP, split_axis=0, concat_axis=0, tiled=True)
    return (key_out[None], grad_weight, grad_gain)


def solution(mesh):
    replicas, tensor = mesh.shape["dp"], mesh.shape["tensor"]
    split = Mesh(mesh.devices.reshape(2, replicas // 2, tensor), ("hi", "low", "tensor"))
    return jax.shard_map(
        on_device,
        mesh=split,
        in_specs=(
            P(DP, "tensor"),
            P("tensor"),
            P(DP, "tensor"),
            P(DP, None, None),
            P(DP),
            P(DP),
        ),
        out_specs=(P(DP, None, None), P(DP, "tensor"), P("tensor")),
        check_vma=False,
    )
```

time: 279 us -> 144 us (0.52)
  blocking collectives: 80.1 us -> 10.5 us
  waiting for transfers between devices: 141 us -> 77.1 us
  starting transfers between devices: 11 us -> 32.8 us
  matrix products: 20.7 us -> 5.65 us
  between operations: 14.8 us -> 1.46 us
    reduce_scatter x1 -> x0, waiting for transfers between devices: 87.3 us -> none  [on_device(): lax.psum_scatter(lax.dot_general(row_cot, normed, (((0,), (0,)), ((), ())...]
    psum x3 -> x0, blocking collectives: 80.1 us -> none  [the longest x1 65.5 us: on_device(): grad_gain = lax.psum(gain_term, 'dp') * factor / norm_gain]
    all_to_all x2 -> x6, waiting for transfers between devices: 0.01 us -> 77.1 us  [the longest x1 21.9 us: on_device(): lax.all_to_all(grad_part.astype(jnp.bfloat16).reshape(replicas, owned, pa...]
    all_gather x1 -> x0, waiting for transfers between devices: 53.1 us -> none  [on_device(): weights_whole = lax.all_gather(key_weight, 'dp', axis=0, tiled=True)]
    all_to_all x2 -> x6, starting transfers between devices: 10.9 us -> 29.9 us  [the longest x1 7.4 us: on_device(): lax.all_to_all(cotangent[0], DP, split_axis=0, concat_axis=0, tiled=True)]
    dot_general x3 -> x4, matrix products: 20.7 us -> 5.65 us  [the longest x1 2.76 us: on_device(): lax.dot_general(half_normed, weights, (((1,), (1,)), ((), ())), preferred...]
    all_to_all x0 -> x1, blocking collectives: none -> 10.5 us  [on_device(): lax.all_to_all(key_slots, DP, split_axis=0, concat_axis=0, tiled=True)]
    ppermute x0 -> x2, starting transfers between devices: none -> 2.92 us  [reduce_tensor(): return value + lax.ppermute(value, 'tensor', [(0, 1), (1, 0)])]
  transfers between devices with their start and end apart: 4 -> 8, of which waited for: 2 -> 6; matrix products, arithmetic and copies ran while one was open for 10% -> 9% of each run, Pallas kernels for 0% -> 0%
where the time goes in v1:
time: 144 us; the launch traced here: 142 us
  waiting for transfers between devices  77.1 us (54%)
  starting transfers between devices  32.8 us (23%)
  blocking collectives  10.5 us (7%)
  other arithmetic  9.08 us (6%)
  matrix products  5.65 us (4%)
  local copies, waits for them, and re-layouts  5.43 us (4%)
  between operations  1.46 us (1%)
    all_to_all x1, waiting for transfers between devices, on_device(): lax.all_to_all(grad_part.astype(jnp.bfloat16).reshape(replicas, owned, pa...  21.9 us
    all_to_all x1, waiting for transfers between devices, on_device(): lax.all_to_all(weight_parts.reshape(replicas, owned, part), DP, split_axi...  21.8 us
    all_to_all x1, waiting for transfers between devices, on_device(): got = lax.all_to_all(sent, 'low', split_axis=0, concat_axis=0, tiled=True)  19.4 us
    all_to_all x1, blocking collectives, on_device(): lax.all_to_all(key_slots, DP, split_axis=0, concat_axis=0, tiled=True)  10.5 us
    all_to_all x1, starting transfers between devices, on_device(): lax.all_to_all(cotangent[0], DP, split_axis=0, concat_axis=0, tiled=True)  7.4 us
    all_to_all x1, waiting for transfers between devices, on_device(): lax.all_to_all(jnp.broadcast_to(gain_part[None, None], (replicas, 1, part...  6.59 us
    all_to_all x1, waiting for transfers between devices, on_device(): lax.all_to_all(key_part.astype(jnp.bfloat16).reshape(low, rows, key_width...  6.45 us
    all_to_all x1, starting transfers between devices, on_device(): lax.all_to_all(key_part.astype(jnp.bfloat16).reshape(low, rows, key_width...  5.89 us
  transfers between devices with their start and end apart: 8, of which 6 were waited for; matrix products, arithmetic and copies ran while one was open for 9% of the time, Pallas kernels for 0%

profile of v1, /device:TPU:0, one launch (start us, length us, event | category | flops | bytes accessed | tf_op | source)
XLA Modules:
  0.0 142.0 jit_solution(16340515660882954472)
XLA Ops:
  0.6 7.4 %all-to-all-start = ((bf16[16,8,512]{2,1,0:T(8,128)(2,1)}), bf16[16,8,512]{2,1,0:T(8,128)(2,1)S(1)}, u32[]{:S(2)}, u32[]{:S(2)}) async-start(bf16[16,8,512]{2,1,0:T(8,128)(2,1)} %bitcast.52), calls=%async_computation | async-start | bytes 262144 | tf_op jit(solution)/shard_map/all_to_all | solution.py:49
  8.0 1.5 %fusion = f32[64]{0:T(128)S(1)} fusion(bf16[64,8192]{1,0:T(8,128)(2,1)} %param.6), kind=kLoop, calls=%fused_computation.2 | loop fusion | flops 1572800 | bytes 1048832 | tf_op jit(solution)/shard_map/reduce_sum | solution.py:54
  9.6 1.6 %collective-permute-start = (f32[64]{0:T(128)S(1)}, f32[64]{0:T(128)S(1)}, u32[]{:S(2)}, u32[]{:S(2)}) collective-permute-start(f32[64]{0:T(128)S(1)} %fusion), channel_id=1, source_target_pairs={{0,1},{1,0},{2,3},{3,2},{4,5},{5,4},{6,7},{7,6},{8,9},{9,8},{10,11... | collective-permute-start | bytes 776 | tf_op jit(solution)/shard_map/ppermute | solution.py:16
  11.8 0.9 convert_reduce_fusion.2
  12.7 0.7 add_select_fusion
  13.4 0.0 collective-permute-done
  13.4 1.6 %fusion.3 = bf16[64,8192]{1,0:T(8,128)(2,1)S(1)} fusion(bf16[64,8192]{1,0:T(8,128)(2,1)} %param.6, f32[8192]{0:T(1024)} %param.7, f32[64]{0:T(128)S(1)} %add_rsqrt_fusion, pred[64]{0:T(512)(128)(4,1)S(1)} %iota_compare_fusion.4), kind=kLoop, calls=%fused_computation.5 | loop fusion | flops 2621440 | bytes 2130240 | tf_op jit(solution)/shard_map/convert_element_type | solution.py:58
  15.0 0.1 copy.27
  15.1 0.9 all-to-all-done
  16.0 0.2 convolution_convert_fusion.2
  16.2 1.3 pad_maximum_fusion
  17.5 0.0 copy-start
  17.5 3.7 %all-to-all-start.1 = ((bf16[8,64,1536]{2,1,0:T(8,128)(2,1)}), bf16[8,64,1536]{2,1,0:T(8,128)(2,1)S(1)}, u32[]{:S(2)}, u32[]{:S(2)}) async-start(bf16[8,64,1536]{2,1,0:T(8,128)(2,1)} %pad_maximum_fusion), calls=%async_computation.1 | async-start | bytes 3145728 | tf_op jit(solution)/shard_map/all_to_all | solution.py:67
  21.2 0.0 copy-done
  21.2 0.3 copy.25
  21.5 0.3 copy.21
  21.8 19.4 %all-to-all-done.1 = bf16[8,64,1536]{2,1,0:T(8,128)(2,1)S(1)} async-done(((bf16[8,64,1536]{2,1,0:T(8,128)(2,1)}), bf16[8,64,1536]{2,1,0:T(8,128)(2,1)S(1)}, u32[]{:S(2)}, u32[]{:S(2)}) %all-to-all-start.1) | async-done | bytes 1572896 | tf_op jit(solution)/shard_map/all_to_all | solution.py:67
  41.2 1.1 broadcast_in_dim.28
  42.3 4.4 %all-to-all-start.2 = ((bf16[16,32,1024]{2,1,0:T(8,128)(2,1)}), bf16[16,32,1024]{2,1,0:T(8,128)(2,1)S(1)}, u32[]{:S(2)}, u32[]{:S(2)}) async-start(bf16[16,32,1024]{2,1,0:T(8,128)(2,1)} %bitcast.43), calls=%async_computation.2 | async-start | bytes 2097152 | tf_op jit(solution)/shard_map/all_to_all | solution.py:45
  46.7 1.1 slice.8
  47.8 21.8 %all-to-all-done.2 = bf16[16,32,1024]{2,1,0:T(8,128)(2,1)S(1)} async-done(((bf16[16,32,1024]{2,1,0:T(8,128)(2,1)}), bf16[16,32,1024]{2,1,0:T(8,128)(2,1)S(1)}, u32[]{:S(2)}, u32[]{:S(2)}) %all-to-all-start.2) | async-done | bytes 1048608 | tf_op jit(solution)/shard_map/all_to_all | solution.py:45
  69.7 2.8 %convolution_convert_fusion = bf16[512,512]{1,0:T(8,128)(2,1)} fusion(bf16[512,1024]{1,0:T(8,128)(2,1)} %bitcast.48, bf16[512,1024]{1,0:T(8,128)(2,1)S(1)} %bitcast.41), kind=kOutput, calls=%fused_computation.11 | convolution fusion | flops 537133056 | bytes 2621440 | tf_op jit(solution)/shard_map/dot_general | solution.py:74
  72.4 5.9 %all-to-all-start.3 = ((bf16[8,64,512]{2,1,0:T(8,128)(2,1)}), bf16[8,64,512]{2,1,0:T(8,128)(2,1)S(1)}, u32[]{:S(2)}, u32[]{:S(2)}) async-start(bf16[8,64,512]{2,1,0:T(8,128)(2,1)} %bitcast.50), calls=%async_computation.3 | async-start | bytes 1048576 | tf_op jit(solution)/shard_map/all_to_all | solution.py:101
  78.3 2.4 %bitcast_convert_fusion = (bf16[512,1024]{1,0:T(8,128)(2,1)}, f32[512,1024,1]{1,0,2:T(8,128)}) fusion(bf16[8,64,1536]{2,1,0:T(8,128)(2,1)S(1)} %all-to-all-done.1), kind=kOutput, calls=%fused_computation.8 | convolution fusion | flops 537395200 | bytes 4718592 | tf_op jit(solution)/shard_map/dot_general | solution.py:71
  80.7 6.5 %all-to-all-done.3 = bf16[8,64,512]{2,1,0:T(8,128)(2,1)S(1)} async-done(((bf16[8,64,512]{2,1,0:T(8,128)(2,1)}), bf16[8,64,512]{2,1,0:T(8,128)(2,1)S(1)}, u32[]{:S(2)}, u32[]{:S(2)}) %all-to-all-start.3) | async-done | bytes 524320 | tf_op jit(solution)/shard_map/all_to_all | solution.py:101
  87.2 0.1 convert_reduce_fusion.1
  87.2 1.4 collective-permute-start.1
  88.6 1.9 %fusion.4 = f32[1024]{0:T(1024)S(1)} fusion(f32[512,1024,1]{1,0,2:T(8,128)} %get-tuple-element.4, bf16[16,32,1024]{2,1,0:T(8,128)(2,1)S(1)} %all-to-all-done.2), kind=kLoop, calls=%fused_computation.9 | loop fusion | flops 1571840 | bytes 3149824 | tf_op jit(solution)/shard_map/reduce_sum | solution.py:77
  90.5 0.0 copy-start.1
  90.5 0.7 broadcast_in_dim.49
  91.1 4.9 %all-to-all-start.6 = ((f32[16,1,1024]{2,1,0:T(1,128)}), f32[16,1,1024]{2,1,0:T(1,128)S(1)}, u32[]{:S(2)}, u32[]{:S(2)}) async-start(f32[16,1,1024]{2,1,0:T(1,128)} %broadcast_in_dim.49), calls=%async_computation.6 | async-start | bytes 131072 | tf_op jit(solution)/shard_map/all_to_all | solution.py:92
  96.0 0.0 collective-permute-done.1
  96.0 0.3 fusion.5
  96.3 6.6 %all-to-all-done.6 = f32[16,1,1024]{2,1,0:T(1,128)S(1)} async-done(((f32[16,1,1024]{2,1,0:T(1,128)}), f32[16,1,1024]{2,1,0:T(1,128)S(1)}, u32[]{:S(2)}, u32[]{:S(2)}) %all-to-all-start.6) | async-done | bytes 65568 | tf_op jit(solution)/shard_map/all_to_all | solution.py:92
  102.9 10.5 %all_to_all.46 = bf16[16,8,512]{2,1,0:T(8,128)(2,1)S(1)} all-to-all(bf16[16,8,512]{2,1,0:T(8,128)(2,1)S(1)} %fusion.5), channel_id=1, replica_groups=mesh['hi'=2,'low'=8,'tensor'=2] {'hi','low'}, dimensions={0} | all-to-all | bytes 262144 | tf_op jit(solution)/shard_map/all_to_all | solution.py:112
  113.4 3.7 %all-to-all-start.5 = ((bf16[16,32,1024]{2,1,0:T(8,128)(2,1)}), bf16[16,32,1024]{2,1,0:T(8,128)(2,1)S(1)}, u32[]{:S(2)}, u32[]{:S(2)}) async-start(bf16[16,32,1024]{2,1,0:T(8,128)(2,1)} %bitcast.46), calls=%async_computation.5 | async-start | bytes 2097152 | tf_op jit(solution)/shard_map/all_to_all | solution.py:80
  117.1 0.2 reduce
  117.3 0.1 reshape.64
  117.3 0.1 reduce_sum.59
  117.4 0.0 copy-done.1
  117.4 0.6 multiply_divide_fusion
  118.0 21.9 %all-to-all-done.5 = bf16[16,32,1024]{2,1,0:T(8,128)(2,1)S(1)} async-done(((bf16[16,32,1024]{2,1,0:T(8,128)(2,1)}), bf16[16,32,1024]{2,1,0:T(8,128)(2,1)S(1)}, u32[]{:S(2)}, u32[]{:S(2)}) %all-to-all-start.5) | async-done | bytes 1048608 | tf_op jit(solution)/shard_map/all_to_all | solution.py:80
  140.0 0.2 convert_reduce_fusion
  140.2 0.1 multiply_bitcast_fusion
  140.3 1.1 copy.24
  141.4 0.7 copy.30
  (3 shorter events, 0.1 us)
Async XLA Ops:
  0.6 15.3 %all-to-all-start = ((bf16[16,8,512]{2,1,0:T(8,128)(2,1)}), bf16[16,8,512]{2,1,0:T(8,128)(2,1)S(1)}, u32[]{:S(2)}, u32[]{:S(2)}) async-start(bf16[16,8,512]{2,1,0:T(8,128)(2,1)} %bitcast.52), calls=%async_computation | async-start | bytes 262144 | tf_op jit(solution)/shard_map/all_to_all | solution.py:49
  9.6 3.8 %collective-permute-start = (f32[64]{0:T(128)S(1)}, f32[64]{0:T(128)S(1)}, u32[]{:S(2)}, u32[]{:S(2)}) collective-permute-start(f32[64]{0:T(128)S(1)} %fusion), channel_id=1, source_target_pairs={{0,1},{1,0},{2,3},{3,2},{4,5},{5,4},{6,7},{7,6},{8,9},{9,8},{10,11... | collective-permute-start | bytes 776 | tf_op jit(solution)/shard_map/ppermute | solution.py:16
  17.5 3.7 %copy-start = (bf16[32,8192]{1,0:T(8,128)(2,1)S(1)}, bf16[32,8192]{1,0:T(8,128)(2,1)}, u32[]{:S(2)}) copy-start(bf16[32,8192]{1,0:T(8,128)(2,1)} %param.8) | copy-start | bytes 1572868
  17.5 23.7 %all-to-all-start.1 = ((bf16[8,64,1536]{2,1,0:T(8,128)(2,1)}), bf16[8,64,1536]{2,1,0:T(8,128)(2,1)S(1)}, u32[]{:S(2)}, u32[]{:S(2)}) async-start(bf16[8,64,1536]{2,1,0:T(8,128)(2,1)} %pad_maximum_fusion), calls=%async_computation.1 | async-start | bytes 3145728 | tf_op jit(solution)/shard_map/all_to_all | solution.py:67
  42.3 27.3 %all-to-all-start.2 = ((bf16[16,32,1024]{2,1,0:T(8,128)(2,1)}), bf16[16,32,1024]{2,1,0:T(8,128)(2,1)S(1)}, u32[]{:S(2)}, u32[]{:S(2)}) async-start(bf16[16,32,1024]{2,1,0:T(8,128)(2,1)} %bitcast.43), calls=%async_computation.2 | async-start | bytes 2097152 | tf_op jit(solution)/shard_map/all_to_all | solution.py:45
  72.4 14.7 %all-to-all-start.3 = ((bf16[8,64,512]{2,1,0:T(8,128)(2,1)}), bf16[8,64,512]{2,1,0:T(8,128)(2,1)S(1)}, u32[]{:S(2)}, u32[]{:S(2)}) async-start(bf16[8,64,512]{2,1,0:T(8,128)(2,1)} %bitcast.50), calls=%async_computation.3 | async-start | bytes 1048576 | tf_op jit(solution)/shard_map/all_to_all | solution.py:101
  87.2 8.8 %collective-permute-start.1 = (f32[64,512]{1,0:T(8,128)S(1)}, f32[64,512]{1,0:T(8,128)S(1)}, u32[]{:S(2)}, u32[]{:S(2)}) collective-permute-start(f32[64,512]{1,0:T(8,128)S(1)} %convert_reduce_fusion.1), channel_id=1, source_target_pairs={{0,1},{1,0},{2,3},{3,2},{4,5},{5,4},{6,7},{7,6},{8,9},{9,8},{10,11... | collective-permute-start | bytes 393224 | tf_op jit(solution)/shard_map/ppermute | solution.py:16
  90.5 27.0 %copy-start.1 = (f32[8192]{0:T(1024)S(1)}, f32[8192]{0:T(1024)}, u32[]{:S(2)}) copy-start(f32[8192]{0:T(1024)} %param.7) | copy-start | bytes 98308
  91.1 11.8 %all-to-all-start.6 = ((f32[16,1,1024]{2,1,0:T(1,128)}), f32[16,1,1024]{2,1,0:T(1,128)S(1)}, u32[]{:S(2)}, u32[]{:S(2)}) async-start(f32[16,1,1024]{2,1,0:T(1,128)} %broadcast_in_dim.49), calls=%async_computation.6 | async-start | bytes 131072 | tf_op jit(solution)/shard_map/all_to_all | solution.py:92
  113.4 26.6 %all-to-all-start.5 = ((bf16[16,32,1024]{2,1,0:T(8,128)(2,1)}), bf16[16,32,1024]{2,1,0:T(8,128)(2,1)S(1)}, u32[]{:S(2)}, u32[]{:S(2)}) async-start(bf16[16,32,1024]{2,1,0:T(8,128)(2,1)} %bitcast.46), calls=%async_computation.5 | async-start | bytes 2097152 | tf_op jit(solution)/shard_map/all_to_all | solution.py:80

commit v2 on v1

v2 whole, which is shorter than its diff:
```python
import math

import jax
import jax.numpy as jnp
from jax import lax
from jax.sharding import Mesh
from jax.sharding import PartitionSpec as P

EPSILON = 1e-05

DP = ("hi", "lo", "core")
SWAP = [(0, 1), (1, 0)]
FEW = 4


def iota2(shape, dim):
    return lax.broadcasted_iota(jnp.int32, shape, dim)


def select(matrix, table):
    return jnp.dot(matrix, table, preferred_element_type=jnp.float32).astype(jnp.bfloat16)


def reduce_tensor(value):
    if lax.axis_size("tensor") == 2:
        return value + lax.ppermute(value, "tensor", SWAP)
    return lax.psum(value, "tensor")


def peer(step):
    if lax.axis_size("lo") <= FEW:
        return lax.axis_index("lo") ^ step
    return step


def swap_lo(block):
    size = lax.axis_size("lo")
    if size > FEW:
        sent = jnp.stack([block(j) for j in range(size)])
        return lax.all_to_all(sent, "lo", split_axis=0, concat_axis=0, tiled=True)
    me = lax.axis_index("lo")
    got = [block(me)]
    for step in range(1, size):
        pairs = [(j, j ^ step) for j in range(size)]
        got.append(lax.ppermute(block(me ^ step), "lo", pairs))
    return jnp.stack(got)


def slot_onehot(dest_rows, count, shards, capacity):
    rows = dest_rows.shape[0]
    same = (dest_rows[:, None] == dest_rows[None, :]) & (
        iota2((rows, rows), 1) < iota2((rows, rows), 0)
    )
    rank = jnp.sum(same.astype(jnp.int32), axis=1)
    accepted = lax.iota(jnp.int32, rows) < count
    position = jnp.where(accepted, dest_rows * capacity + rank, -1)
    slots = iota2((rows, shards * capacity), 1)
    return accepted, (position[:, None] == slots).astype(jnp.bfloat16)


def on_device(hidden_rows, norm_gain, key_weight, cotangent, accepted_counts, destination):
    halves, low, cores = lax.axis_size("hi"), lax.axis_size("lo"), lax.axis_size("core")
    hi, core = lax.axis_index("hi"), lax.axis_index("core")
    replicas = halves * low * cores
    rows, width = hidden_rows.shape
    model_width = width * lax.axis_size("tensor")
    owned, key_width = key_weight.shape[0], cotangent.shape[2]
    part = width // low
    core_keys = key_width // cores
    capacity = cotangent.shape[1] // replicas

    weight_here = swap_lo(lambda j: lax.dynamic_slice(key_weight, (0, j * part), (owned, part)))
    weight_there = lax.ppermute(weight_here, "hi", SWAP)
    stacked = jnp.concatenate([weight_here, weight_there]).reshape(core_keys, part)
    square = (core_keys, core_keys)
    to, of = iota2(square, 0), iota2(square, 1)
    half_keys = low * owned
    same = (to // half_keys) == (hi ^ (of // half_keys))
    same &= (to % half_keys) // owned == peer((of % half_keys) // owned)
    same &= to % owned == of % owned
    weights = select(same.astype(jnp.bfloat16), stacked)

    returned = lax.all_to_all(cotangent[0], DP, split_axis=0, concat_axis=0, tiled=True)
    accepted, onehot = slot_onehot(destination, accepted_counts[0], replicas, capacity)
    row_cot = select(onehot, returned)

    row_float = hidden_rows.astype(jnp.float32)
    squares = reduce_tensor(jnp.sum(row_float * row_float, axis=1))
    scale = lax.rsqrt(squares / model_width + EPSILON)
    normed = jnp.where(
        accepted[:, None], row_float * scale[:, None] * norm_gain[None, :], jnp.float32(0.0)
    ).astype(jnp.bfloat16)

    sent = jnp.concatenate(
        [
            normed.reshape(rows, low, part).transpose(1, 0, 2),
            jnp.broadcast_to(row_cot[None], (low, rows, key_width)),
        ],
        axis=2,
    )
    got = lax.all_to_all(sent, "lo", split_axis=0, concat_axis=0, tiled=True)
    rows_here = got[:, :, :part].reshape(low * rows, part)
    rows_there = lax.ppermute(rows_here, "core", SWAP)
    square = (key_width, key_width)
    nat, col = iota2(square, 0), iota2(square, 1)
    from_col = (
        ((col % core_keys) // owned) * cores + (core ^ (col // core_keys))
    ) * owned + col % owned
    by_core = (nat == from_col).astype(jnp.bfloat16)
    cot_sorted = select(got[:, :, part:].reshape(low * rows, key_width), by_core)
    cot_here = cot_sorted[:, :core_keys]
    cot_there = lax.ppermute(cot_sorted[:, core_keys:], "core", SWAP)

    def grad_of(cot, normed_rows):
        return lax.dot_general(
            cot, normed_rows, (((0,), (0,)), ((), ())), preferred_element_type=jnp.float32
        )

    grad_part = grad_of(cot_here, rows_here) + grad_of(cot_there, rows_there)
    gain_part = jnp.sum(grad_part * weights.astype(jnp.float32), axis=0)

    factor = 1.0 / math.sqrt(rows * replicas)
    grad_terms = lax.all_to_all(
        grad_part.astype(jnp.bfloat16).reshape(halves * low, owned, part),
        ("hi", "lo"),
        split_axis=0,
        concat_axis=0,
        tiled=True,
    ).reshape(halves, low, owned, part)
    grad_weight = (
        jnp.sum(grad_terms.astype(jnp.float32), axis=0).transpose(1, 0, 2).reshape(owned, width)
        * factor
    )

    gain_terms = lax.all_to_all(
        jnp.broadcast_to(gain_part[None, None], (replicas, 1, part)),
        DP,
        split_axis=0,
        concat_axis=0,
        tiled=True,
    ).reshape(halves, low, cores, part)
    grad_gain = jnp.sum(gain_terms, axis=(0, 2)).reshape(width) * factor / norm_gain

    def keys_of(normed_rows):
        return lax.dot_general(
            normed_rows, weights, (((1,), (1,)), ((), ())), preferred_element_type=jnp.float32
        ).astype(jnp.bfloat16).reshape(low, 1, rows, core_keys)

    key_part = jnp.concatenate([keys_of(rows_here), keys_of(rows_there)], axis=1)
    key_terms = swap_lo(lambda j: lax.dynamic_index_in_dim(key_part, j, 0, keepdims=False))
    chip_keys = reduce_tensor(jnp.sum(key_terms.astype(jnp.float32), axis=0)).astype(jnp.bfloat16)
    row_keys = jnp.concatenate(
        [chip_keys[0], lax.ppermute(chip_keys[1], "core", SWAP)], axis=1
    )
    key_slots = lax.dot_general(
        onehot, row_keys, (((0,), (0,)), ((), ())), preferred_element_type=jnp.float32
    ).astype(jnp.bfloat16)
    key_slots = lax.dot_general(
        key_slots, by_core, (((1,), (1,)), ((), ())), preferred_element_type=jnp.float32
    ).astype(jnp.bfloat16)
    key_out = lax.all_to_all(key_slots, DP, split_axis=0, concat_axis=0, tiled=True)
    return (key_out[None], grad_weight, grad_gain)


def solution(mesh):
    replicas, tensor = mesh.shape["dp"], mesh.shape["tensor"]
    split = Mesh(
        mesh.devices.reshape(2, replicas // 4, 2, tensor), ("hi", "lo", "core", "tensor")
    )
    return jax.shard_map(
        on_device,
        mesh=split,
        in_specs=(
            P(DP, "tensor"),
            P("tensor"),
            P(DP, "tensor"),
            P(DP, None, None),
            P(DP),
            P(DP),
        ),
        out_specs=(P(DP, None, None), P(DP, "tensor"), P("tensor")),
        check_vma=False,
    )
```

time: 144 us -> 124 us (0.86)
  waiting for transfers between devices: 77.1 us -> 60.4 us
  local copies, waits for them, and re-layouts: 5.43 us -> 10.4 us
  other arithmetic: 9.08 us -> 4.23 us
  starting transfers between devices: 32.8 us -> 30.6 us
    all_to_all x4 -> x2, waiting for transfers between devices: 69.6 us -> 45.8 us  [the longest x1 24.4 us: on_device(): lax.all_to_all(grad_part.astype(jnp.bfloat16).reshape(halves * low, owned...]
    all_to_all x4 -> x2, starting transfers between devices: 17.6 us -> 7.66 us  [the longest x1 4.1 us: on_device(): got = lax.all_to_all(sent, 'lo', split_axis=0, concat_axis=0, tiled=True)]
    ppermute x2 -> x12, starting transfers between devices: 2.92 us -> 11.9 us  [the longest x6 7.11 us: swap_lo(): got.append(lax.ppermute(block(me ^ step), 'lo', pairs))]
    ppermute x2 -> x12, waiting for transfers between devices: 0.01 us -> 7.21 us  [the longest x2 3.89 us: reduce_tensor(): return value + lax.ppermute(value, 'tensor', SWAP)]
    unnamed x6 -> x16, local copies, waits for them, and re-layouts: 0.96 us -> 5.09 us
    reduce_sum x2 -> x1, other arithmetic: 1.95 us -> 0.1 us  [on_device(): jnp.sum(gain_terms, axis=(0, 2)).reshape(width) * factor / norm_gain]
    dot_general x4 -> x8, matrix products: 5.65 us -> 5.22 us  [the longest x2 1.98 us: grad_of(): lax.dot_general(cot, normed_rows, (((0,), (0,)), ((), ())), preferred_ele...]
  transfers between devices with their start and end apart: 8 -> 16, of which waited for: 6 -> 7; matrix products, arithmetic and copies ran while one was open for 9% -> 13% of each run, Pallas kernels for 0% -> 0%
where the time goes in v2:
time: 124 us; the launch traced here: 123 us
  waiting for transfers between devices  60.4 us (49%)
  starting transfers between devices  30.6 us (25%)
  blocking collectives  10.5 us (8%)
  local copies, waits for them, and re-layouts  10.4 us (8%)
  matrix products  5.22 us (4%)
  other arithmetic  4.23 us (3%)
  between operations  1.72 us (1%)
    all_to_all x1, waiting for transfers between devices, on_device(): lax.all_to_all(grad_part.astype(jnp.bfloat16).reshape(halves * low, owned...  24.4 us
    all_to_all x1, waiting for transfers between devices, on_device(): got = lax.all_to_all(sent, 'lo', split_axis=0, concat_axis=0, tiled=True)  21.4 us
    all_to_all x1, blocking collectives, on_device(): lax.all_to_all(key_slots, DP, split_axis=0, concat_axis=0, tiled=True)  10.5 us
    all_to_all x1, starting transfers between devices, on_device(): lax.all_to_all(cotangent[0], DP, split_axis=0, concat_axis=0, tiled=True)  7.53 us
    all_to_all x1, waiting for transfers between devices, on_device(): lax.all_to_all(jnp.broadcast_to(gain_part[None, None], (replicas, 1, part...  7.37 us
    ppermute x6, starting transfers between devices, swap_lo(): got.append(lax.ppermute(block(me ^ step), 'lo', pairs))  7.11 us
    unnamed x16, local copies, waits for them, and re-layouts  5.09 us
    all_to_all x1, starting transfers between devices, on_device(): got = lax.all_to_all(sent, 'lo', split_axis=0, concat_axis=0, tiled=True)  4.1 us
  transfers between devices with their start and end apart: 16, of which 7 were waited for; matrix products, arithmetic and copies ran while one was open for 13% of the time, Pallas kernels for 0%

profile of v2, /device:TPU:0, one launch (start us, length us, event | category | flops | bytes accessed | tf_op | source)
XLA Modules:
  0.0 123.0 jit_solution(17542178410431515891)
XLA Ops:
  0.7 7.5 %all-to-all-start = ((bf16[16,8,512]{2,1,0:T(8,128)(2,1)}), bf16[16,8,512]{2,1,0:T(8,128)(2,1)S(1)}, u32[]{:S(2)}, u32[]{:S(2)}) async-start(bf16[16,8,512]{2,1,0:T(8,128)(2,1)} %bitcast.71), calls=%async_computation | async-start | bytes 262144 | tf_op jit(solution)/shard_map/all_to_all | solution.py:83
  8.2 1.5 %fusion = f32[64]{0:T(128)S(1)} fusion(bf16[64,8192]{1,0:T(8,128)(2,1)} %param.6), kind=kLoop, calls=%fused_computation.8 | loop fusion | flops 1572800 | bytes 1048832 | tf_op jit(solution)/shard_map/reduce_sum | solution.py:88
  9.7 1.6 %collective-permute-start = (f32[64]{0:T(128)S(1)}, f32[64]{0:T(128)S(1)}, u32[]{:S(2)}, u32[]{:S(2)}) collective-permute-start(f32[64]{0:T(128)S(1)} %fusion), channel_id=1, source_target_pairs={{0,1},{1,0},{2,3},{3,2},{4,5},{5,4},{6,7},{7,6},{8,9},{9,8},{10,11... | collective-permute-start | bytes 776 | tf_op jit(solution)/shard_map/ppermute | solution.py:26
  11.3 1.1 constant_dynamic-slice_fusion
  12.3 2.0 %collective-permute-start.1 = (bf16[32,2048]{1,0:T(8,128)(2,1)S(1)}, bf16[32,2048]{1,0:T(8,128)(2,1)S(1)}, u32[]{:S(2)}, u32[]{:S(2)}) collective-permute-start(bf16[32,2048]{1,0:T(8,128)(2,1)S(1)} %get-tuple-element.8), channel_id=1, source_target_pairs={{0,4},{4,0},{8,12},{12,8},{1,5},{5,1},{9,13},{13,9},{2,6},{6,2},{1... | collective-permute-start | bytes 393224 | tf_op jit(solution)/shard_map/ppermute | solution.py:45
  14.3 1.5 %collective-permute-start.2 = (bf16[32,2048]{1,0:T(8,128)(2,1)S(1)}, bf16[32,2048]{1,0:T(8,128)(2,1)S(1)}, u32[]{:S(2)}, u32[]{:S(2)}) collective-permute-start(bf16[32,2048]{1,0:T(8,128)(2,1)S(1)} %get-tuple-element.9), channel_id=1, source_target_pairs={{0,8},{4,12},{8,0},{12,4},{1,9},{5,13},{9,1},{13,5},{2,10},{6,14},... | collective-permute-start | bytes 393224 | tf_op jit(solution)/shard_map/ppermute | solution.py:45
  15.8 0.1 collective-permute-start.3
  15.9 0.2 convert_reduce_fusion.2
  16.8 0.0 collective-permute-done
  16.8 0.4 fusion.3
  17.2 0.8 reshape.58
  18.0 0.0 all-to-all-done
  18.0 0.2 convolution_convert_fusion.6
  18.2 0.1 broadcast_in_dim.40
  18.3 0.6 pad_maximum_fusion
  19.0 1.3 %copy.19 = bf16[4,64,2560]{2,1,0:T(8,128)(2,1)} copy(bf16[4,64,2560]{2,0,1:T(4,128)(2,1)S(1)} %pad_maximum_fusion) | data formatting | bytes 2621440 | tf_op jit(solution)/shard_map/concatenate | solution.py:94
  20.3 4.1 %all-to-all-start.1 = ((bf16[4,64,2560]{2,1,0:T(8,128)(2,1)}), bf16[4,64,2560]{2,1,0:T(8,128)(2,1)S(1)}, u32[]{:S(2)}, u32[]{:S(2)}) async-start(bf16[4,64,2560]{2,1,0:T(8,128)(2,1)} %copy.19), calls=%async_computation.1 | async-start | bytes 2621440 | tf_op jit(solution)/shard_map/all_to_all | solution.py:101
  24.4 1.6 %constant_dynamic-update-slice_fusion.4 = (bf16[8,32,2048]{2,1,0:T(8,128)(2,1)}, bf16[1,32,2048]{2,1,0:T(8,128)(2,1)S(1)}) fusion(bf16[32,8192]{1,0:T(8,128)(2,1)} %param.8, s32[]{:T(128)S(6)} %select_n.94), kind=kLoop, calls=%fused_computation.129 | loop fusion | bytes 393220
  26.0 0.0 collective-permute-done.1
  26.0 0.0 collective-permute-done.2
  26.0 0.0 collective-permute-done.3
  26.0 0.1 pad_maximum_fusion.1
  26.1 2.4 %collective-permute-start.4 = (bf16[4,32,2048]{2,1,0:T(8,128)(2,1)S(1)}, bf16[4,32,2048]{2,1,0:T(8,128)(2,1)S(1)}, u32[]{:S(2)}, u32[]{:S(2)}) collective-permute-start(bf16[4,32,2048]{2,1,0:T(8,128)(2,1)S(1)} %pad_maximum_fusion.1), channel_id=1, source_target_pairs={{0,16},{16,0},{1,17},{17,1},{2,18},{18,2},{3,19},{19,3},{4,20},{20... | collective-permute-start | bytes 1572872 | tf_op jit(solution)/shard_map/ppermute | solution.py:73
  28.5 0.7 constant_dynamic-update-slice_fusion.3
  29.2 0.7 constant_dynamic-update-slice_fusion.2
  29.9 21.4 %all-to-all-done.1 = bf16[4,64,2560]{2,1,0:T(8,128)(2,1)S(1)} async-done(((bf16[4,64,2560]{2,1,0:T(8,128)(2,1)}), bf16[4,64,2560]{2,1,0:T(8,128)(2,1)S(1)}, u32[]{:S(2)}, u32[]{:S(2)}) %all-to-all-start.1) | async-done | bytes 1310752 | tf_op jit(solution)/shard_map/all_to_all | solution.py:101
  51.2 0.1 slice.24
  51.4 0.1 collective-permute-start.5
  51.4 1.5 %copy-done.3 = bf16[8,32,2048]{2,1,0:T(8,128)(2,1)S(1)} copy-done((bf16[8,32,2048]{2,1,0:T(8,128)(2,1)S(1)}, bf16[8,32,2048]{2,1,0:T(8,128)(2,1)}, u32[]{:S(2)}) %copy-start.3) | copy-done | bytes 1048600
  52.9 0.0 collective-permute-done.4
  53.0 1.1 convolution_convert_fusion
  54.1 0.0 slice-start
  54.1 0.6 convolution_convert_fusion.5
  54.7 0.0 collective-permute-done.5
  54.7 0.5 convolution_convert_fusion.4
  55.2 1.8 %collective-permute-start.8 = (bf16[2,64,256]{2,1,0:T(8,128)(2,1)S(1)}, bf16[2,64,256]{2,1,0:T(8,128)(2,1)S(1)}, u32[]{:S(2)}, u32[]{:S(2)}) collective-permute-start(bf16[2,64,256]{2,1,0:T(8,128)(2,1)S(1)} %get-tuple-element.13), channel_id=1, source_target_pairs={{0,12},{4,8},{8,4},{12,0},{1,13},{5,9},{9,5},{13,1},{2,14},{6,10},... | collective-permute-start | bytes 196616 | tf_op jit(solution)/shard_map/ppermute | solution.py:45
  57.0 1.2 %collective-permute-start.7 = (bf16[2,64,256]{2,1,0:T(8,128)(2,1)S(1)}, bf16[2,64,256]{2,1,0:T(8,128)(2,1)S(1)}, u32[]{:S(2)}, u32[]{:S(2)}) collective-permute-start(bf16[2,64,256]{2,1,0:T(8,128)(2,1)S(1)} %get-tuple-element.12), channel_id=1, source_target_pairs={{0,8},{4,12},{8,0},{12,4},{1,9},{5,13},{9,1},{13,5},{2,10},{6,14},... | collective-permute-start | bytes 196616 | tf_op jit(solution)/shard_map/ppermute | solution.py:45
  58.2 0.6 collective-permute-start.6
  58.8 0.4 convolution_convert_fusion.1
  59.2 1.3 %collective-permute-done.8 = bf16[2,64,256]{2,1,0:T(8,128)(2,1)S(1)} collective-permute-done((bf16[2,64,256]{2,1,0:T(8,128)(2,1)S(1)}, bf16[2,64,256]{2,1,0:T(8,128)(2,1)S(1)}, u32[]{:S(2)}, u32[]{:S(2)}) %collective-permute-start.8) | collective-permute-done | bytes 65568 | tf_op jit(solution)/shard_map/ppermute | solution.py:45
  60.5 0.7 collective-permute-done.7
  61.3 1.2 %collective-permute-done.6 = bf16[2,64,256]{2,1,0:T(8,128)(2,1)S(1)} collective-permute-done((bf16[2,64,256]{2,1,0:T(8,128)(2,1)S(1)}, bf16[2,64,256]{2,1,0:T(8,128)(2,1)S(1)}, u32[]{:S(2)}, u32[]{:S(2)}) %collective-permute-start.6) | collective-permute-done | bytes 65568 | tf_op jit(solution)/shard_map/ppermute | solution.py:45
  62.5 0.6 collective-permute-start.9
  63.1 0.5 fusion.30
  63.6 0.1 collective-permute-start.11
  63.7 3.9 %collective-permute-done.9 = f32[2,64,256]{2,1,0:T(8,128)S(1)} collective-permute-done((f32[2,64,256]{2,1,0:T(8,128)S(1)}, f32[2,64,256]{2,1,0:T(8,128)S(1)}, u32[]{:S(2)}, u32[]{:S(2)}) %collective-permute-start.9) | collective-permute-done | bytes 131104 | tf_op jit(solution)/shard_map/ppermute | solution.py:26
  67.6 0.1 collective-permute-start.10
  67.7 1.5 %multiply_reduce_fusion = (f32[2048]{0:T(1024)S(1)}, bf16[256,2048]{1,0:T(8,128)(2,1)}) fusion(bf16[256,2048]{1,0:T(8,128)(2,1)S(1)} %convolution_convert_fusion, f32[256,2048]{1,0:T(8,128)S(1)} %fusion.30, bf16[256,256]{1,0:T(8,128)(2,1)S(1)} %collective-permute-done.11, bf16[256,2048]{1,0:T(8,128)(2,1)S(1)} %collective-permute-done.5), kind=kOutput, calls=%fused_computation.13 | convolution fusion | flops 271054848 | bytes 5382144 | tf_op jit(solution)/shard_map/dot_general | solution.py:115
  69.2 0.7 broadcast_in_dim.42
  69.9 3.5 %all-to-all-start.4 = ((f32[16,1,2048]{2,1,0:T(1,128)}), f32[16,1,2048]{2,1,0:T(1,128)S(1)}, u32[]{:S(2)}, u32[]{:S(2)}) async-start(f32[16,1,2048]{2,1,0:T(1,128)} %broadcast_in_dim.42), calls=%async_computation.4 | async-start | bytes 262144 | tf_op jit(solution)/shard_map/all_to_all | solution.py:135
  73.5 0.0 collective-permute-done.10
  73.5 0.5 fusion.4
  74.0 7.4 %all-to-all-done.4 = f32[16,1,2048]{2,1,0:T(1,128)S(1)} async-done(((f32[16,1,2048]{2,1,0:T(1,128)}), f32[16,1,2048]{2,1,0:T(1,128)S(1)}, u32[]{:S(2)}, u32[]{:S(2)}) %all-to-all-start.4) | async-done | bytes 131104 | tf_op jit(solution)/shard_map/all_to_all | solution.py:135
  81.4 10.5 %all_to_all.36 = bf16[16,8,512]{2,1,0:T(8,128)(2,1)S(1)} all-to-all(bf16[16,8,512]{2,1,0:T(8,128)(2,1)S(1)} %fusion.4), channel_id=1, replica_groups=mesh['hi'=2,'lo'=4,'core'=2,'tensor'=2] {'hi','lo','core'}, dimensions={0} | all-to-all | bytes 262144 | tf_op jit(solution)/shard_map/all_to_all | solution.py:161
  91.9 3.6 %all-to-all-start.3 = ((bf16[8,32,2048]{2,1,0:T(8,128)(2,1)}), bf16[8,32,2048]{2,1,0:T(8,128)(2,1)S(1)}, u32[]{:S(2)}, u32[]{:S(2)}) async-start(bf16[8,32,2048]{2,1,0:T(8,128)(2,1)} %bitcast.23), calls=%async_computation.3 | async-start | bytes 2097152 | tf_op jit(solution)/shard_map/all_to_all | solution.py:123
  95.4 0.3 reduce
  95.7 0.1 reshape.65
  95.8 0.1 reduce_sum.59
  96.0 0.6 div.77
  96.6 24.4 %all-to-all-done.3 = bf16[8,32,2048]{2,1,0:T(8,128)(2,1)S(1)} async-done(((bf16[8,32,2048]{2,1,0:T(8,128)(2,1)}), bf16[8,32,2048]{2,1,0:T(8,128)(2,1)S(1)}, u32[]{:S(2)}, u32[]{:S(2)}) %all-to-all-start.3) | async-done | bytes 1048608 | tf_op jit(solution)/shard_map/all_to_all | solution.py:123
  121.0 0.2 convert_reduce_fusion
  121.2 0.1 multiply_bitcast_fusion
  121.3 1.1 copy.24
  122.3 0.7 copy.32
  (33 shorter events, 0.2 us)
Async XLA Ops:
  0.6 16.2 %copy-start.1 = (bf16[64,8192]{1,0:T(8,128)(2,1)S(1)}, bf16[64,8192]{1,0:T(8,128)(2,1)}, u32[]{:S(2)}) copy-start(bf16[64,8192]{1,0:T(8,128)(2,1)} %param.6) | copy-start | bytes 3145732
  0.6 15.3 %copy-start.4 = (s32[64]{0:T(128)S(1)}, s32[64]{0:T(128)}, u32[]{:S(2)}) copy-start(s32[64]{0:T(128)} %param.11) | copy-start | bytes 772
  0.7 16.2 %copy-start.2 = (f32[8192]{0:T(1024)S(1)}, f32[8192]{0:T(1024)}, u32[]{:S(2)}) copy-start(f32[8192]{0:T(1024)} %param.7) | copy-start | bytes 98308
  0.7 17.4 %all-to-all-start = ((bf16[16,8,512]{2,1,0:T(8,128)(2,1)}), bf16[16,8,512]{2,1,0:T(8,128)(2,1)S(1)}, u32[]{:S(2)}, u32[]{:S(2)}) async-start(bf16[16,8,512]{2,1,0:T(8,128)(2,1)} %bitcast.71), calls=%async_computation | async-start | bytes 262144 | tf_op jit(solution)/shard_map/all_to_all | solution.py:83
  9.7 7.1 %collective-permute-start = (f32[64]{0:T(128)S(1)}, f32[64]{0:T(128)S(1)}, u32[]{:S(2)}, u32[]{:S(2)}) collective-permute-start(f32[64]{0:T(128)S(1)} %fusion), channel_id=1, source_target_pairs={{0,1},{1,0},{2,3},{3,2},{4,5},{5,4},{6,7},{7,6},{8,9},{9,8},{10,11... | collective-permute-start | bytes 776 | tf_op jit(solution)/shard_map/ppermute | solution.py:26
  12.3 13.6 %collective-permute-start.1 = (bf16[32,2048]{1,0:T(8,128)(2,1)S(1)}, bf16[32,2048]{1,0:T(8,128)(2,1)S(1)}, u32[]{:S(2)}, u32[]{:S(2)}) collective-permute-start(bf16[32,2048]{1,0:T(8,128)(2,1)S(1)} %get-tuple-element.8), channel_id=1, source_target_pairs={{0,4},{4,0},{8,12},{12,8},{1,5},{5,1},{9,13},{13,9},{2,6},{6,2},{1... | collective-permute-start | bytes 393224 | tf_op jit(solution)/shard_map/ppermute | solution.py:45
  14.3 11.7 %collective-permute-start.2 = (bf16[32,2048]{1,0:T(8,128)(2,1)S(1)}, bf16[32,2048]{1,0:T(8,128)(2,1)S(1)}, u32[]{:S(2)}, u32[]{:S(2)}) collective-permute-start(bf16[32,2048]{1,0:T(8,128)(2,1)S(1)} %get-tuple-element.9), channel_id=1, source_target_pairs={{0,8},{4,12},{8,0},{12,4},{1,9},{5,13},{9,1},{13,5},{2,10},{6,14},... | collective-permute-start | bytes 393224 | tf_op jit(solution)/shard_map/ppermute | solution.py:45
  15.8 10.2 %collective-permute-start.3 = (bf16[32,2048]{1,0:T(8,128)(2,1)S(1)}, bf16[32,2048]{1,0:T(8,128)(2,1)S(1)}, u32[]{:S(2)}, u32[]{:S(2)}) collective-permute-start(bf16[32,2048]{1,0:T(8,128)(2,1)S(1)} %get-tuple-element.7), channel_id=1, source_target_pairs={{0,12},{4,8},{8,4},{12,0},{1,13},{5,9},{9,5},{13,1},{2,14},{6,10},... | collective-permute-start | bytes 393224 | tf_op jit(solution)/shard_map/ppermute | solution.py:45
  20.3 31.0 %all-to-all-start.1 = ((bf16[4,64,2560]{2,1,0:T(8,128)(2,1)}), bf16[4,64,2560]{2,1,0:T(8,128)(2,1)S(1)}, u32[]{:S(2)}, u32[]{:S(2)}) async-start(bf16[4,64,2560]{2,1,0:T(8,128)(2,1)} %copy.19), calls=%async_computation.1 | async-start | bytes 2621440 | tf_op jit(solution)/shard_map/all_to_all | solution.py:101
  26.1 26.8 %collective-permute-start.4 = (bf16[4,32,2048]{2,1,0:T(8,128)(2,1)S(1)}, bf16[4,32,2048]{2,1,0:T(8,128)(2,1)S(1)}, u32[]{:S(2)}, u32[]{:S(2)}) collective-permute-start(bf16[4,32,2048]{2,1,0:T(8,128)(2,1)S(1)} %pad_maximum_fusion.1), channel_id=1, source_target_pairs={{0,16},{16,0},{1,17},{17,1},{2,18},{18,2},{3,19},{19,3},{4,20},{20... | collective-permute-start | bytes 1572872 | tf_op jit(solution)/shard_map/ppermute | solution.py:73
  51.2 2.9 %copy-start = (bf16[4,64,2560]{2,1,0:T(8,128)(2,1)}, bf16[4,64,2560]{2,1,0:T(8,128)(2,1)S(1)}, u32[]{:S(2)}) copy-start(bf16[4,64,2560]{2,1,0:T(8,128)(2,1)S(1)} %all-to-all-done.1) | copy-start | bytes 3932164
  51.2 1.7 %copy-start.3 = (bf16[8,32,2048]{2,1,0:T(8,128)(2,1)S(1)}, bf16[8,32,2048]{2,1,0:T(8,128)(2,1)}, u32[]{:S(2)}) copy-start(bf16[8,32,2048]{2,1,0:T(8,128)(2,1)} %constant_dynamic-update-slice_fusion.2) | copy-start | bytes 3145732
  51.4 3.3 %collective-permute-start.5 = (bf16[256,2048]{1,0:T(8,128)(2,1)S(1)}, bf16[256,2048]{1,0:T(8,128)(2,1)S(1)}, u32[]{:S(2)}, u32[]{:S(2)}) collective-permute-start(bf16[256,2048]{1,0:T(8,128)(2,1)S(1)} %bitcast.57), channel_id=1, source_target_pairs={{0,2},{2,0},{1,3},{3,1},{4,6},{6,4},{5,7},{7,5},{8,10},{10,8},{9,1... | collective-permute-start | bytes 3145736 | tf_op jit(solution)/shard_map/ppermute | solution.py:103
  54.1 4.7 %slice-start = ((bf16[4,64,2560]{2,1,0:T(8,128)(2,1)}), bf16[4,64,512]{2,1,0:T(8,128)(2,1)S(1)}, s32[]{:S(2)}) async-start(bf16[4,64,2560]{2,1,0:T(8,128)(2,1)} %copy-done), calls=%async_computation.5 | async-start | bytes 524288 | tf_op jit(solution)/shard_map/slice | solution.py:110
  55.2 5.3 %collective-permute-start.8 = (bf16[2,64,256]{2,1,0:T(8,128)(2,1)S(1)}, bf16[2,64,256]{2,1,0:T(8,128)(2,1)S(1)}, u32[]{:S(2)}, u32[]{:S(2)}) collective-permute-start(bf16[2,64,256]{2,1,0:T(8,128)(2,1)S(1)} %get-tuple-element.13), channel_id=1, source_target_pairs={{0,12},{4,8},{8,4},{12,0},{1,13},{5,9},{9,5},{13,1},{2,14},{6,10},... | collective-permute-start | bytes 196616 | tf_op jit(solution)/shard_map/ppermute | solution.py:45
  57.0 4.3 %collective-permute-start.7 = (bf16[2,64,256]{2,1,0:T(8,128)(2,1)S(1)}, bf16[2,64,256]{2,1,0:T(8,128)(2,1)S(1)}, u32[]{:S(2)}, u32[]{:S(2)}) collective-permute-start(bf16[2,64,256]{2,1,0:T(8,128)(2,1)S(1)} %get-tuple-element.12), channel_id=1, source_target_pairs={{0,8},{4,12},{8,0},{12,4},{1,9},{5,13},{9,1},{13,5},{2,10},{6,14},... | collective-permute-start | bytes 196616 | tf_op jit(solution)/shard_map/ppermute | solution.py:45
  58.2 4.3 %collective-permute-start.6 = (bf16[2,64,256]{2,1,0:T(8,128)(2,1)S(1)}, bf16[2,64,256]{2,1,0:T(8,128)(2,1)S(1)}, u32[]{:S(2)}, u32[]{:S(2)}) collective-permute-start(bf16[2,64,256]{2,1,0:T(8,128)(2,1)S(1)} %get-tuple-element.11), channel_id=1, source_target_pairs={{0,4},{4,0},{8,12},{12,8},{1,5},{5,1},{9,13},{13,9},{2,6},{6,2},{1... | collective-permute-start | bytes 196616 | tf_op jit(solution)/shard_map/ppermute | solution.py:45
  62.5 5.0 %collective-permute-start.9 = (f32[2,64,256]{2,1,0:T(8,128)S(1)}, f32[2,64,256]{2,1,0:T(8,128)S(1)}, u32[]{:S(2)}, u32[]{:S(2)}) collective-permute-start(f32[2,64,256]{2,1,0:T(8,128)S(1)} %convert_reduce_fusion.1), channel_id=1, source_target_pairs={{0,1},{1,0},{2,3},{3,2},{4,5},{5,4},{6,7},{7,6},{8,9},{9,8},{10,11... | collective-permute-start | bytes 393224 | tf_op jit(solution)/shard_map/ppermute | solution.py:26
  63.6 4.1 %collective-permute-start.11 = (bf16[256,256]{1,0:T(8,128)(2,1)S(1)}, bf16[256,256]{1,0:T(8,128)(2,1)S(1)}, u32[]{:S(2)}, u32[]{:S(2)}) collective-permute-start(bf16[256,256]{1,0:T(8,128)(2,1)S(1)} %slice.29), channel_id=1, source_target_pairs={{0,2},{2,0},{1,3},{3,1},{4,6},{6,4},{5,7},{7,5},{8,10},{10,8},{9,1... | collective-permute-start | bytes 393224 | tf_op jit(solution)/shard_map/ppermute | solution.py:112
  67.6 5.9 %collective-permute-start.10 = (bf16[64,256]{1,0:T(8,128)(2,1)S(1)}, bf16[64,256]{1,0:T(8,128)(2,1)S(1)}, u32[]{:S(2)}, u32[]{:S(2)}) collective-permute-start(bf16[64,256]{1,0:T(8,128)(2,1)S(1)} %get-tuple-element.15), channel_id=1, source_target_pairs={{0,2},{2,0},{1,3},{3,1},{4,6},{6,4},{5,7},{7,5},{8,10},{10,8},{9,1... | collective-permute-start | bytes 98312 | tf_op jit(solution)/shard_map/ppermute | solution.py:153
  69.9 11.4 %all-to-all-start.4 = ((f32[16,1,2048]{2,1,0:T(1,128)}), f32[16,1,2048]{2,1,0:T(1,128)S(1)}, u32[]{:S(2)}, u32[]{:S(2)}) async-start(f32[16,1,2048]{2,1,0:T(1,128)} %broadcast_in_dim.42), calls=%async_computation.4 | async-start | bytes 262144 | tf_op jit(solution)/shard_map/all_to_all | solution.py:135
  91.9 29.1 %all-to-all-start.3 = ((bf16[8,32,2048]{2,1,0:T(8,128)(2,1)}), bf16[8,32,2048]{2,1,0:T(8,128)(2,1)S(1)}, u32[]{:S(2)}, u32[]{:S(2)}) async-start(bf16[8,32,2048]{2,1,0:T(8,128)(2,1)} %bitcast.23), calls=%async_computation.3 | async-start | bytes 2097152 | tf_op jit(solution)/shard_map/all_to_all | solution.py:123

commit v3 on v2

v3 whole, which is shorter than its diff:
```python
import functools
import math

import jax
import jax.numpy as jnp
from jax import lax
from jax.experimental import pallas as pl
from jax.experimental.pallas import tpu as pltpu
from jax.sharding import Mesh
from jax.sharding import PartitionSpec as P

EPSILON = 1e-05

DP = ("hi", "lo", "core")
SWAP = [(0, 1), (1, 0)]
FEW = 4
CHUNK = 512


def iota2(shape, dim):
    return lax.broadcasted_iota(jnp.int32, shape, dim)


def one_hot(index, size):
    return (index[:, None] == iota2((index.shape[0], size), 1)).astype(jnp.bfloat16)


def select(matrix, table):
    return jnp.dot(matrix, table, preferred_element_type=jnp.float32).astype(jnp.bfloat16)


def reduce_tensor(value):
    if lax.axis_size("tensor") == 2:
        return value + lax.ppermute(value, "tensor", SWAP)
    return lax.psum(value, "tensor")


def swap_core(value):
    return lax.ppermute(value, "core", SWAP)


def swap_lo(block):
    size, me = lax.axis_size("lo"), lax.axis_index("lo")
    if size <= FEW:
        pieces = [block(me)]
        for step in range(1, size):
            pairs = [(j, j ^ step) for j in range(size)]
            pieces.append(lax.ppermute(block(me ^ step), "lo", pairs))
        return pieces, [me ^ step for step in range(size)]
    sent = jnp.stack([block(j) for j in range(size)])
    got = lax.all_to_all(sent, "lo", split_axis=0, concat_axis=0, tiled=True)
    return [got.reshape((-1,) + got.shape[2:])], [jnp.int32(0)]


def slot_onehot(dest_rows, count, shards, capacity):
    rows = dest_rows.shape[0]
    same = (dest_rows[:, None] == dest_rows[None, :]) & (
        iota2((rows, rows), 1) < iota2((rows, rows), 0)
    )
    rank = jnp.sum(same.astype(jnp.int32), axis=1)
    accepted = lax.iota(jnp.int32, rows) < count
    position = jnp.where(accepted, dest_rows * capacity + rank, -1)
    return accepted, one_hot(position, shards * capacity)


def products_kernel(pieces, owned, low, core_keys, part, chunk, place_ref, *refs):
    row_refs, weight_refs = refs[: 2 * pieces], refs[2 * pieces : 2 * pieces + 2]
    own_ref, away_ref, gain_ref = refs[2 * pieces + 2 : 2 * pieces + 5]
    key_refs = refs[2 * pieces + 5 : 3 * pieces + 5]
    rows_ref, weights_ref, cot_ref, sums_ref, row_sem, weight_sem = refs[3 * pieces + 5 :]
    piece_rows = row_refs[0].shape[0]
    half_keys = core_keys // 2
    key_width = 2 * core_keys

    row_copies = [
        pltpu.make_async_copy(
            ref, rows_ref.at[pl.ds(j * piece_rows, piece_rows)], row_sem.at[j]
        )
        for j, ref in enumerate(row_refs)
    ]
    weight_copies = []
    block = half_keys // pieces
    for j in range(2 * pieces):
        first = place_ref[2 + j % pieces] * owned + (j // pieces) * half_keys
        if owned % 16 == 0:
            first = pl.multiple_of(first, 16)
        weight_copies.append(
            pltpu.make_async_copy(
                weight_refs[j // pieces].at[pl.ds((j % pieces) * block, block)],
                weights_ref.at[pl.ds(first, block)],
                weight_sem.at[j],
            )
        )
    for copy in row_copies + weight_copies:
        copy.start()
    for copy in row_copies:
        copy.wait()

    column = iota2((key_width, core_keys), 1)
    half = place_ref[0] ^ (column // half_keys)
    whole = ((half * low + (column % half_keys) // owned) * 2 + place_ref[1]) * owned
    whole = whole + column % owned
    chosen = jnp.where(iota2((key_width, core_keys), 0) == whole, 1.0, 0.0).astype(jnp.bfloat16)
    cot_ref[...] = lax.dot_general(
        rows_ref[:, part:], chosen, (((1,), (0,)), ((), ())), preferred_element_type=jnp.float32
    ).astype(jnp.bfloat16)
    for copy in weight_copies:
        copy.wait()

    for c in range(part // chunk):
        at = pl.ds(c * chunk, chunk)
        rows = rows_ref[:, at]
        weights = weights_ref[:, at]
        grad = lax.dot_general(
            cot_ref[...], rows, (((0,), (0,)), ((), ())), preferred_element_type=jnp.float32
        )
        own_ref[:, at] = grad[:half_keys]
        away_ref[:, at] = grad[half_keys:].astype(jnp.bfloat16)
        gain_ref[:, at] = jnp.sum(grad * weights.astype(jnp.float32), axis=0, keepdims=True)
        term = lax.dot_general(
            rows, weights, (((1,), (1,)), ((), ())), preferred_element_type=jnp.float32
        )
        if c == 0:
            sums_ref[...] = term
        else:
            sums_ref[...] += term
    for j, ref in enumerate(key_refs):
        for k in range(2):
            first = (k * pieces + j) * piece_rows
            ref[k] = sums_ref[first : first + piece_rows].astype(jnp.bfloat16)


def products(rows_here, rows_there, weights, places, core_keys, part, owned):
    pieces, low = len(rows_here), lax.axis_size("lo")
    piece_rows, columns = rows_here[0].shape
    half_keys = core_keys // 2
    scalars = jnp.stack([lax.axis_index("hi"), lax.axis_index("core")] + places).astype(jnp.int32)
    total = 2 * pieces * piece_rows
    return pl.pallas_call(
        functools.partial(
            products_kernel, pieces, owned, low, core_keys, part, min(CHUNK, part)
        ),
        out_shape=[
            jax.ShapeDtypeStruct((half_keys, part), jnp.float32),
            jax.ShapeDtypeStruct((half_keys, part), jnp.bfloat16),
            jax.ShapeDtypeStruct((1, part), jnp.float32),
        ]
        + [jax.ShapeDtypeStruct((2, piece_rows, core_keys), jnp.bfloat16)] * pieces,
        in_specs=[pl.BlockSpec(memory_space=pltpu.SMEM)]
        + [pl.BlockSpec(memory_space=pl.ANY)] * (2 * pieces + 2),
        scratch_shapes=[
            pltpu.VMEM((total, columns), jnp.bfloat16),
            pltpu.VMEM((core_keys, part), jnp.bfloat16),
            pltpu.VMEM((total, core_keys), jnp.bfloat16),
            pltpu.VMEM((total, core_keys), jnp.float32),
            pltpu.SemaphoreType.DMA((2 * pieces,)),
            pltpu.SemaphoreType.DMA((2 * pieces,)),
        ],
        compiler_params=pltpu.CompilerParams(vmem_limit_bytes=60 * 1024 * 1024),
        cost_estimate=pl.CostEstimate(
            flops=4 * total * core_keys * part,
            bytes_accessed=2 * total * columns + 8 * core_keys * part,
            transcendentals=0,
        ),
    )(scalars, *rows_here, *rows_there, *weights)


def on_device(hidden_rows, norm_gain, key_weight, cotangent, accepted_counts, destination):
    halves, low, cores = lax.axis_size("hi"), lax.axis_size("lo"), lax.axis_size("core")
    hi, core = lax.axis_index("hi"), lax.axis_index("core")
    replicas = halves * low * cores
    rows, width = hidden_rows.shape
    model_width = width * lax.axis_size("tensor")
    owned, key_width = key_weight.shape[0], cotangent.shape[2]
    part = width // low
    core_keys, half_keys = key_width // cores, low * owned
    capacity = cotangent.shape[1] // replicas
    factor = 1.0 / math.sqrt(rows * replicas)

    weight_here, places = swap_lo(
        lambda j: lax.dynamic_slice(key_weight, (0, j * part), (owned, part))
    )
    weight_here = jnp.concatenate(weight_here)
    weight_there = lax.ppermute(weight_here, "hi", SWAP)

    returned = lax.all_to_all(cotangent[0], DP, split_axis=0, concat_axis=0, tiled=True)
    accepted, onehot = slot_onehot(destination, accepted_counts[0], replicas, capacity)
    row_cot = select(onehot, returned)

    row_float = hidden_rows.astype(jnp.float32)
    squares = jnp.sum(row_float * row_float, axis=1)
    scale = lax.rsqrt(reduce_tensor(squares) / model_width + EPSILON)
    normed = jnp.where(
        accepted[:, None], row_float * scale[:, None] * norm_gain[None, :], jnp.float32(0.0)
    ).astype(jnp.bfloat16)

    rows_here, _ = swap_lo(
        lambda j: jnp.concatenate(
            [lax.dynamic_slice(normed, (0, j * part), (rows, part)), row_cot], axis=1
        )
    )
    rows_there = [swap_core(piece) for piece in rows_here]
    grad_own, grad_away, gain_part, *key_parts = products(
        rows_here, rows_there, (weight_here, weight_there), places, core_keys, part, owned
    )
    gain_part = gain_part[0]

    if low <= FEW:
        key_terms = [key_parts[0]] + [
            lax.ppermute(key_parts[step], "lo", [(j, j ^ step) for j in range(low)])
            for step in range(1, low)
        ]
    else:
        sent = key_parts[0].reshape(2, low, rows, core_keys).transpose(1, 0, 2, 3)
        got = lax.all_to_all(sent, "lo", split_axis=0, concat_axis=0, tiled=True)
        key_terms = [got[j] for j in range(low)]
    grad_away = lax.ppermute(grad_away, "hi", SWAP)
    key_sum = sum(term.astype(jnp.float32) for term in key_terms)
    chip_keys = reduce_tensor(key_sum).astype(jnp.bfloat16)
    row_keys = jnp.concatenate([chip_keys[0], swap_core(chip_keys[1])], axis=1)
    key_slots = lax.dot_general(
        onehot, row_keys, (((0,), (0,)), ((), ())), preferred_element_type=jnp.float32
    ).astype(jnp.bfloat16)
    place = lax.iota(jnp.int32, key_width)
    from_core = core ^ (place // core_keys)
    from_half = hi ^ ((place % core_keys) // half_keys)
    whole = ((from_half * low + (place % half_keys) // owned) * cores + from_core) * owned
    key_slots = select(key_slots, one_hot(whole + place % owned, key_width))
    upper = lax.reduce_precision(gain_part, 8, 7)
    terms = jnp.concatenate([upper, gain_part - upper]).astype(jnp.bfloat16)
    extra = -(-2 * part // (8 * key_width)) * 8
    terms = jnp.pad(terms, (0, extra * key_width - 2 * part)).reshape(1, extra, key_width)
    routed = jnp.concatenate(
        [
            key_slots.reshape(replicas, capacity, key_width),
            jnp.broadcast_to(terms, (replicas, extra, key_width)),
        ],
        axis=1,
    )

    grad_own, _ = lax.optimization_barrier((grad_own, routed))
    grad_own = ((grad_own + grad_away.astype(jnp.float32)) * factor).astype(jnp.bfloat16)
    grad_terms, _ = swap_lo(
        lambda j: lax.dynamic_slice(grad_own, (j * owned, 0), (owned, part))
    )
    if low <= FEW:
        grad_weight = jnp.zeros((owned, width), jnp.float32)
        for place, term in zip(places, grad_terms):
            grad_weight = lax.dynamic_update_slice(
                grad_weight, term.astype(jnp.float32), (0, place * part)
            )
    else:
        grad_weight = grad_terms[0].reshape(low, owned, part).transpose(1, 0, 2)
        grad_weight = grad_weight.reshape(owned, width).astype(jnp.float32)

    routed = lax.all_to_all(routed, DP, split_axis=0, concat_axis=0, tiled=True)
    key_out = routed[:, :capacity].reshape(1, replicas * capacity, key_width)
    gain_terms = routed[:, capacity:].reshape(replicas, extra * key_width)[:, : 2 * part]
    gain_sums = jnp.sum(
        gain_terms.astype(jnp.float32).reshape(halves, low, cores, 2, part), axis=(0, 2, 3)
    )
    grad_gain = gain_sums.reshape(width) * factor / norm_gain
    return (key_out, grad_weight, grad_gain)


def solution(mesh):
    replicas, tensor = mesh.shape["dp"], mesh.shape["tensor"]
    split = Mesh(
        mesh.devices.reshape(2, replicas // 4, 2, tensor), ("hi", "lo", "core", "tensor")
    )
    return jax.shard_map(
        on_device,
        mesh=split,
        in_specs=(
            P(DP, "tensor"),
            P("tensor"),
            P(DP, "tensor"),
            P(DP, None, None),
            P(DP),
            P(DP),
        ),
        out_specs=(P(DP, None, None), P(DP, "tensor"), P("tensor")),
        check_vma=False,
    )
```

time: 124 us -> 102 us (0.82)
  blocking collectives: 10.5 us -> 0 us
  waiting for transfers between devices: 60.4 us -> 53 us
  local copies, waits for them, and re-layouts: 10.4 us -> 3.56 us
  Pallas kernels: 0 us -> 5.51 us
  matrix products: 5.22 us -> 0.68 us
  other arithmetic: 4.23 us -> 7.1 us
    all_to_all x3 -> x1, waiting for transfers between devices: 53.1 us -> 0.01 us  [on_device(): routed = lax.all_to_all(routed, DP, split_axis=0, concat_axis=0, tiled=True)]
    ppermute x9 -> x18, waiting for transfers between devices: 3.32 us -> 46.3 us  [the longest x9 28.7 us: swap_lo(): pieces.append(lax.ppermute(block(me ^ step), 'lo', pairs))]
    all_to_all x1 -> x0, blocking collectives: 10.5 us -> none  [on_device(): lax.all_to_all(key_slots, DP, split_axis=0, concat_axis=0, tiled=True)]
    ppermute x9 -> x18, starting transfers between devices: 7.32 us -> 15.1 us  [the longest x9 10.7 us: swap_lo(): pieces.append(lax.ppermute(block(me ^ step), 'lo', pairs))]
    all_to_all x3 -> x1, starting transfers between devices: 11.2 us -> 3.87 us  [on_device(): routed = lax.all_to_all(routed, DP, split_axis=0, concat_axis=0, tiled=True)]
    pallas_call x0 -> x1, Pallas kernels: none -> 5.51 us  [products(): pl.pallas_call(functools.partial(products_kernel, pieces, owned, low, cor...]
    unnamed x16 -> x27, local copies, waits for them, and re-layouts: 5.09 us -> 0.78 us
    dot_general x5 -> x0, matrix products: 3.52 us -> none  [the longest x2 1.98 us: grad_of(): lax.dot_general(cot, normed_rows, (((0,), (0,)), ((), ())), preferred_ele...]
  transfers between devices with their start and end apart: 16 -> 23, of which waited for: 7 -> 12; matrix products, arithmetic and copies ran while one was open for 13% -> 7% of each run, Pallas kernels for 0% -> 0%
where the time goes in v3:
time: 102 us
  waiting for transfers between devices  53 us (52%)
  starting transfers between devices  30.4 us (30%)
  other arithmetic  7.1 us (7%)
  Pallas kernels  5.51 us (5%)
  local copies, waits for them, and re-layouts  3.56 us (3%)
  between operations  1.7 us (2%)
    ppermute x9, waiting for transfers between devices, swap_lo(): pieces.append(lax.ppermute(block(me ^ step), 'lo', pairs))  28.7 us
    ppermute x1, waiting for transfers between devices, on_device(): grad_away = lax.ppermute(grad_away, 'hi', SWAP)  14.4 us
    ppermute x9, starting transfers between devices, swap_lo(): pieces.append(lax.ppermute(block(me ^ step), 'lo', pairs))  10.7 us
    all_to_all x1, starting transfers between devices, on_device(): lax.all_to_all(cotangent[0], DP, split_axis=0, concat_axis=0, tiled=True)  5.94 us
    pallas_call x1, Pallas kernels, products(): pl.pallas_call(functools.partial(products_kernel, pieces, owned, low, cor...  5.51 us
    ppermute x2, waiting for transfers between devices, reduce_tensor(): return value + lax.ppermute(value, 'tensor', SWAP)  4.43 us
    all_to_all x1, starting transfers between devices, on_device(): routed = lax.all_to_all(routed, DP, split_axis=0, concat_axis=0, tiled=True)  3.87 us
    ppermute x2, starting transfers between devices, reduce_tensor(): return value + lax.ppermute(value, 'tensor', SWAP)  3.6 us
  transfers between devices with their start and end apart: 23, of which 12 were waited for; matrix products, arithmetic and copies ran while one was open for 7% of the time, Pallas kernels for 0%

profile of v3, /device:TPU:0, one launch (start us, length us, event | category | flops | bytes accessed | tf_op | source)
XLA Modules:
  0.0 102.0 jit_solution(17045587832048502776)
XLA Ops:
  0.7 1.6 %fusion = f32[64]{0:T(128)S(1)} fusion(bf16[64,8192]{1,0:T(8,128)(2,1)} %param.6), kind=kLoop, calls=%fused_computation.2 | loop fusion | flops 1572800 | bytes 1048832 | tf_op jit(solution)/shard_map/reduce_sum | solution.py:191
  2.3 3.0 %collective-permute-start = (f32[64]{0:T(128)S(1)}, f32[64]{0:T(128)S(1)}, u32[]{:S(2)}, u32[]{:S(2)}) collective-permute-start(f32[64]{0:T(128)S(1)} %fusion), channel_id=1, source_target_pairs={{0,1},{1,0},{2,3},{3,2},{4,5},{5,4},{6,7},{7,6},{8,9},{9,8},{10,11... | collective-permute-start | bytes 776 | tf_op jit(solution)/shard_map/ppermute | solution.py:34
  5.3 5.9 %all-to-all-start = ((bf16[16,8,512]{2,1,0:T(8,128)(2,1)}), bf16[16,8,512]{2,1,0:T(8,128)(2,1)S(1)}, u32[]{:S(2)}, u32[]{:S(2)}) async-start(bf16[16,8,512]{2,1,0:T(8,128)(2,1)} %bitcast.25), calls=%async_computation | async-start | bytes 262144 | tf_op jit(solution)/shard_map/all_to_all | solution.py:186
  11.3 1.1 %constant_dynamic-slice_fusion.6 = (bf16[32,2048]{1,0:T(8,128)(2,1)S(1)}, bf16[32,2048]{1,0:T(8,128)(2,1)S(1)}, bf16[32,2048]{1,0:T(8,128)(2,1)S(1)}, bf16[32,2048]{1,0:T(8,128)(2,1)S(1)}) fusion(bf16[32,8192]{1,0:T(8,128)(2,1)} %param.8, s32[]{:T(128)S(6)} %select_n.92, s32[]{:T(128)S(6)} %select_n.93, s32[]{:T(128)S(6)} %select_n.95, s32[]{:T(128)S(6)} %select_n.94), kind=kLoop, calls=%fused_computation.50 | loop fusion | bytes 1048592 | tf_op jit(solution)/shard_map/dynamic_slice | solution.py:181
  12.4 2.9 %collective-permute-start.10 = (bf16[32,2048]{1,0:T(8,128)(2,1)S(1)}, bf16[32,2048]{1,0:T(8,128)(2,1)S(1)}, u32[]{:S(2)}, u32[]{:S(2)}) collective-permute-start(bf16[32,2048]{1,0:T(8,128)(2,1)S(1)} %get-tuple-element.28), channel_id=1, source_target_pairs={{0,12},{4,8},{8,4},{12,0},{1,13},{5,9},{9,5},{13,1},{2,14},{6,10},... | collective-permute-start | bytes 393224 | tf_op jit(solution)/shard_map/ppermute | solution.py:48
  15.3 0.6 collective-permute-start.8
  15.8 0.2 collective-permute-start.9
  16.6 0.2 convert_reduce_fusion
  16.8 0.0 collective-permute-done
  16.9 0.4 fusion.3
  17.2 0.1 constant_dynamic-slice_fusion.7
  17.3 2.4 %all-to-all-done = bf16[16,8,512]{2,1,0:T(8,128)(2,1)S(1)} async-done(((bf16[16,8,512]{2,1,0:T(8,128)(2,1)}), bf16[16,8,512]{2,1,0:T(8,128)(2,1)S(1)}, u32[]{:S(2)}, u32[]{:S(2)}) %all-to-all-start) | async-done | bytes 131104 | tf_op jit(solution)/shard_map/all_to_all | solution.py:186
  19.7 0.2 convolution_convert_fusion.2
  19.9 0.1 pad_maximum_fusion
  20.0 0.1 collective-permute-start.1
  20.1 1.0 collective-permute-start.2
  21.1 0.0 collective-permute-done.10
  21.1 2.5 %collective-permute-start.3 = (bf16[64,2560]{1,0:T(8,128)(2,1)S(1)}, bf16[64,2560]{1,0:T(8,128)(2,1)}, u32[]{:S(2)}, u32[]{:S(2)}) collective-permute-start(bf16[64,2560]{1,0:T(8,128)(2,1)S(1)} %get-tuple-element.34), channel_id=1, source_target_pairs={{0,12},{4,8},{8,4},{12,0},{1,13},{5,9},{9,5},{13,1},{2,14},{6,10},... | collective-permute-start | bytes 983048 | tf_op jit(solution)/shard_map/ppermute | solution.py:48
  23.6 0.0 collective-permute-done.8
  23.6 0.0 collective-permute-done.9
  23.6 1.9 %collective-permute-start.11 = (bf16[128,2048]{1,0:T(8,128)(2,1)S(1)}, bf16[128,2048]{1,0:T(8,128)(2,1)S(1)}, u32[]{:S(2)}, u32[]{:S(2)}) collective-permute-start(bf16[128,2048]{1,0:T(8,128)(2,1)S(1)} %pad_maximum_fusion.4.refs_8_), channel_id=1, source_target_pairs={{0,16},{16,0},{1,17},{17,1},{2,18},{18,2},{3,19},{19,3},{4,20},{20... | collective-permute-start | bytes 1572872 | tf_op jit(solution)/shard_map/ppermute | solution.py:184
  25.5 0.0 collective-permute-start.4
  25.5 4.4 %collective-permute-done.1.refs_1_ = bf16[64,2560]{1,0:T(8,128)(2,1)S(1)} collective-permute-done((bf16[64,2560]{1,0:T(8,128)(2,1)S(1)}, bf16[64,2560]{1,0:T(8,128)(2,1)S(1)}, u32[]{:S(2)}, u32[]{:S(2)}) %collective-permute-start.1) | collective-permute-done | bytes 327712 | tf_op jit(solution)/shard_map/ppermute | solution.py:48
  30.0 0.0 collective-permute-start.5
  30.0 12.1 %collective-permute-done.2.refs_2_ = bf16[64,2560]{1,0:T(8,128)(2,1)S(1)} collective-permute-done((bf16[64,2560]{1,0:T(8,128)(2,1)S(1)}, bf16[64,2560]{1,0:T(8,128)(2,1)S(1)}, u32[]{:S(2)}, u32[]{:S(2)}) %collective-permute-start.2) | collective-permute-done | bytes 327712 | tf_op jit(solution)/shard_map/ppermute | solution.py:48
  42.0 0.0 collective-permute-start.6
  42.0 6.5 %collective-permute-done.3.refs_3_ = bf16[64,2560]{1,0:T(8,128)(2,1)} collective-permute-done((bf16[64,2560]{1,0:T(8,128)(2,1)S(1)}, bf16[64,2560]{1,0:T(8,128)(2,1)}, u32[]{:S(2)}, u32[]{:S(2)}) %collective-permute-start.3) | collective-permute-done | bytes 327712 | tf_op jit(solution)/shard_map/ppermute | solution.py:48
  48.6 0.7 stack.27.place_ref
  49.2 0.0 collective-permute-done.4.refs_4_
  49.2 0.0 collective-permute-done.5.refs_5_
  49.3 0.0 collective-permute-done.6.refs_6_
  49.3 1.1 %collective-permute-done.7.refs_7_ = bf16[64,2560]{1,0:T(8,128)(2,1)S(1)} collective-permute-done((bf16[64,2560]{1,0:T(8,128)(2,1)}, bf16[64,2560]{1,0:T(8,128)(2,1)S(1)}, u32[]{:S(2)}, u32[]{:S(2)}) %collective-permute-start.7) | collective-permute-done | bytes 327712 | tf_op jit(solution)/shard_map/ppermute | solution.py:39
  50.5 0.7 copy-done.12
  51.2 5.5 %shard_map.85 = (f32[128,2048]{1,0:T(8,128)}, bf16[128,2048]{1,0:T(8,128)(2,1)}, f32[1,2048]{1,0:T(1,128)}, bf16[2,64,256]{2,1,0:T(8,128)(2,1)}, bf16[2,64,256]{...) custom-call(s32[6]{0:T(128)} %stack.27.place_ref, bf16[64,2560]{1,0:T(8,128)(2,1)} %copy-done.4, ...), custom_call_target="tpu_custom_call" | custom-call | flops 1073741824 | bytes 6815744 | tf_op jit(solution)/shard_map/pallas_call | solution.py:139
  56.7 1.2 %collective-permute-start.12 = (bf16[2,64,256]{2,1,0:T(8,128)(2,1)}, bf16[2,64,256]{2,1,0:T(8,128)(2,1)S(1)}, u32[]{:S(2)}, u32[]{:S(2)}) collective-permute-start(bf16[2,64,256]{2,1,0:T(8,128)(2,1)} %get-tuple-element.12), channel_id=1, source_target_pairs={{0,4},{4,0},{8,12},{12,8},{1,5},{5,1},{9,13},{13,9},{2,6},{6,2},{1... | collective-permute-start | bytes 196616 | tf_op jit(solution)/shard_map/ppermute | solution.py:210
  57.9 0.5 collective-permute-start.13
  58.4 1.8 %collective-permute-start.14 = (bf16[2,64,256]{2,1,0:T(8,128)(2,1)}, bf16[2,64,256]{2,1,0:T(8,128)(2,1)S(1)}, u32[]{:S(2)}, u32[]{:S(2)}) collective-permute-start(bf16[2,64,256]{2,1,0:T(8,128)(2,1)} %get-tuple-element.14), channel_id=1, source_target_pairs={{0,12},{4,8},{8,4},{12,0},{1,13},{5,9},{9,5},{13,1},{2,14},{6,10},... | collective-permute-start | bytes 196616 | tf_op jit(solution)/shard_map/ppermute | solution.py:210
  60.3 0.6 broadcast.189
  60.8 1.3 %reduce.3 = f32[2048]{0:T(1024)S(1)} reduce(f32[1,2048]{1,0:T(1,128)} %get-tuple-element.15, f32[]{:T(128)} %broadcast.189), dimensions={0}, to_apply=%get-tuple-element.15.reduce_sub_computation.3 | reduce | bytes 16388 | tf_op jit(solution)/shard_map/pallas_call | solution.py:139
  62.2 0.8 collective-permute-start.17
  63.0 0.0 collective-permute-done.13
  63.0 0.9 collective-permute-done.14
  63.9 0.9 convert_add_fusion
  64.8 0.6 collective-permute-start.15
  65.4 4.4 %collective-permute-done.15 = f32[2,64,256]{2,1,0:T(8,128)S(1)} collective-permute-done((f32[2,64,256]{2,1,0:T(8,128)S(1)}, f32[2,64,256]{2,1,0:T(8,128)S(1)}, u32[]{:S(2)}, u32[]{:S(2)}) %collective-permute-start.15) | collective-permute-done | bytes 131104 | tf_op jit(solution)/shard_map/ppermute | solution.py:34
  69.8 0.0 copy-start.1
  69.8 0.1 collective-permute-start.16
  69.9 1.2 %collective-permute-done.16 = bf16[64,256]{1,0:T(8,128)(2,1)S(1)} collective-permute-done((bf16[64,256]{1,0:T(8,128)(2,1)S(1)}, bf16[64,256]{1,0:T(8,128)(2,1)S(1)}, u32[]{:S(2)}, u32[]{:S(2)}) %collective-permute-start.16) | collective-permute-done | bytes 32800 | tf_op jit(solution)/shard_map/ppermute | solution.py:39
  71.1 0.5 fusion.4
  71.6 0.7 pad_maximum_fusion.5
  72.3 3.9 %all-to-all-start.1 = ((bf16[16,16,512]{2,1,0:T(8,128)(2,1)}), bf16[16,16,512]{2,1,0:T(8,128)(2,1)S(1)}, u32[]{:S(2)}, u32[]{:S(2)}) async-start(bf16[16,16,512]{2,1,0:T(8,128)(2,1)} %pad_maximum_fusion.5), calls=%async_computation.1 | async-start | bytes 524288 | tf_op jit(solution)/shard_map/all_to_all | solution.py:256
  76.2 14.4 %collective-permute-done.17 = bf16[128,2048]{1,0:T(8,128)(2,1)S(1)} collective-permute-done((bf16[128,2048]{1,0:T(8,128)(2,1)}, bf16[128,2048]{1,0:T(8,128)(2,1)S(1)}, u32[]{:S(2)}, u32[]{:S(2)}) %collective-permute-start.17) | collective-permute-done | bytes 524320 | tf_op jit(solution)/shard_map/ppermute | solution.py:217
  90.6 0.1 multiply_convert_fusion
  90.8 1.2 %collective-permute-start.18 = (bf16[32,2048]{1,0:T(8,128)(2,1)S(1)}, bf16[32,2048]{1,0:T(8,128)(2,1)S(1)}, u32[]{:S(2)}, u32[]{:S(2)}) collective-permute-start(bf16[32,2048]{1,0:T(8,128)(2,1)S(1)} %get-tuple-element.25), channel_id=1, source_target_pairs={{0,4},{4,0},{8,12},{12,8},{1,5},{5,1},{9,13},{13,9},{2,6},{6,2},{1... | collective-permute-start | bytes 393224 | tf_op jit(solution)/shard_map/ppermute | solution.py:48
  92.0 2.3 %collective-permute-start.20 = (bf16[32,2048]{1,0:T(8,128)(2,1)S(1)}, bf16[32,2048]{1,0:T(8,128)(2,1)S(1)}, u32[]{:S(2)}, u32[]{:S(2)}) collective-permute-start(bf16[32,2048]{1,0:T(8,128)(2,1)S(1)} %get-tuple-element.23), channel_id=1, source_target_pairs={{0,12},{4,8},{8,4},{12,0},{1,13},{5,9},{9,5},{13,1},{2,14},{6,10},... | collective-permute-start | bytes 393224 | tf_op jit(solution)/shard_map/ppermute | solution.py:48
  94.3 0.1 broadcast_in_dim.35
  94.4 1.9 %collective-permute-done.18 = bf16[32,2048]{1,0:T(8,128)(2,1)S(1)} collective-permute-done((bf16[32,2048]{1,0:T(8,128)(2,1)S(1)}, bf16[32,2048]{1,0:T(8,128)(2,1)S(1)}, u32[]{:S(2)}, u32[]{:S(2)}) %collective-permute-start.18) | collective-permute-done | bytes 131104 | tf_op jit(solution)/shard_map/ppermute | solution.py:48
  96.4 2.0 %collective-permute-done.19 = bf16[32,2048]{1,0:T(8,128)(2,1)S(1)} collective-permute-done((bf16[32,2048]{1,0:T(8,128)(2,1)S(1)}, bf16[32,2048]{1,0:T(8,128)(2,1)S(1)}, u32[]{:S(2)}, u32[]{:S(2)}) %collective-permute-start.19) | collective-permute-done | bytes 131104 | tf_op jit(solution)/shard_map/ppermute | solution.py:48
  98.4 1.7 %collective-permute-done.20 = bf16[32,2048]{1,0:T(8,128)(2,1)S(1)} collective-permute-done((bf16[32,2048]{1,0:T(8,128)(2,1)S(1)}, bf16[32,2048]{1,0:T(8,128)(2,1)S(1)}, u32[]{:S(2)}, u32[]{:S(2)}) %collective-permute-start.20) | collective-permute-done | bytes 131104 | tf_op jit(solution)/shard_map/ppermute | solution.py:48
  100.2 0.0 copy-start.2
  100.2 0.8 slice_convert_fusion
  101.0 0.2 reshape.120
  101.2 0.2 reduce_sum.29
  101.4 0.6 div.49
  (46 shorter events, 0.3 us)
Async XLA Ops:
  0.6 16.2 %copy-start = (bf16[64,8192]{1,0:T(8,128)(2,1)S(1)}, bf16[64,8192]{1,0:T(8,128)(2,1)}, u32[]{:S(2)}) copy-start(bf16[64,8192]{1,0:T(8,128)(2,1)} %param.6) | copy-start | bytes 3145732
  0.6 16.0 %copy-start.6 = (s32[64]{0:T(128)S(1)}, s32[64]{0:T(128)}, u32[]{:S(2)}) copy-start(s32[64]{0:T(128)} %param.11) | copy-start | bytes 772
  0.7 16.2 %copy-start.5 = (f32[8192]{0:T(1024)S(1)}, f32[8192]{0:T(1024)}, u32[]{:S(2)}) copy-start(f32[8192]{0:T(1024)} %param.7) | copy-start | bytes 98308
  2.3 14.6 %collective-permute-start = (f32[64]{0:T(128)S(1)}, f32[64]{0:T(128)S(1)}, u32[]{:S(2)}, u32[]{:S(2)}) collective-permute-start(f32[64]{0:T(128)S(1)} %fusion), channel_id=1, source_target_pairs={{0,1},{1,0},{2,3},{3,2},{4,5},{5,4},{6,7},{7,6},{8,9},{9,8},{10,11... | collective-permute-start | bytes 776 | tf_op jit(solution)/shard_map/ppermute | solution.py:34
  5.3 14.4 %all-to-all-start = ((bf16[16,8,512]{2,1,0:T(8,128)(2,1)}), bf16[16,8,512]{2,1,0:T(8,128)(2,1)S(1)}, u32[]{:S(2)}, u32[]{:S(2)}) async-start(bf16[16,8,512]{2,1,0:T(8,128)(2,1)} %bitcast.25), calls=%async_computation | async-start | bytes 262144 | tf_op jit(solution)/shard_map/all_to_all | solution.py:186
  12.4 8.7 %collective-permute-start.10 = (bf16[32,2048]{1,0:T(8,128)(2,1)S(1)}, bf16[32,2048]{1,0:T(8,128)(2,1)S(1)}, u32[]{:S(2)}, u32[]{:S(2)}) collective-permute-start(bf16[32,2048]{1,0:T(8,128)(2,1)S(1)} %get-tuple-element.28), channel_id=1, source_target_pairs={{0,12},{4,8},{8,4},{12,0},{1,13},{5,9},{9,5},{13,1},{2,14},{6,10},... | collective-permute-start | bytes 393224 | tf_op jit(solution)/shard_map/ppermute | solution.py:48
  15.3 8.3 %collective-permute-start.8 = (bf16[32,2048]{1,0:T(8,128)(2,1)S(1)}, bf16[32,2048]{1,0:T(8,128)(2,1)S(1)}, u32[]{:S(2)}, u32[]{:S(2)}) collective-permute-start(bf16[32,2048]{1,0:T(8,128)(2,1)S(1)} %get-tuple-element.27), channel_id=1, source_target_pairs={{0,4},{4,0},{8,12},{12,8},{1,5},{5,1},{9,13},{13,9},{2,6},{6,2},{1... | collective-permute-start | bytes 393224 | tf_op jit(solution)/shard_map/ppermute | solution.py:48
  15.8 7.8 %collective-permute-start.9 = (bf16[32,2048]{1,0:T(8,128)(2,1)S(1)}, bf16[32,2048]{1,0:T(8,128)(2,1)S(1)}, u32[]{:S(2)}, u32[]{:S(2)}) collective-permute-start(bf16[32,2048]{1,0:T(8,128)(2,1)S(1)} %get-tuple-element.29), channel_id=1, source_target_pairs={{0,8},{4,12},{8,0},{12,4},{1,9},{5,13},{9,1},{13,5},{2,10},{6,14},... | collective-permute-start | bytes 393224 | tf_op jit(solution)/shard_map/ppermute | solution.py:48
  20.0 30.4 %copy-start.4 = (bf16[64,2560]{1,0:T(8,128)(2,1)}, bf16[64,2560]{1,0:T(8,128)(2,1)S(1)}, u32[]{:S(2)}) copy-start(bf16[64,2560]{1,0:T(8,128)(2,1)S(1)} %get-tuple-element.37.refs_0_) | copy-start | bytes 983044
  20.0 10.0 %collective-permute-start.1 = (bf16[64,2560]{1,0:T(8,128)(2,1)S(1)}, bf16[64,2560]{1,0:T(8,128)(2,1)S(1)}, u32[]{:S(2)}, u32[]{:S(2)}) collective-permute-start(bf16[64,2560]{1,0:T(8,128)(2,1)S(1)} %get-tuple-element.35), channel_id=1, source_target_pairs={{0,4},{4,0},{8,12},{12,8},{1,5},{5,1},{9,13},{13,9},{2,6},{6,2},{1... | collective-permute-start | bytes 983048 | tf_op jit(solution)/shard_map/ppermute | solution.py:48
  20.1 22.0 %collective-permute-start.2 = (bf16[64,2560]{1,0:T(8,128)(2,1)S(1)}, bf16[64,2560]{1,0:T(8,128)(2,1)S(1)}, u32[]{:S(2)}, u32[]{:S(2)}) collective-permute-start(bf16[64,2560]{1,0:T(8,128)(2,1)S(1)} %get-tuple-element.36), channel_id=1, source_target_pairs={{0,8},{4,12},{8,0},{12,4},{1,9},{5,13},{9,1},{13,5},{2,10},{6,14},... | collective-permute-start | bytes 983048 | tf_op jit(solution)/shard_map/ppermute | solution.py:48
  21.1 27.5 %collective-permute-start.3 = (bf16[64,2560]{1,0:T(8,128)(2,1)S(1)}, bf16[64,2560]{1,0:T(8,128)(2,1)}, u32[]{:S(2)}, u32[]{:S(2)}) collective-permute-start(bf16[64,2560]{1,0:T(8,128)(2,1)S(1)} %get-tuple-element.34), channel_id=1, source_target_pairs={{0,12},{4,8},{8,4},{12,0},{1,13},{5,9},{9,5},{13,1},{2,14},{6,10},... | collective-permute-start | bytes 983048 | tf_op jit(solution)/shard_map/ppermute | solution.py:48
  23.6 26.8 %copy-start.3 = (bf16[128,2048]{1,0:T(8,128)(2,1)}, bf16[128,2048]{1,0:T(8,128)(2,1)S(1)}, u32[]{:S(2)}) copy-start(bf16[128,2048]{1,0:T(8,128)(2,1)S(1)} %pad_maximum_fusion.4.refs_8_) | copy-start | bytes 1572868
  23.6 25.6 %collective-permute-start.11 = (bf16[128,2048]{1,0:T(8,128)(2,1)S(1)}, bf16[128,2048]{1,0:T(8,128)(2,1)S(1)}, u32[]{:S(2)}, u32[]{:S(2)}) collective-permute-start(bf16[128,2048]{1,0:T(8,128)(2,1)S(1)} %pad_maximum_fusion.4.refs_8_), channel_id=1, source_target_pairs={{0,16},{16,0},{1,17},{17,1},{2,18},{18,2},{3,19},{19,3},{4,20},{20... | collective-permute-start | bytes 1572872 | tf_op jit(solution)/shard_map/ppermute | solution.py:184
  25.5 23.7 %collective-permute-start.4 = (bf16[64,2560]{1,0:T(8,128)(2,1)S(1)}, bf16[64,2560]{1,0:T(8,128)(2,1)S(1)}, u32[]{:S(2)}, u32[]{:S(2)}) collective-permute-start(bf16[64,2560]{1,0:T(8,128)(2,1)S(1)} %get-tuple-element.37.refs_0_), channel_id=1, source_target_pairs={{0,2},{2,0},{1,3},{3,1},{4,6},{6,4},{5,7},{7,5},{8,10},{10,8},{9,1... | collective-permute-start | bytes 983048 | tf_op jit(solution)/shard_map/ppermute | solution.py:39
  30.0 20.4 %copy-start.8 = (bf16[64,2560]{1,0:T(8,128)(2,1)}, bf16[64,2560]{1,0:T(8,128)(2,1)S(1)}, u32[]{:S(2)}) copy-start(bf16[64,2560]{1,0:T(8,128)(2,1)S(1)} %collective-permute-done.1.refs_1_) | copy-start | bytes 983044
  30.0 19.3 %collective-permute-start.5 = (bf16[64,2560]{1,0:T(8,128)(2,1)S(1)}, bf16[64,2560]{1,0:T(8,128)(2,1)S(1)}, u32[]{:S(2)}, u32[]{:S(2)}) collective-permute-start(bf16[64,2560]{1,0:T(8,128)(2,1)S(1)} %collective-permute-done.1.refs_1_), channel_id=1, source_target_pairs={{0,2},{2,0},{1,3},{3,1},{4,6},{6,4},{5,7},{7,5},{8,10},{10,8},{9,1... | collective-permute-start | bytes 983048 | tf_op jit(solution)/shard_map/ppermute | solution.py:39
  42.0 8.4 %copy-start.9 = (bf16[64,2560]{1,0:T(8,128)(2,1)}, bf16[64,2560]{1,0:T(8,128)(2,1)S(1)}, u32[]{:S(2)}) copy-start(bf16[64,2560]{1,0:T(8,128)(2,1)S(1)} %collective-permute-done.2.refs_2_) | copy-start | bytes 983044
  42.0 7.2 %collective-permute-start.6 = (bf16[64,2560]{1,0:T(8,128)(2,1)S(1)}, bf16[64,2560]{1,0:T(8,128)(2,1)}, u32[]{:S(2)}, u32[]{:S(2)}) collective-permute-start(bf16[64,2560]{1,0:T(8,128)(2,1)S(1)} %collective-permute-done.2.refs_2_), channel_id=1, source_target_pairs={{0,2},{2,0},{1,3},{3,1},{4,6},{6,4},{5,7},{7,5},{8,10},{10,8},{9,1... | collective-permute-start | bytes 983048 | tf_op jit(solution)/shard_map/ppermute | solution.py:39
  48.6 1.8 %collective-permute-start.7 = (bf16[64,2560]{1,0:T(8,128)(2,1)}, bf16[64,2560]{1,0:T(8,128)(2,1)S(1)}, u32[]{:S(2)}, u32[]{:S(2)}) collective-permute-start(bf16[64,2560]{1,0:T(8,128)(2,1)} %collective-permute-done.3.refs_3_), channel_id=1, source_target_pairs={{0,2},{2,0},{1,3},{3,1},{4,6},{6,4},{5,7},{7,5},{8,10},{10,8},{9,1... | collective-permute-start | bytes 983048 | tf_op jit(solution)/shard_map/ppermute | solution.py:39
  49.2 1.2 %copy-start.10 = (bf16[64,2560]{1,0:T(8,128)(2,1)}, bf16[64,2560]{1,0:T(8,128)(2,1)S(1)}, u32[]{:S(2)}) copy-start(bf16[64,2560]{1,0:T(8,128)(2,1)S(1)} %collective-permute-done.4.refs_4_) | copy-start | bytes 983044
  49.2 1.2 %copy-start.7 = (bf16[128,2048]{1,0:T(8,128)(2,1)}, bf16[128,2048]{1,0:T(8,128)(2,1)S(1)}, u32[]{:S(2)}) copy-start(bf16[128,2048]{1,0:T(8,128)(2,1)S(1)} %collective-permute-done.11.refs_9_) | copy-start | bytes 1572868
  49.3 1.2 %copy-start.11 = (bf16[64,2560]{1,0:T(8,128)(2,1)}, bf16[64,2560]{1,0:T(8,128)(2,1)S(1)}, u32[]{:S(2)}) copy-start(bf16[64,2560]{1,0:T(8,128)(2,1)S(1)} %collective-permute-done.5.refs_5_) | copy-start | bytes 983044
  50.5 0.7 copy-start.12
  56.7 6.3 %collective-permute-start.12 = (bf16[2,64,256]{2,1,0:T(8,128)(2,1)}, bf16[2,64,256]{2,1,0:T(8,128)(2,1)S(1)}, u32[]{:S(2)}, u32[]{:S(2)}) collective-permute-start(bf16[2,64,256]{2,1,0:T(8,128)(2,1)} %get-tuple-element.12), channel_id=1, source_target_pairs={{0,4},{4,0},{8,12},{12,8},{1,5},{5,1},{9,13},{13,9},{2,6},{6,2},{1... | collective-permute-start | bytes 196616 | tf_op jit(solution)/shard_map/ppermute | solution.py:210
  57.9 5.1 %collective-permute-start.13 = (bf16[2,64,256]{2,1,0:T(8,128)(2,1)}, bf16[2,64,256]{2,1,0:T(8,128)(2,1)S(1)}, u32[]{:S(2)}, u32[]{:S(2)}) collective-permute-start(bf16[2,64,256]{2,1,0:T(8,128)(2,1)} %get-tuple-element.13), channel_id=1, source_target_pairs={{0,8},{4,12},{8,0},{12,4},{1,9},{5,13},{9,1},{13,5},{2,10},{6,14},... | collective-permute-start | bytes 196616 | tf_op jit(solution)/shard_map/ppermute | solution.py:210
  58.4 5.5 %collective-permute-start.14 = (bf16[2,64,256]{2,1,0:T(8,128)(2,1)}, bf16[2,64,256]{2,1,0:T(8,128)(2,1)S(1)}, u32[]{:S(2)}, u32[]{:S(2)}) collective-permute-start(bf16[2,64,256]{2,1,0:T(8,128)(2,1)} %get-tuple-element.14), channel_id=1, source_target_pairs={{0,12},{4,8},{8,4},{12,0},{1,13},{5,9},{9,5},{13,1},{2,14},{6,10},... | collective-permute-start | bytes 196616 | tf_op jit(solution)/shard_map/ppermute | solution.py:210
  62.2 28.4 %collective-permute-start.17 = (bf16[128,2048]{1,0:T(8,128)(2,1)}, bf16[128,2048]{1,0:T(8,128)(2,1)S(1)}, u32[]{:S(2)}, u32[]{:S(2)}) collective-permute-start(bf16[128,2048]{1,0:T(8,128)(2,1)} %get-tuple-element.18), channel_id=1, source_target_pairs={{0,16},{16,0},{1,17},{17,1},{2,18},{18,2},{3,19},{19,3},{4,20},{20... | collective-permute-start | bytes 1572872 | tf_op jit(solution)/shard_map/ppermute | solution.py:217
  64.8 5.0 %collective-permute-start.15 = (f32[2,64,256]{2,1,0:T(8,128)S(1)}, f32[2,64,256]{2,1,0:T(8,128)S(1)}, u32[]{:S(2)}, u32[]{:S(2)}) collective-permute-start(f32[2,64,256]{2,1,0:T(8,128)S(1)} %convert_add_fusion), channel_id=1, source_target_pairs={{0,1},{1,0},{2,3},{3,2},{4,5},{5,4},{6,7},{7,6},{8,9},{9,8},{10,11... | collective-permute-start | bytes 393224 | tf_op jit(solution)/shard_map/ppermute | solution.py:34
  69.8 20.8 %copy-start.1 = (f32[128,2048]{1,0:T(8,128)S(1)}, f32[128,2048]{1,0:T(8,128)}, u32[]{:S(2)}) copy-start(f32[128,2048]{1,0:T(8,128)} %get-tuple-element.17) | copy-start | bytes 3145732
  69.8 1.3 %collective-permute-start.16 = (bf16[64,256]{1,0:T(8,128)(2,1)S(1)}, bf16[64,256]{1,0:T(8,128)(2,1)S(1)}, u32[]{:S(2)}, u32[]{:S(2)}) collective-permute-start(bf16[64,256]{1,0:T(8,128)(2,1)S(1)} %get-tuple-element.33), channel_id=1, source_target_pairs={{0,2},{2,0},{1,3},{3,1},{4,6},{6,4},{5,7},{7,5},{8,10},{10,8},{9,1... | collective-permute-start | bytes 98312 | tf_op jit(solution)/shard_map/ppermute | solution.py:39
  72.3 27.9 %all-to-all-start.1 = ((bf16[16,16,512]{2,1,0:T(8,128)(2,1)}), bf16[16,16,512]{2,1,0:T(8,128)(2,1)S(1)}, u32[]{:S(2)}, u32[]{:S(2)}) async-start(bf16[16,16,512]{2,1,0:T(8,128)(2,1)} %pad_maximum_fusion.5), calls=%async_computation.1 | async-start | bytes 524288 | tf_op jit(solution)/shard_map/all_to_all | solution.py:256
  90.8 5.6 %collective-permute-start.18 = (bf16[32,2048]{1,0:T(8,128)(2,1)S(1)}, bf16[32,2048]{1,0:T(8,128)(2,1)S(1)}, u32[]{:S(2)}, u32[]{:S(2)}) collective-permute-start(bf16[32,2048]{1,0:T(8,128)(2,1)S(1)} %get-tuple-element.25), channel_id=1, source_target_pairs={{0,4},{4,0},{8,12},{12,8},{1,5},{5,1},{9,13},{13,9},{2,6},{6,2},{1... | collective-permute-start | bytes 393224 | tf_op jit(solution)/shard_map/ppermute | solution.py:48
  92.0 6.4 %collective-permute-start.19 = (bf16[32,2048]{1,0:T(8,128)(2,1)S(1)}, bf16[32,2048]{1,0:T(8,128)(2,1)S(1)}, u32[]{:S(2)}, u32[]{:S(2)}) collective-permute-start(bf16[32,2048]{1,0:T(8,128)(2,1)S(1)} %get-tuple-element.24), channel_id=1, source_target_pairs={{0,8},{4,12},{8,0},{12,4},{1,9},{5,13},{9,1},{13,5},{2,10},{6,14},... | collective-permute-start | bytes 393224 | tf_op jit(solution)/shard_map/ppermute | solution.py:48
  92.0 8.2 %collective-permute-start.20 = (bf16[32,2048]{1,0:T(8,128)(2,1)S(1)}, bf16[32,2048]{1,0:T(8,128)(2,1)S(1)}, u32[]{:S(2)}, u32[]{:S(2)}) collective-permute-start(bf16[32,2048]{1,0:T(8,128)(2,1)S(1)} %get-tuple-element.23), channel_id=1, source_target_pairs={{0,12},{4,8},{8,4},{12,0},{1,13},{5,9},{9,5},{13,1},{2,14},{6,10},... | collective-permute-start | bytes 393224 | tf_op jit(solution)/shard_map/ppermute | solution.py:48
  100.2 1.8 %copy-start.2 = (f32[32,8192]{1,0:T(8,128)}, f32[32,8192]{1,0:T(8,128)S(1)}, u32[]{:S(2)}) copy-start(f32[32,8192]{1,0:T(8,128)S(1)} %convert_dynamic-update-slice_fusion) | copy-start | bytes 3145732

commit v4 on v3

--- a/solution.py
+++ b/solution.py
@@ -14,6 +14,8 @@
 DP = ("hi", "lo", "core")
 SWAP = [(0, 1), (1, 0)]
 FEW = 4
+EARLY = 7
+LANES = 128
 CHUNK = 512
 
 
@@ -65,46 +67,39 @@
 
 def products_kernel(pieces, owned, low, core_keys, part, chunk, place_ref, *refs):
     row_refs, weight_refs = refs[: 2 * pieces], refs[2 * pieces : 2 * pieces + 2]
-    own_ref, away_ref, gain_ref = refs[2 * pieces + 2 : 2 * pieces + 5]
-    key_refs = refs[2 * pieces + 5 : 3 * pieces + 5]
-    rows_ref, weights_ref, cot_ref, sums_ref, row_sem, weight_sem = refs[3 * pieces + 5 :]
+    grad_ref, gain_ref = refs[2 * pieces + 2 : 2 * pieces + 4]
+    key_refs = refs[2 * pieces + 4 : 3 * pieces + 4]
+    rows_ref, cot_ref, weights_ref, sums_ref, row_sem, cot_sem, weight_sem = refs[
+        3 * pieces + 4 :
+    ]
     piece_rows = row_refs[0].shape[0]
     half_keys = core_keys // 2
     key_width = 2 * core_keys
 
-    row_copies = [
-        pltpu.make_async_copy(
-            ref, rows_ref.at[pl.ds(j * piece_rows, piece_rows)], row_sem.at[j]
-        )
-        for j, ref in enumerate(row_refs)
-    ]
-    weight_copies = []
+    copies = []
+    for j, ref in enumerate(row_refs):
+        at = pl.ds(j * piece_rows, piece_rows)
+        first = part + j // pieces * core_keys
+        for source, to, sem in (
+            (ref.at[:, pl.ds(0, part)], rows_ref, row_sem),
+            (ref.at[:, pl.ds(first, core_keys)], cot_ref, cot_sem),
+        ):
+            copies.append(pltpu.make_async_copy(source, to.at[at], sem.at[j]))
     block = half_keys // pieces
     for j in range(2 * pieces):
-        first = place_ref[2 + j % pieces] * owned + (j // pieces) * half_keys
+        first = place_ref[2 + j % pieces] * owned + (place_ref[0] ^ (j // pieces)) * half_keys
         if owned % 16 == 0:
             first = pl.multiple_of(first, 16)
-        weight_copies.append(
+        copies.append(
             pltpu.make_async_copy(
                 weight_refs[j // pieces].at[pl.ds((j % pieces) * block, block)],
                 weights_ref.at[pl.ds(first, block)],
                 weight_sem.at[j],
             )
         )
-    for copy in row_copies + weight_copies:
+    for copy in copies:
         copy.start()
-    for copy in row_copies:
-        copy.wait()
-
-    column = iota2((key_width, core_keys), 1)
-    half = place_ref[0] ^ (column // half_keys)
-    whole = ((half * low + (column % half_keys) // owned) * 2 + place_ref[1]) * owned
-    whole = whole + column % owned
-    chosen = jnp.where(iota2((key_width, core_keys), 0) == whole, 1.0, 0.0).astype(jnp.bfloat16)
-    cot_ref[...] = lax.dot_general(
-        rows_ref[:, part:], chosen, (((1,), (0,)), ((), ())), preferred_element_type=jnp.float32
-    ).astype(jnp.bfloat16)
-    for copy in weight_copies:
+    for copy in copies:
         copy.wait()
 
     for c in range(part // chunk):
@@ -114,8 +109,7 @@
         grad = lax.dot_general(
             cot_ref[...], rows, (((0,), (0,)), ((), ())), preferred_element_type=jnp.float32
         )
-        own_ref[:, at] = grad[:half_keys]
-        away_ref[:, at] = grad[half_keys:].astype(jnp.bfloat16)
+        grad_ref[:, at] = grad.astype(jnp.bfloat16)
         gain_ref[:, at] = jnp.sum(grad * weights.astype(jnp.float32), axis=0, keepdims=True)
         term = lax.dot_general(
             rows, weights, (((1,), (1,)), ((), ())), preferred_element_type=jnp.float32
@@ -141,18 +135,18 @@
             products_kernel, pieces, owned, low, core_keys, part, min(CHUNK, part)
         ),
         out_shape=[
-            jax.ShapeDtypeStruct((half_keys, part), jnp.float32),
-            jax.ShapeDtypeStruct((half_keys, part), jnp.bfloat16),
+            jax.ShapeDtypeStruct((core_keys, part), jnp.bfloat16),
             jax.ShapeDtypeStruct((1, part), jnp.float32),
         ]
         + [jax.ShapeDtypeStruct((2, piece_rows, core_keys), jnp.bfloat16)] * pieces,
         in_specs=[pl.BlockSpec(memory_space=pltpu.SMEM)]
         + [pl.BlockSpec(memory_space=pl.ANY)] * (2 * pieces + 2),
         scratch_shapes=[
-            pltpu.VMEM((total, columns), jnp.bfloat16),
+            pltpu.VMEM((total, part), jnp.bfloat16),
+            pltpu.VMEM((total, core_keys), jnp.bfloat16),
             pltpu.VMEM((core_keys, part), jnp.bfloat16),
-            pltpu.VMEM((total, core_keys), jnp.bfloat16),
             pltpu.VMEM((total, core_keys), jnp.float32),
+            pltpu.SemaphoreType.DMA((2 * pieces,)),
             pltpu.SemaphoreType.DMA((2 * pieces,)),
             pltpu.SemaphoreType.DMA((2 * pieces,)),
         ],
@@ -165,9 +159,64 @@
     )(scalars, *rows_here, *rows_there, *weights)
 
 
+def sum_kernel(factor, terms_ref, grad_ref):
+    low, _, part = terms_ref.shape[1:]
+    for j in range(low):
+        total = terms_ref[0, j].astype(jnp.float32) + terms_ref[1, j].astype(jnp.float32)
+        grad_ref[:, pl.ds(j * part, part)] = total * factor
+
+
+def sum_terms(terms, factor):
+    _, low, owned, part = terms.shape
+    return pl.pallas_call(
+        functools.partial(sum_kernel, factor),
+        out_shape=jax.ShapeDtypeStruct((owned, low * part), jnp.float32),
+        in_specs=[pl.BlockSpec(memory_space=pltpu.VMEM)],
+        out_specs=pl.BlockSpec(memory_space=pltpu.VMEM),
+        compiler_params=pltpu.CompilerParams(vmem_limit_bytes=32 * 1024 * 1024),
+        cost_estimate=pl.CostEstimate(
+            flops=2 * terms.size, bytes_accessed=4 * terms.size, transcendentals=0
+        ),
+    )(terms)
+
+
+def gather_kernel(key_rows, factor, place_ref, *refs):
+    pieces, norm_ref, key_ref, gain_ref = refs[:-3], refs[-3], refs[-2], refs[-1]
+    low, columns = len(pieces) // 2, key_ref.shape[1]
+    half_rows, wide = (pieces[0].shape[0] - key_rows) // 2, columns // LANES
+    for step, piece in enumerate(pieces):
+        at = pl.multiple_of((place_ref[0] ^ step) * key_rows, key_rows)
+        key_ref[pl.ds(at, key_rows)] = piece[:key_rows]
+    for step in range(low):
+        total = jnp.zeros((half_rows, columns), jnp.float32)
+        for piece in pieces[step::low]:
+            terms = piece[key_rows:].astype(jnp.float32)
+            total = total + terms[:half_rows] + terms[half_rows:]
+        for i in range(half_rows):
+            for j in range(wide):
+                at = pl.ds(((place_ref[1] ^ step) * half_rows + i) * wide + j, 1)
+                sums = total[i : i + 1, j * LANES : (j + 1) * LANES]
+                gain_ref[at] = sums * factor / norm_ref[at]
+
+
+def gather_pieces(pieces, norm_gain, chip, key_rows, factor):
+    places = jnp.stack([chip, lax.axis_index("lo")]).astype(jnp.int32)
+    key_width, width = pieces[0].shape[1], norm_gain.shape[0]
+    return pl.pallas_call(
+        functools.partial(gather_kernel, key_rows, factor),
+        out_shape=[
+            jax.ShapeDtypeStruct((len(pieces) * key_rows, key_width), jnp.bfloat16),
+            jax.ShapeDtypeStruct((width // LANES, LANES), jnp.float32),
+        ],
+        in_specs=[pl.BlockSpec(memory_space=pltpu.SMEM)]
+        + [pl.BlockSpec(memory_space=pltpu.VMEM)] * (len(pieces) + 1),
+        out_specs=[pl.BlockSpec(memory_space=pltpu.VMEM)] * 2,
+    )(places, *pieces, norm_gain.reshape(width // LANES, LANES))
+
+
 def on_device(hidden_rows, norm_gain, key_weight, cotangent, accepted_counts, destination):
     halves, low, cores = lax.axis_size("hi"), lax.axis_size("lo"), lax.axis_size("core")
-    hi, core = lax.axis_index("hi"), lax.axis_index("core")
+    hi, lo, core = (lax.axis_index(name) for name in DP)
     replicas = halves * low * cores
     rows, width = hidden_rows.shape
     model_width = width * lax.axis_size("tensor")
@@ -185,7 +234,16 @@
 
     returned = lax.all_to_all(cotangent[0], DP, split_axis=0, concat_axis=0, tiled=True)
     accepted, onehot = slot_onehot(destination, accepted_counts[0], replicas, capacity)
-    row_cot = select(onehot, returned)
+    place = lax.iota(jnp.int32, key_width)
+    from_core = core ^ (place // core_keys)
+    whole = ((place % core_keys) // owned * cores + from_core) * owned + place % owned
+    by_core = one_hot(whole, key_width)
+    row_cot = lax.dot_general(
+        select(onehot, returned),
+        by_core,
+        (((1,), (1,)), ((), ())),
+        preferred_element_type=jnp.float32,
+    ).astype(jnp.bfloat16)
 
     row_float = hidden_rows.astype(jnp.float32)
     squares = jnp.sum(row_float * row_float, axis=1)
@@ -200,7 +258,7 @@
         )
     )
     rows_there = [swap_core(piece) for piece in rows_here]
-    grad_own, grad_away, gain_part, *key_parts = products(
+    grad_part, gain_part, *key_parts = products(
         rows_here, rows_there, (weight_here, weight_there), places, core_keys, part, owned
     )
     gain_part = gain_part[0]
@@ -214,53 +272,59 @@
         sent = key_parts[0].reshape(2, low, rows, core_keys).transpose(1, 0, 2, 3)
         got = lax.all_to_all(sent, "lo", split_axis=0, concat_axis=0, tiled=True)
         key_terms = [got[j] for j in range(low)]
-    grad_away = lax.ppermute(grad_away, "hi", SWAP)
+    grad_terms = lax.all_to_all(
+        grad_part.reshape(halves * low, owned, part),
+        ("hi", "lo"),
+        split_axis=0,
+        concat_axis=0,
+        tiled=True,
+    ).reshape(halves, low, owned, part)
     key_sum = sum(term.astype(jnp.float32) for term in key_terms)
     chip_keys = reduce_tensor(key_sum).astype(jnp.bfloat16)
     row_keys = jnp.concatenate([chip_keys[0], swap_core(chip_keys[1])], axis=1)
     key_slots = lax.dot_general(
         onehot, row_keys, (((0,), (0,)), ((), ())), preferred_element_type=jnp.float32
     ).astype(jnp.bfloat16)
-    place = lax.iota(jnp.int32, key_width)
-    from_core = core ^ (place // core_keys)
-    from_half = hi ^ ((place % core_keys) // half_keys)
-    whole = ((from_half * low + (place % half_keys) // owned) * cores + from_core) * owned
-    key_slots = select(key_slots, one_hot(whole + place % owned, key_width))
+    key_slots = select(key_slots, by_core)
+
+    key_slots = key_slots.reshape(halves * low, cores, capacity, key_width)
+    mine = lax.dynamic_index_in_dim(key_slots, core, 1, keepdims=False)
+    other = swap_core(lax.dynamic_index_in_dim(key_slots, 1 - core, 1, keepdims=False))
+    mine, other = jnp.where(core == 0, mine, other), jnp.where(core == 0, other, mine)
+    gain_part = gain_part + swap_core(gain_part)
     upper = lax.reduce_precision(gain_part, 8, 7)
     terms = jnp.concatenate([upper, gain_part - upper]).astype(jnp.bfloat16)
     extra = -(-2 * part // (8 * key_width)) * 8
     terms = jnp.pad(terms, (0, extra * key_width - 2 * part)).reshape(1, extra, key_width)
     routed = jnp.concatenate(
-        [
-            key_slots.reshape(replicas, capacity, key_width),
-            jnp.broadcast_to(terms, (replicas, extra, key_width)),
-        ],
-        axis=1,
-    )
-
-    grad_own, _ = lax.optimization_barrier((grad_own, routed))
-    grad_own = ((grad_own + grad_away.astype(jnp.float32)) * factor).astype(jnp.bfloat16)
-    grad_terms, _ = swap_lo(
-        lambda j: lax.dynamic_slice(grad_own, (j * owned, 0), (owned, part))
-    )
+        [mine, other, jnp.broadcast_to(terms, (halves * low, extra, key_width))], axis=1
+    )
+    late, grad_terms = lax.optimization_barrier((routed, grad_terms))
+    grad_weight = sum_terms(grad_terms, factor)
     if low <= FEW:
-        grad_weight = jnp.zeros((owned, width), jnp.float32)
-        for place, term in zip(places, grad_terms):
-            grad_weight = lax.dynamic_update_slice(
-                grad_weight, term.astype(jnp.float32), (0, place * part)
+        pieces = [
+            lax.ppermute(
+                lax.dynamic_index_in_dim(
+                    routed if step < EARLY else late, (hi * low + lo) ^ step, 0, keepdims=False
+                ),
+                ("hi", "lo"),
+                [(j, j ^ step) for j in range(halves * low)],
             )
+            for step in range(1, halves * low)
+        ]
+        own = lax.dynamic_index_in_dim(routed, hi * low + lo, 0, keepdims=False)
+        key_out, grad_gain = gather_pieces(
+            [own] + pieces, norm_gain, hi * low + lo, cores * capacity, factor
+        )
+        grad_gain = grad_gain.reshape(width)
     else:
-        grad_weight = grad_terms[0].reshape(low, owned, part).transpose(1, 0, 2)
-        grad_weight = grad_weight.reshape(owned, width).astype(jnp.float32)
-
-    routed = lax.all_to_all(routed, DP, split_axis=0, concat_axis=0, tiled=True)
-    key_out = routed[:, :capacity].reshape(1, replicas * capacity, key_width)
-    gain_terms = routed[:, capacity:].reshape(replicas, extra * key_width)[:, : 2 * part]
-    gain_sums = jnp.sum(
-        gain_terms.astype(jnp.float32).reshape(halves, low, cores, 2, part), axis=(0, 2, 3)
-    )
-    grad_gain = gain_sums.reshape(width) * factor / norm_gain
-    return (key_out, grad_weight, grad_gain)
+        routed = lax.all_to_all(routed, ("hi", "lo"), split_axis=0, concat_axis=0, tiled=True)
+        key_out = routed[:, : cores * capacity].reshape(replicas * capacity, key_width)
+        gain_sums = routed[:, cores * capacity :].reshape(halves, low, extra * key_width)
+        gain_sums = gain_sums[:, :, : 2 * part].astype(jnp.float32)
+        gain_sums = jnp.sum(gain_sums.reshape(halves, low, 2, part), axis=(0, 2))
+        grad_gain = gain_sums.reshape(width) * factor / norm_gain
+    return (key_out[None], grad_weight, grad_gain)
 
 
 def solution(mesh):

time: 102 us -> 100 us (0.980)
  waiting for transfers between devices: 53 us -> 44.4 us
  starting transfers between devices: 30.4 us -> 38.4 us
  other arithmetic: 7.1 us -> 3.07 us
  Pallas kernels: 5.51 us -> 7.8 us
    ppermute x1 -> x7, waiting for transfers between devices: 14.4 us -> 0.89 us  [on_device(): lax.ppermute(lax.dynamic_index_in_dim(routed if step < EARLY else late, h...]
    ppermute x1 -> x7, starting transfers between devices: 0.8 us -> 12.4 us  [on_device(): lax.ppermute(lax.dynamic_index_in_dim(routed if step < EARLY else late, h...]
    all_to_all x1, waiting for transfers between devices: 0.01 us -> 10.5 us  [on_device(): lax.all_to_all(grad_part.reshape(halves * low, owned, part), ('hi', 'lo')...]
    ppermute x9 -> x6, waiting for transfers between devices: 28.7 us -> 22.9 us  [swap_lo(): pieces.append(lax.ppermute(block(me ^ step), 'lo', pairs))]
    ppermute x9 -> x6, starting transfers between devices: 10.7 us -> 7.11 us  [swap_lo(): pieces.append(lax.ppermute(block(me ^ step), 'lo', pairs))]
    pallas_call x0 -> x2, Pallas kernels: none -> 2.7 us  [the longest x1 1.59 us: gather_pieces(): pl.pallas_call(functools.partial(gather_kernel, key_rows, factor), out_sh...]
    pallas_call x1 -> x0, other arithmetic: 1.35 us -> none  [products(): pl.pallas_call(functools.partial(products_kernel, pieces, owned, low, cor...]
    ppermute x5 -> x7, waiting for transfers between devices: 2.31 us -> 3.32 us  [swap_core(): return lax.ppermute(value, 'core', SWAP)]
  transfers between devices with their start and end apart: 23 -> 28, of which waited for: 12 -> 10; matrix products, arithmetic and copies ran while one was open for 7% -> 5% of each run, Pallas kernels for 0% -> 1%
where the time goes in v4:
time: 100 us; the launch traced here: 99.5 us
  waiting for transfers between devices  44.4 us (44%)
  starting transfers between devices  38.4 us (38%)
  Pallas kernels  7.8 us (8%)
  local copies, waits for them, and re-layouts  3.2 us (3%)
  other arithmetic  3.07 us (3%)
  between operations  1.76 us (2%)
    ppermute x6, waiting for transfers between devices, swap_lo(): pieces.append(lax.ppermute(block(me ^ step), 'lo', pairs))  22.9 us
    ppermute x7, starting transfers between devices, on_device(): lax.ppermute(lax.dynamic_index_in_dim(routed if step < EARLY else late, h...  12.4 us
    all_to_all x1, waiting for transfers between devices, on_device(): lax.all_to_all(grad_part.reshape(halves * low, owned, part), ('hi', 'lo')...  10.5 us
    ppermute x6, starting transfers between devices, swap_lo(): pieces.append(lax.ppermute(block(me ^ step), 'lo', pairs))  7.11 us
    all_to_all x1, starting transfers between devices, on_device(): lax.all_to_all(cotangent[0], DP, split_axis=0, concat_axis=0, tiled=True)  5.94 us
    pallas_call x1, Pallas kernels, products(): pl.pallas_call(functools.partial(products_kernel, pieces, owned, low, cor...  5.1 us
    ppermute x2, waiting for transfers between devices, reduce_tensor(): return value + lax.ppermute(value, 'tensor', SWAP)  4.43 us
    all_to_all x1, starting transfers between devices, on_device(): lax.all_to_all(grad_part.reshape(halves * low, owned, part), ('hi', 'lo')...  3.78 us
  transfers between devices with their start and end apart: 28, of which 10 were waited for; matrix products, arithmetic and copies ran while one was open for 5% of the time, Pallas kernels for 1%

profile of v4, /device:TPU:0, one launch (start us, length us, event | category | flops | bytes accessed | tf_op | source)
XLA Modules:
  0.0 99.5 jit_solution(11256985571742042706)
XLA Ops:
  0.6 0.0 copy-start.3
  0.7 1.6 %fusion = f32[64]{0:T(128)S(1)} fusion(bf16[64,8192]{1,0:T(8,128)(2,1)} %param.6), kind=kLoop, calls=%fused_computation.2 | loop fusion | flops 1572800 | bytes 1048832 | tf_op jit(solution)/shard_map/reduce_sum | solution.py:249
  2.3 3.0 %collective-permute-start = (f32[64]{0:T(128)S(1)}, f32[64]{0:T(128)S(1)}, u32[]{:S(2)}, u32[]{:S(2)}) collective-permute-start(f32[64]{0:T(128)S(1)} %fusion), channel_id=1, source_target_pairs={{0,1},{1,0},{2,3},{3,2},{4,5},{5,4},{6,7},{7,6},{8,9},{9,8},{10,11... | collective-permute-start | bytes 776 | tf_op jit(solution)/shard_map/ppermute | solution.py:36
  5.3 5.9 %all-to-all-start = ((bf16[16,8,512]{2,1,0:T(8,128)(2,1)}), bf16[16,8,512]{2,1,0:T(8,128)(2,1)S(1)}, u32[]{:S(2)}, u32[]{:S(2)}) async-start(bf16[16,8,512]{2,1,0:T(8,128)(2,1)} %bitcast.50), calls=%async_computation | async-start | bytes 262144 | tf_op jit(solution)/shard_map/all_to_all | solution.py:235
  11.2 1.1 %constant_dynamic-slice_fusion.3 = (bf16[32,2048]{1,0:T(8,128)(2,1)S(1)}, bf16[32,2048]{1,0:T(8,128)(2,1)S(1)}, bf16[32,2048]{1,0:T(8,128)(2,1)S(1)}, bf16[32,2048]{1,0:T(8,128)(2,1)S(1)}) fusion(bf16[32,8192]{1,0:T(8,128)(2,1)} %param.8, s32[]{:T(128)S(6)} %select_n.106, s32[]{:T(128)S(6)} %select_n.111, s32[]{:T(128)S(6)} %select_n.113, s32[]{:T(128)S(6)} %select_n.112), kind=kLoop, calls=%fused_computation.51 | loop fusion | bytes 1048592 | tf_op jit(solution)/shard_map/dynamic_slice | solution.py:230
  12.4 2.9 %collective-permute-start.10 = (bf16[32,2048]{1,0:T(8,128)(2,1)S(1)}, bf16[32,2048]{1,0:T(8,128)(2,1)S(1)}, u32[]{:S(2)}, u32[]{:S(2)}) collective-permute-start(bf16[32,2048]{1,0:T(8,128)(2,1)S(1)} %get-tuple-element.29), channel_id=1, source_target_pairs={{0,12},{4,8},{8,4},{12,0},{1,13},{5,9},{9,5},{13,1},{2,14},{6,10},... | collective-permute-start | bytes 393224 | tf_op jit(solution)/shard_map/ppermute | solution.py:50
  15.3 0.6 collective-permute-start.8
  15.8 0.2 collective-permute-start.9
  16.6 0.2 convert_reduce_fusion
  16.9 0.0 collective-permute-done
  16.9 0.4 fusion.3
  17.3 0.1 constant_dynamic-slice_fusion.4
  17.4 2.3 %all-to-all-done = bf16[16,8,512]{2,1,0:T(8,128)(2,1)S(1)} async-done(((bf16[16,8,512]{2,1,0:T(8,128)(2,1)}), bf16[16,8,512]{2,1,0:T(8,128)(2,1)S(1)}, u32[]{:S(2)}, u32[]{:S(2)}) %all-to-all-start) | async-done | bytes 131104 | tf_op jit(solution)/shard_map/all_to_all | solution.py:235
  19.7 0.4 convolution_convert_fusion.2
  20.1 0.1 pad_maximum_fusion
  20.2 0.1 collective-permute-start.1
  20.3 1.0 %collective-permute-start.2 = (bf16[64,2560]{1,0:T(8,128)(2,1)S(1)}, bf16[64,2560]{1,0:T(8,128)(2,1)S(1)}, u32[]{:S(2)}, u32[]{:S(2)}) collective-permute-start(bf16[64,2560]{1,0:T(8,128)(2,1)S(1)} %get-tuple-element.44), channel_id=1, source_target_pairs={{0,8},{4,12},{8,0},{12,4},{1,9},{5,13},{9,1},{13,5},{2,10},{6,14},... | collective-permute-start | bytes 983048 | tf_op jit(solution)/shard_map/ppermute | solution.py:50
  21.3 0.0 collective-permute-done.10
  21.3 2.5 %collective-permute-start.3 = (bf16[64,2560]{1,0:T(8,128)(2,1)S(1)}, bf16[64,2560]{1,0:T(8,128)(2,1)S(1)}, u32[]{:S(2)}, u32[]{:S(2)}) collective-permute-start(bf16[64,2560]{1,0:T(8,128)(2,1)S(1)} %get-tuple-element.42), channel_id=1, source_target_pairs={{0,12},{4,8},{8,4},{12,0},{1,13},{5,9},{9,5},{13,1},{2,14},{6,10},... | collective-permute-start | bytes 983048 | tf_op jit(solution)/shard_map/ppermute | solution.py:50
  23.8 0.0 collective-permute-done.8
  23.8 0.0 collective-permute-done.9
  23.8 1.7 %collective-permute-start.11 = (bf16[128,2048]{1,0:T(8,128)(2,1)S(1)}, bf16[128,2048]{1,0:T(8,128)(2,1)S(1)}, u32[]{:S(2)}, u32[]{:S(2)}) collective-permute-start(bf16[128,2048]{1,0:T(8,128)(2,1)S(1)} %pad_maximum_fusion.4.refs_8_), channel_id=1, source_target_pairs={{0,16},{16,0},{1,17},{17,1},{2,18},{18,2},{3,19},{19,3},{4,20},{20... | collective-permute-start | bytes 1572872 | tf_op jit(solution)/shard_map/ppermute | solution.py:233
  25.5 0.0 collective-permute-start.4
  25.5 4.4 %collective-permute-done.1.refs_1_ = bf16[64,2560]{1,0:T(8,128)(2,1)S(1)} collective-permute-done((bf16[64,2560]{1,0:T(8,128)(2,1)S(1)}, bf16[64,2560]{1,0:T(8,128)(2,1)S(1)}, u32[]{:S(2)}, u32[]{:S(2)}) %collective-permute-start.1) | collective-permute-done | bytes 327712 | tf_op jit(solution)/shard_map/ppermute | solution.py:50
  30.0 12.3 %collective-permute-done.2.refs_2_ = bf16[64,2560]{1,0:T(8,128)(2,1)S(1)} collective-permute-done((bf16[64,2560]{1,0:T(8,128)(2,1)S(1)}, bf16[64,2560]{1,0:T(8,128)(2,1)S(1)}, u32[]{:S(2)}, u32[]{:S(2)}) %collective-permute-start.2) | collective-permute-done | bytes 327712 | tf_op jit(solution)/shard_map/ppermute | solution.py:50
  42.3 0.0 collective-permute-start.6
  42.3 6.2 %collective-permute-done.3.refs_3_ = bf16[64,2560]{1,0:T(8,128)(2,1)S(1)} collective-permute-done((bf16[64,2560]{1,0:T(8,128)(2,1)S(1)}, bf16[64,2560]{1,0:T(8,128)(2,1)S(1)}, u32[]{:S(2)}, u32[]{:S(2)}) %collective-permute-start.3) | collective-permute-done | bytes 327712 | tf_op jit(solution)/shard_map/ppermute | solution.py:50
  48.5 0.0 collective-permute-start.7
  48.5 0.6 stack.36.place_ref
  49.1 0.0 collective-permute-done.4.refs_4_
  49.1 0.0 collective-permute-done.11.refs_9_
  49.1 0.0 collective-permute-done.6.refs_6_
  49.1 1.1 %collective-permute-done.7.refs_7_ = bf16[64,2560]{1,0:T(8,128)(2,1)} collective-permute-done((bf16[64,2560]{1,0:T(8,128)(2,1)S(1)}, bf16[64,2560]{1,0:T(8,128)(2,1)}, u32[]{:S(2)}, u32[]{:S(2)}) %collective-permute-start.7) | collective-permute-done | bytes 327712 | tf_op jit(solution)/shard_map/ppermute | solution.py:41
  50.3 5.1 %shard_map.85 = (bf16[256,2048]{1,0:T(8,128)(2,1)}, f32[1,2048]{1,0:T(1,128)}, bf16[2,64,256]{2,1,0:T(8,128)(2,1)}, bf16[2,64,256]{2,1,0:T(8,128)(2,1)}, bf16[2,...) custom-call(s32[6]{0:T(128)} %stack.36.place_ref, bf16[64,2560]{1,0:T(8,128)(2,1)} %copy-done.2, ...), custom_call_target="tpu_custom_call" | custom-call | flops 1073741824 | bytes 6815744 | tf_op jit(solution)/shard_map/pallas_call | solution.py:133
  55.4 1.2 %collective-permute-start.12 = (bf16[2,64,256]{2,1,0:T(8,128)(2,1)}, bf16[2,64,256]{2,1,0:T(8,128)(2,1)S(1)}, u32[]{:S(2)}, u32[]{:S(2)}) collective-permute-start(bf16[2,64,256]{2,1,0:T(8,128)(2,1)} %get-tuple-element.14), channel_id=1, source_target_pairs={{0,4},{4,0},{8,12},{12,8},{1,5},{5,1},{9,13},{13,9},{2,6},{6,2},{1... | collective-permute-start | bytes 196616 | tf_op jit(solution)/shard_map/ppermute | solution.py:268
  56.6 0.7 collective-permute-start.13
  57.3 1.7 %collective-permute-start.14 = (bf16[2,64,256]{2,1,0:T(8,128)(2,1)}, bf16[2,64,256]{2,1,0:T(8,128)(2,1)S(1)}, u32[]{:S(2)}, u32[]{:S(2)}) collective-permute-start(bf16[2,64,256]{2,1,0:T(8,128)(2,1)} %get-tuple-element.16), channel_id=1, source_target_pairs={{0,12},{4,8},{8,4},{12,0},{1,13},{5,9},{9,5},{13,1},{2,14},{6,10},... | collective-permute-start | bytes 196616 | tf_op jit(solution)/shard_map/ppermute | solution.py:268
  58.9 3.8 %all-to-all-start.1 = ((bf16[8,32,2048]{2,1,0:T(8,128)(2,1)}), bf16[8,32,2048]{2,1,0:T(8,128)(2,1)S(1)}, u32[]{:S(2)}, u32[]{:S(2)}) async-start(bf16[8,32,2048]{2,1,0:T(8,128)(2,1)} %bitcast.48), calls=%async_computation.1 | async-start | bytes 2097152 | tf_op jit(solution)/shard_map/all_to_all | solution.py:275
  62.7 0.0 collective-permute-done.12
  62.7 0.0 collective-permute-done.14
  62.8 0.6 collective-permute-start.15
  63.4 0.0 collective-permute-start.18
  63.4 4.4 %collective-permute-done.15 = f32[2,64,256]{2,1,0:T(8,128)S(1)} collective-permute-done((f32[2,64,256]{2,1,0:T(8,128)S(1)}, f32[2,64,256]{2,1,0:T(8,128)S(1)}, u32[]{:S(2)}, u32[]{:S(2)}) %collective-permute-start.15) | collective-permute-done | bytes 131104 | tf_op jit(solution)/shard_map/ppermute | solution.py:36
  67.9 0.1 collective-permute-start.16
  68.0 1.1 %collective-permute-done.16 = bf16[64,256]{1,0:T(8,128)(2,1)S(1)} collective-permute-done((bf16[64,256]{1,0:T(8,128)(2,1)S(1)}, bf16[64,256]{1,0:T(8,128)(2,1)S(1)}, u32[]{:S(2)}, u32[]{:S(2)}) %collective-permute-start.16) | collective-permute-done | bytes 32800 | tf_op jit(solution)/shard_map/ppermute | solution.py:41
  69.1 0.5 convolution_convert_fusion
  69.7 0.2 collective-permute-start.17
  69.9 1.1 %collective-permute-done.17 = bf16[8,8,512]{2,1,0:T(8,128)(2,1)S(1)} collective-permute-done((bf16[8,8,512]{2,1,0:T(8,128)(2,1)S(1)}, bf16[8,8,512]{2,1,0:T(8,128)(2,1)S(1)}, u32[]{:S(2)}, u32[]{:S(2)}) %collective-permute-start.17) | collective-permute-done | bytes 65568 | tf_op jit(solution)/shard_map/ppermute | solution.py:41
  71.0 0.6 dynamic-slice_bitcast_fusion.2
  71.7 2.0 %collective-permute-start.19 = (bf16[24,512]{1,0:T(8,128)(2,1)S(1)}, bf16[24,512]{1,0:T(8,128)(2,1)S(1)}, u32[]{:S(2)}, u32[]{:S(2)}) collective-permute-start(bf16[24,512]{1,0:T(8,128)(2,1)S(1)} %get-tuple-element.36), channel_id=1, source_target_pairs={{0,4},{4,0},{8,12},{12,8},{16,20},{20,16},{24,28},{28,24},{1,5},{5... | collective-permute-start | bytes 73736 | tf_op jit(solution)/shard_map/ppermute | solution.py:306
  73.7 1.5 %collective-permute-start.20 = (bf16[24,512]{1,0:T(8,128)(2,1)S(1)}, bf16[24,512]{1,0:T(8,128)(2,1)S(1)}, u32[]{:S(2)}, u32[]{:S(2)}) collective-permute-start(bf16[24,512]{1,0:T(8,128)(2,1)S(1)} %get-tuple-element.35), channel_id=1, source_target_pairs={{0,8},{4,12},{8,0},{12,4},{16,24},{20,28},{24,16},{28,20},{1,9},{5... | collective-permute-start | bytes 73736 | tf_op jit(solution)/shard_map/ppermute | solution.py:306
  75.1 0.0 collective-permute-start.21
  75.1 2.9 %collective-permute-start.22 = (bf16[24,512]{1,0:T(8,128)(2,1)S(1)}, bf16[24,512]{1,0:T(8,128)(2,1)S(1)}, u32[]{:S(2)}, u32[]{:S(2)}) collective-permute-start(bf16[24,512]{1,0:T(8,128)(2,1)S(1)} %get-tuple-element.33), channel_id=1, source_target_pairs={{0,16},{4,20},{8,24},{12,28},{16,0},{20,4},{24,8},{28,12},{1,17},{... | collective-permute-start | bytes 73736 | tf_op jit(solution)/shard_map/ppermute | solution.py:306
  78.1 1.5 %collective-permute-start.23 = (bf16[24,512]{1,0:T(8,128)(2,1)S(1)}, bf16[24,512]{1,0:T(8,128)(2,1)S(1)}, u32[]{:S(2)}, u32[]{:S(2)}) collective-permute-start(bf16[24,512]{1,0:T(8,128)(2,1)S(1)} %get-tuple-element.32), channel_id=1, source_target_pairs={{0,20},{4,16},{8,28},{12,24},{16,4},{20,0},{24,12},{28,8},{1,21},{... | collective-permute-start | bytes 73736 | tf_op jit(solution)/shard_map/ppermute | solution.py:306
  79.5 10.5 %all-to-all-done.1 = bf16[8,32,2048]{2,1,0:T(8,128)(2,1)S(1)} async-done(((bf16[8,32,2048]{2,1,0:T(8,128)(2,1)}), bf16[8,32,2048]{2,1,0:T(8,128)(2,1)S(1)}, u32[]{:S(2)}, u32[]{:S(2)}) %all-to-all-start.1) | async-done | bytes 1048608 | tf_op jit(solution)/shard_map/all_to_all | solution.py:275
  90.0 0.7 collective-permute-start.24
  90.8 3.8 %collective-permute-start.25 = (bf16[24,512]{1,0:T(8,128)(2,1)S(1)}, bf16[24,512]{1,0:T(8,128)(2,1)S(1)}, u32[]{:S(2)}, u32[]{:S(2)}) collective-permute-start(bf16[24,512]{1,0:T(8,128)(2,1)S(1)} %dynamic-slice_bitcast_fusion.1), channel_id=1, source_target_pairs={{0,28},{4,24},{8,20},{12,16},{16,12},{20,8},{24,4},{28,0},{1,29},{... | collective-permute-start | bytes 73736 | tf_op jit(solution)/shard_map/ppermute | solution.py:306
  94.6 0.6 pad_add_fusion.place_ref
  95.3 1.1 %shard_map.87 = f32[32,8192]{1,0:T(8,128)} custom-call(bf16[2,4,32,2048]{3,2,1,0:T(8,128)(2,1)S(1)} %bitcast.47), custom_call_target="tpu_custom_call" | custom-call | flops 1048576 | bytes 2097152 | tf_op jit(solution)/shard_map/pallas_call | solution.py:171
  96.4 0.0 collective-permute-done.22.refs_4_
  96.4 0.0 collective-permute-done.23.refs_5_
  96.4 0.9 collective-permute-done.25.refs_7_
  97.3 0.6 copy-done.11
  97.9 1.6 %shard_map.86 = (bf16[128,512]{1,0:T(8,128)(2,1)}, f32[64,128]{1,0:T(8,128)}) custom-call(s32[2]{0:T(128)} %pad_add_fusion.place_ref, bf16[24,512]{1,0:T(8,128)(2,1)} %get-tuple-element.37.refs_0_, bf16[24,512]{1,0:T(8,128)(2,1)} %copy-done.5, bf16[24,512]{1,0:T(8,128)(2,1)} %copy-done.6, bf16[24,512]{1,0:T(8,128)(2,1)} %copy-done.7, ...), custom_call_target="tpu_custom_call" | custom-call | tf_op jit(solution)/shard_map/pallas_call | solution.py:205
  (63 shorter events, 0.3 us)
Async XLA Ops:
  0.6 16.2 %copy-start = (bf16[64,8192]{1,0:T(8,128)(2,1)S(1)}, bf16[64,8192]{1,0:T(8,128)(2,1)}, u32[]{:S(2)}) copy-start(bf16[64,8192]{1,0:T(8,128)(2,1)} %param.6) | copy-start | bytes 3145732
  0.6 16.0 %copy-start.13 = (s32[64]{0:T(128)S(1)}, s32[64]{0:T(128)}, u32[]{:S(2)}) copy-start(s32[64]{0:T(128)} %param.11) | copy-start | bytes 772
  0.6 16.2 %copy-start.3 = (f32[8192]{0:T(1024)S(1)}, f32[8192]{0:T(1024)}, u32[]{:S(2)}) copy-start(f32[8192]{0:T(1024)} %param.7) | copy-start | bytes 98308
  2.3 14.6 %collective-permute-start = (f32[64]{0:T(128)S(1)}, f32[64]{0:T(128)S(1)}, u32[]{:S(2)}, u32[]{:S(2)}) collective-permute-start(f32[64]{0:T(128)S(1)} %fusion), channel_id=1, source_target_pairs={{0,1},{1,0},{2,3},{3,2},{4,5},{5,4},{6,7},{7,6},{8,9},{9,8},{10,11... | collective-permute-start | bytes 776 | tf_op jit(solution)/shard_map/ppermute | solution.py:36
  5.3 14.4 %all-to-all-start = ((bf16[16,8,512]{2,1,0:T(8,128)(2,1)}), bf16[16,8,512]{2,1,0:T(8,128)(2,1)S(1)}, u32[]{:S(2)}, u32[]{:S(2)}) async-start(bf16[16,8,512]{2,1,0:T(8,128)(2,1)} %bitcast.50), calls=%async_computation | async-start | bytes 262144 | tf_op jit(solution)/shard_map/all_to_all | solution.py:235
  12.4 8.9 %collective-permute-start.10 = (bf16[32,2048]{1,0:T(8,128)(2,1)S(1)}, bf16[32,2048]{1,0:T(8,128)(2,1)S(1)}, u32[]{:S(2)}, u32[]{:S(2)}) collective-permute-start(bf16[32,2048]{1,0:T(8,128)(2,1)S(1)} %get-tuple-element.29), channel_id=1, source_target_pairs={{0,12},{4,8},{8,4},{12,0},{1,13},{5,9},{9,5},{13,1},{2,14},{6,10},... | collective-permute-start | bytes 393224 | tf_op jit(solution)/shard_map/ppermute | solution.py:50
  15.3 8.5 %collective-permute-start.8 = (bf16[32,2048]{1,0:T(8,128)(2,1)S(1)}, bf16[32,2048]{1,0:T(8,128)(2,1)S(1)}, u32[]{:S(2)}, u32[]{:S(2)}) collective-permute-start(bf16[32,2048]{1,0:T(8,128)(2,1)S(1)} %get-tuple-element.28), channel_id=1, source_target_pairs={{0,4},{4,0},{8,12},{12,8},{1,5},{5,1},{9,13},{13,9},{2,6},{6,2},{1... | collective-permute-start | bytes 393224 | tf_op jit(solution)/shard_map/ppermute | solution.py:50
  15.8 8.0 %collective-permute-start.9 = (bf16[32,2048]{1,0:T(8,128)(2,1)S(1)}, bf16[32,2048]{1,0:T(8,128)(2,1)S(1)}, u32[]{:S(2)}, u32[]{:S(2)}) collective-permute-start(bf16[32,2048]{1,0:T(8,128)(2,1)S(1)} %get-tuple-element.30), channel_id=1, source_target_pairs={{0,8},{4,12},{8,0},{12,4},{1,9},{5,13},{9,1},{13,5},{2,10},{6,14},... | collective-permute-start | bytes 393224 | tf_op jit(solution)/shard_map/ppermute | solution.py:50
  20.2 30.0 %copy-start.2 = (bf16[64,2560]{1,0:T(8,128)(2,1)}, bf16[64,2560]{1,0:T(8,128)(2,1)S(1)}, u32[]{:S(2)}) copy-start(bf16[64,2560]{1,0:T(8,128)(2,1)S(1)} %get-tuple-element.45.refs_0_) | copy-start | bytes 983044
  20.2 9.8 %collective-permute-start.1 = (bf16[64,2560]{1,0:T(8,128)(2,1)S(1)}, bf16[64,2560]{1,0:T(8,128)(2,1)S(1)}, u32[]{:S(2)}, u32[]{:S(2)}) collective-permute-start(bf16[64,2560]{1,0:T(8,128)(2,1)S(1)} %get-tuple-element.43), channel_id=1, source_target_pairs={{0,4},{4,0},{8,12},{12,8},{1,5},{5,1},{9,13},{13,9},{2,6},{6,2},{1... | collective-permute-start | bytes 983048 | tf_op jit(solution)/shard_map/ppermute | solution.py:50
  20.3 22.0 %collective-permute-start.2 = (bf16[64,2560]{1,0:T(8,128)(2,1)S(1)}, bf16[64,2560]{1,0:T(8,128)(2,1)S(1)}, u32[]{:S(2)}, u32[]{:S(2)}) collective-permute-start(bf16[64,2560]{1,0:T(8,128)(2,1)S(1)} %get-tuple-element.44), channel_id=1, source_target_pairs={{0,8},{4,12},{8,0},{12,4},{1,9},{5,13},{9,1},{13,5},{2,10},{6,14},... | collective-permute-start | bytes 983048 | tf_op jit(solution)/shard_map/ppermute | solution.py:50
  21.3 27.1 %collective-permute-start.3 = (bf16[64,2560]{1,0:T(8,128)(2,1)S(1)}, bf16[64,2560]{1,0:T(8,128)(2,1)S(1)}, u32[]{:S(2)}, u32[]{:S(2)}) collective-permute-start(bf16[64,2560]{1,0:T(8,128)(2,1)S(1)} %get-tuple-element.42), channel_id=1, source_target_pairs={{0,12},{4,8},{8,4},{12,0},{1,13},{5,9},{9,5},{13,1},{2,14},{6,10},... | collective-permute-start | bytes 983048 | tf_op jit(solution)/shard_map/ppermute | solution.py:50
  23.8 26.4 %copy-start.1 = (bf16[128,2048]{1,0:T(8,128)(2,1)}, bf16[128,2048]{1,0:T(8,128)(2,1)S(1)}, u32[]{:S(2)}) copy-start(bf16[128,2048]{1,0:T(8,128)(2,1)S(1)} %pad_maximum_fusion.4.refs_8_) | copy-start | bytes 1572868
  23.8 25.2 %collective-permute-start.11 = (bf16[128,2048]{1,0:T(8,128)(2,1)S(1)}, bf16[128,2048]{1,0:T(8,128)(2,1)S(1)}, u32[]{:S(2)}, u32[]{:S(2)}) collective-permute-start(bf16[128,2048]{1,0:T(8,128)(2,1)S(1)} %pad_maximum_fusion.4.refs_8_), channel_id=1, source_target_pairs={{0,16},{16,0},{1,17},{17,1},{2,18},{18,2},{3,19},{19,3},{4,20},{20... | collective-permute-start | bytes 1572872 | tf_op jit(solution)/shard_map/ppermute | solution.py:233
  25.5 23.6 %collective-permute-start.4 = (bf16[64,2560]{1,0:T(8,128)(2,1)S(1)}, bf16[64,2560]{1,0:T(8,128)(2,1)S(1)}, u32[]{:S(2)}, u32[]{:S(2)}) collective-permute-start(bf16[64,2560]{1,0:T(8,128)(2,1)S(1)} %get-tuple-element.45.refs_0_), channel_id=1, source_target_pairs={{0,2},{2,0},{1,3},{3,1},{4,6},{6,4},{5,7},{7,5},{8,10},{10,8},{9,1... | collective-permute-start | bytes 983048 | tf_op jit(solution)/shard_map/ppermute | solution.py:41
  30.0 20.3 %copy-start.15 = (bf16[64,2560]{1,0:T(8,128)(2,1)}, bf16[64,2560]{1,0:T(8,128)(2,1)S(1)}, u32[]{:S(2)}) copy-start(bf16[64,2560]{1,0:T(8,128)(2,1)S(1)} %collective-permute-done.1.refs_1_) | copy-start | bytes 983044
  30.0 19.1 %collective-permute-start.5 = (bf16[64,2560]{1,0:T(8,128)(2,1)S(1)}, bf16[64,2560]{1,0:T(8,128)(2,1)S(1)}, u32[]{:S(2)}, u32[]{:S(2)}) collective-permute-start(bf16[64,2560]{1,0:T(8,128)(2,1)S(1)} %collective-permute-done.1.refs_1_), channel_id=1, source_target_pairs={{0,2},{2,0},{1,3},{3,1},{4,6},{6,4},{5,7},{7,5},{8,10},{10,8},{9,1... | collective-permute-start | bytes 983048 | tf_op jit(solution)/shard_map/ppermute | solution.py:41
  42.3 8.0 %copy-start.16 = (bf16[64,2560]{1,0:T(8,128)(2,1)}, bf16[64,2560]{1,0:T(8,128)(2,1)S(1)}, u32[]{:S(2)}) copy-start(bf16[64,2560]{1,0:T(8,128)(2,1)S(1)} %collective-permute-done.2.refs_2_) | copy-start | bytes 983044
  42.3 6.9 %collective-permute-start.6 = (bf16[64,2560]{1,0:T(8,128)(2,1)S(1)}, bf16[64,2560]{1,0:T(8,128)(2,1)}, u32[]{:S(2)}, u32[]{:S(2)}) collective-permute-start(bf16[64,2560]{1,0:T(8,128)(2,1)S(1)} %collective-permute-done.2.refs_2_), channel_id=1, source_target_pairs={{0,2},{2,0},{1,3},{3,1},{4,6},{6,4},{5,7},{7,5},{8,10},{10,8},{9,1... | collective-permute-start | bytes 983048 | tf_op jit(solution)/shard_map/ppermute | solution.py:41
  48.5 1.8 %copy-start.17 = (bf16[64,2560]{1,0:T(8,128)(2,1)}, bf16[64,2560]{1,0:T(8,128)(2,1)S(1)}, u32[]{:S(2)}) copy-start(bf16[64,2560]{1,0:T(8,128)(2,1)S(1)} %collective-permute-done.3.refs_3_) | copy-start | bytes 983044
  48.5 1.8 %collective-permute-start.7 = (bf16[64,2560]{1,0:T(8,128)(2,1)S(1)}, bf16[64,2560]{1,0:T(8,128)(2,1)}, u32[]{:S(2)}, u32[]{:S(2)}) collective-permute-start(bf16[64,2560]{1,0:T(8,128)(2,1)S(1)} %collective-permute-done.3.refs_3_), channel_id=1, source_target_pairs={{0,2},{2,0},{1,3},{3,1},{4,6},{6,4},{5,7},{7,5},{8,10},{10,8},{9,1... | collective-permute-start | bytes 983048 | tf_op jit(solution)/shard_map/ppermute | solution.py:41
  49.1 1.2 %copy-start.18 = (bf16[64,2560]{1,0:T(8,128)(2,1)}, bf16[64,2560]{1,0:T(8,128)(2,1)S(1)}, u32[]{:S(2)}) copy-start(bf16[64,2560]{1,0:T(8,128)(2,1)S(1)} %collective-permute-done.4.refs_4_) | copy-start | bytes 983044
  49.1 1.2 %copy-start.14 = (bf16[128,2048]{1,0:T(8,128)(2,1)}, bf16[128,2048]{1,0:T(8,128)(2,1)S(1)}, u32[]{:S(2)}) copy-start(bf16[128,2048]{1,0:T(8,128)(2,1)S(1)} %collective-permute-done.11.refs_9_) | copy-start | bytes 1572868
  49.1 1.2 %copy-start.19 = (bf16[64,2560]{1,0:T(8,128)(2,1)}, bf16[64,2560]{1,0:T(8,128)(2,1)S(1)}, u32[]{:S(2)}) copy-start(bf16[64,2560]{1,0:T(8,128)(2,1)S(1)} %collective-permute-done.5.refs_5_) | copy-start | bytes 983044
  55.4 7.3 %collective-permute-start.12 = (bf16[2,64,256]{2,1,0:T(8,128)(2,1)}, bf16[2,64,256]{2,1,0:T(8,128)(2,1)S(1)}, u32[]{:S(2)}, u32[]{:S(2)}) collective-permute-start(bf16[2,64,256]{2,1,0:T(8,128)(2,1)} %get-tuple-element.14), channel_id=1, source_target_pairs={{0,4},{4,0},{8,12},{12,8},{1,5},{5,1},{9,13},{13,9},{2,6},{6,2},{1... | collective-permute-start | bytes 196616 | tf_op jit(solution)/shard_map/ppermute | solution.py:268
  56.6 6.1 %collective-permute-start.13 = (bf16[2,64,256]{2,1,0:T(8,128)(2,1)}, bf16[2,64,256]{2,1,0:T(8,128)(2,1)S(1)}, u32[]{:S(2)}, u32[]{:S(2)}) collective-permute-start(bf16[2,64,256]{2,1,0:T(8,128)(2,1)} %get-tuple-element.15), channel_id=1, source_target_pairs={{0,8},{4,12},{8,0},{12,4},{1,9},{5,13},{9,1},{13,5},{2,10},{6,14},... | collective-permute-start | bytes 196616 | tf_op jit(solution)/shard_map/ppermute | solution.py:268
  57.3 5.5 %collective-permute-start.14 = (bf16[2,64,256]{2,1,0:T(8,128)(2,1)}, bf16[2,64,256]{2,1,0:T(8,128)(2,1)S(1)}, u32[]{:S(2)}, u32[]{:S(2)}) collective-permute-start(bf16[2,64,256]{2,1,0:T(8,128)(2,1)} %get-tuple-element.16), channel_id=1, source_target_pairs={{0,12},{4,8},{8,4},{12,0},{1,13},{5,9},{9,5},{13,1},{2,14},{6,10},... | collective-permute-start | bytes 196616 | tf_op jit(solution)/shard_map/ppermute | solution.py:268
  58.9 3.8 %copy-start.4 = (bf16[2,64,256]{2,1,0:T(8,128)(2,1)S(1)}, bf16[2,64,256]{2,1,0:T(8,128)(2,1)}, u32[]{:S(2)}) copy-start(bf16[2,64,256]{2,1,0:T(8,128)(2,1)} %get-tuple-element.13) | copy-start | bytes 196612
  58.9 4.5 %copy-start.12 = (f32[1,2048]{1,0:T(1,128)S(1)}, f32[1,2048]{1,0:T(1,128)}, u32[]{:S(2)}) copy-start(f32[1,2048]{1,0:T(1,128)} %get-tuple-element.17) | copy-start | bytes 24580
  58.9 31.1 %all-to-all-start.1 = ((bf16[8,32,2048]{2,1,0:T(8,128)(2,1)}), bf16[8,32,2048]{2,1,0:T(8,128)(2,1)S(1)}, u32[]{:S(2)}, u32[]{:S(2)}) async-start(bf16[8,32,2048]{2,1,0:T(8,128)(2,1)} %bitcast.48), calls=%async_computation.1 | async-start | bytes 2097152 | tf_op jit(solution)/shard_map/all_to_all | solution.py:275
  62.8 5.0 %collective-permute-start.15 = (f32[2,64,256]{2,1,0:T(8,128)S(1)}, f32[2,64,256]{2,1,0:T(8,128)S(1)}, u32[]{:S(2)}, u32[]{:S(2)}) collective-permute-start(f32[2,64,256]{2,1,0:T(8,128)S(1)} %convert_add_fusion), channel_id=1, source_target_pairs={{0,1},{1,0},{2,3},{3,2},{4,5},{5,4},{6,7},{7,6},{8,9},{9,8},{10,11... | collective-permute-start | bytes 393224 | tf_op jit(solution)/shard_map/ppermute | solution.py:36
  63.4 4.5 %collective-permute-start.18 = (f32[2048]{0:T(1024)S(1)}, f32[2048]{0:T(1024)S(1)}, u32[]{:S(2)}, u32[]{:S(2)}) collective-permute-start(f32[2048]{0:T(1024)S(1)} %bitcast.53), channel_id=1, source_target_pairs={{0,2},{2,0},{1,3},{3,1},{4,6},{6,4},{5,7},{7,5},{8,10},{10,8},{9,1... | collective-permute-start | bytes 24584 | tf_op jit(solution)/shard_map/ppermute | solution.py:41
  67.9 1.3 %collective-permute-start.16 = (bf16[64,256]{1,0:T(8,128)(2,1)S(1)}, bf16[64,256]{1,0:T(8,128)(2,1)S(1)}, u32[]{:S(2)}, u32[]{:S(2)}) collective-permute-start(bf16[64,256]{1,0:T(8,128)(2,1)S(1)} %get-tuple-element.41), channel_id=1, source_target_pairs={{0,2},{2,0},{1,3},{3,1},{4,6},{6,4},{5,7},{7,5},{8,10},{10,8},{9,1... | collective-permute-start | bytes 98312 | tf_op jit(solution)/shard_map/ppermute | solution.py:41
  69.7 1.3 %collective-permute-start.17 = (bf16[8,8,512]{2,1,0:T(8,128)(2,1)S(1)}, bf16[8,8,512]{2,1,0:T(8,128)(2,1)S(1)}, u32[]{:S(2)}, u32[]{:S(2)}) collective-permute-start(bf16[8,8,512]{2,1,0:T(8,128)(2,1)S(1)} %dynamic-slice_bitcast_fusion), channel_id=1, source_target_pairs={{0,2},{2,0},{1,3},{3,1},{4,6},{6,4},{5,7},{7,5},{8,10},{10,8},{9,1... | collective-permute-start | bytes 196616 | tf_op jit(solution)/shard_map/ppermute | solution.py:41
  71.7 18.4 %collective-permute-start.19 = (bf16[24,512]{1,0:T(8,128)(2,1)S(1)}, bf16[24,512]{1,0:T(8,128)(2,1)S(1)}, u32[]{:S(2)}, u32[]{:S(2)}) collective-permute-start(bf16[24,512]{1,0:T(8,128)(2,1)S(1)} %get-tuple-element.36), channel_id=1, source_target_pairs={{0,4},{4,0},{8,12},{12,8},{16,20},{20,16},{24,28},{28,24},{1,5},{5... | collective-permute-start | bytes 73736 | tf_op jit(solution)/shard_map/ppermute | solution.py:306
  73.7 17.1 %collective-permute-start.20 = (bf16[24,512]{1,0:T(8,128)(2,1)S(1)}, bf16[24,512]{1,0:T(8,128)(2,1)S(1)}, u32[]{:S(2)}, u32[]{:S(2)}) collective-permute-start(bf16[24,512]{1,0:T(8,128)(2,1)S(1)} %get-tuple-element.35), channel_id=1, source_target_pairs={{0,8},{4,12},{8,0},{12,4},{16,24},{20,28},{24,16},{28,20},{1,9},{5... | collective-permute-start | bytes 73736 | tf_op jit(solution)/shard_map/ppermute | solution.py:306
  75.1 21.2 %collective-permute-start.21 = (bf16[24,512]{1,0:T(8,128)(2,1)S(1)}, bf16[24,512]{1,0:T(8,128)(2,1)S(1)}, u32[]{:S(2)}, u32[]{:S(2)}) collective-permute-start(bf16[24,512]{1,0:T(8,128)(2,1)S(1)} %get-tuple-element.34), channel_id=1, source_target_pairs={{0,12},{4,8},{8,4},{12,0},{16,28},{20,24},{24,20},{28,16},{1,13},{... | collective-permute-start | bytes 73736 | tf_op jit(solution)/shard_map/ppermute | solution.py:306
  75.1 21.2 %collective-permute-start.22 = (bf16[24,512]{1,0:T(8,128)(2,1)S(1)}, bf16[24,512]{1,0:T(8,128)(2,1)S(1)}, u32[]{:S(2)}, u32[]{:S(2)}) collective-permute-start(bf16[24,512]{1,0:T(8,128)(2,1)S(1)} %get-tuple-element.33), channel_id=1, source_target_pairs={{0,16},{4,20},{8,24},{12,28},{16,0},{20,4},{24,8},{28,12},{1,17},{... | collective-permute-start | bytes 73736 | tf_op jit(solution)/shard_map/ppermute | solution.py:306
  78.1 18.3 %collective-permute-start.23 = (bf16[24,512]{1,0:T(8,128)(2,1)S(1)}, bf16[24,512]{1,0:T(8,128)(2,1)S(1)}, u32[]{:S(2)}, u32[]{:S(2)}) collective-permute-start(bf16[24,512]{1,0:T(8,128)(2,1)S(1)} %get-tuple-element.32), channel_id=1, source_target_pairs={{0,20},{4,16},{8,28},{12,24},{16,4},{20,0},{24,12},{28,8},{1,21},{... | collective-permute-start | bytes 73736 | tf_op jit(solution)/shard_map/ppermute | solution.py:306
  90.0 6.3 %copy-start.5 = (bf16[24,512]{1,0:T(8,128)(2,1)}, bf16[24,512]{1,0:T(8,128)(2,1)S(1)}, u32[]{:S(2)}) copy-start(bf16[24,512]{1,0:T(8,128)(2,1)S(1)} %collective-permute-done.19.refs_1_) | copy-start | bytes 73732
  90.0 6.4 %collective-permute-start.24 = (bf16[24,512]{1,0:T(8,128)(2,1)S(1)}, bf16[24,512]{1,0:T(8,128)(2,1)S(1)}, u32[]{:S(2)}, u32[]{:S(2)}) collective-permute-start(bf16[24,512]{1,0:T(8,128)(2,1)S(1)} %get-tuple-element.31), channel_id=1, source_target_pairs={{0,24},{4,28},{8,16},{12,20},{16,8},{20,12},{24,0},{28,4},{1,25},{... | collective-permute-start | bytes 73736 | tf_op jit(solution)/shard_map/ppermute | solution.py:306
  90.8 5.6 %copy-start.6 = (bf16[24,512]{1,0:T(8,128)(2,1)}, bf16[24,512]{1,0:T(8,128)(2,1)S(1)}, u32[]{:S(2)}) copy-start(bf16[24,512]{1,0:T(8,128)(2,1)S(1)} %collective-permute-done.20.refs_2_) | copy-start | bytes 73732
  90.8 6.5 %collective-permute-start.25 = (bf16[24,512]{1,0:T(8,128)(2,1)S(1)}, bf16[24,512]{1,0:T(8,128)(2,1)S(1)}, u32[]{:S(2)}, u32[]{:S(2)}) collective-permute-start(bf16[24,512]{1,0:T(8,128)(2,1)S(1)} %dynamic-slice_bitcast_fusion.1), channel_id=1, source_target_pairs={{0,28},{4,24},{8,20},{12,16},{16,12},{20,8},{24,4},{28,0},{1,29},{... | collective-permute-start | bytes 73736 | tf_op jit(solution)/shard_map/ppermute | solution.py:306
  96.4 1.0 copy-start.7
  96.4 0.9 copy-start.8
  96.4 0.9 copy-start.9
  96.4 0.9 copy-start.10
  97.3 0.6 copy-start.11

commit v5 on v4

--- a/solution.py
+++ b/solution.py
@@ -14,7 +14,7 @@
 DP = ("hi", "lo", "core")
 SWAP = [(0, 1), (1, 0)]
 FEW = 4
-EARLY = 7
+PIN = 1
 LANES = 128
 CHUNK = 512
 
@@ -65,7 +65,7 @@
     return accepted, one_hot(position, shards * capacity)
 
 
-def products_kernel(pieces, owned, low, core_keys, part, chunk, place_ref, *refs):
+def products_kernel(pieces, owned, low, core_keys, part, chunk, *refs):
     row_refs, weight_refs = refs[: 2 * pieces], refs[2 * pieces : 2 * pieces + 2]
     grad_ref, gain_ref = refs[2 * pieces + 2 : 2 * pieces + 4]
     key_refs = refs[2 * pieces + 4 : 3 * pieces + 4]
@@ -87,7 +87,8 @@
             copies.append(pltpu.make_async_copy(source, to.at[at], sem.at[j]))
     block = half_keys // pieces
     for j in range(2 * pieces):
-        first = place_ref[2 + j % pieces] * owned + (place_ref[0] ^ (j // pieces)) * half_keys
+        place = lax.axis_index("lo") ^ j % pieces if pieces > 1 else 0
+        first = place * owned + (lax.axis_index("hi") ^ (j // pieces)) * half_keys
         if owned % 16 == 0:
             first = pl.multiple_of(first, 16)
         copies.append(
@@ -128,7 +129,6 @@
     pieces, low = len(rows_here), lax.axis_size("lo")
     piece_rows, columns = rows_here[0].shape
     half_keys = core_keys // 2
-    scalars = jnp.stack([lax.axis_index("hi"), lax.axis_index("core")] + places).astype(jnp.int32)
     total = 2 * pieces * piece_rows
     return pl.pallas_call(
         functools.partial(
@@ -139,8 +139,7 @@
             jax.ShapeDtypeStruct((1, part), jnp.float32),
         ]
         + [jax.ShapeDtypeStruct((2, piece_rows, core_keys), jnp.bfloat16)] * pieces,
-        in_specs=[pl.BlockSpec(memory_space=pltpu.SMEM)]
-        + [pl.BlockSpec(memory_space=pl.ANY)] * (2 * pieces + 2),
+        in_specs=[pl.BlockSpec(memory_space=pl.ANY)] * (2 * pieces + 2),
         scratch_shapes=[
             pltpu.VMEM((total, part), jnp.bfloat16),
             pltpu.VMEM((total, core_keys), jnp.bfloat16),
@@ -150,13 +149,13 @@
             pltpu.SemaphoreType.DMA((2 * pieces,)),
             pltpu.SemaphoreType.DMA((2 * pieces,)),
         ],
-        compiler_params=pltpu.CompilerParams(vmem_limit_bytes=60 * 1024 * 1024),
+        compiler_params=pltpu.CompilerParams(vmem_limit_bytes=16 * 1024 * 1024),
         cost_estimate=pl.CostEstimate(
             flops=4 * total * core_keys * part,
             bytes_accessed=2 * total * columns + 8 * core_keys * part,
             transcendentals=0,
         ),
-    )(scalars, *rows_here, *rows_there, *weights)
+    )(*rows_here, *rows_there, *weights)
 
 
 def sum_kernel(factor, terms_ref, grad_ref):
@@ -173,34 +172,36 @@
         out_shape=jax.ShapeDtypeStruct((owned, low * part), jnp.float32),
         in_specs=[pl.BlockSpec(memory_space=pltpu.VMEM)],
         out_specs=pl.BlockSpec(memory_space=pltpu.VMEM),
-        compiler_params=pltpu.CompilerParams(vmem_limit_bytes=32 * 1024 * 1024),
+        compiler_params=pltpu.CompilerParams(vmem_limit_bytes=8 * 1024 * 1024),
         cost_estimate=pl.CostEstimate(
             flops=2 * terms.size, bytes_accessed=4 * terms.size, transcendentals=0
         ),
     )(terms)
 
 
-def gather_kernel(key_rows, factor, place_ref, *refs):
+def gather_kernel(key_rows, factor, *refs):
     pieces, norm_ref, key_ref, gain_ref = refs[:-3], refs[-3], refs[-2], refs[-1]
     low, columns = len(pieces) // 2, key_ref.shape[1]
-    half_rows, wide = (pieces[0].shape[0] - key_rows) // 2, columns // LANES
-    for step, piece in enumerate(pieces):
-        at = pl.multiple_of((place_ref[0] ^ step) * key_rows, key_rows)
-        key_ref[pl.ds(at, key_rows)] = piece[:key_rows]
+    half_rows, wide = (pieces[0].shape[0] - 2 * key_rows) // 2, columns // LANES
+    hi, lo, core = (lax.axis_index(name) for name in DP)
+    mine = pl.ds(pl.multiple_of(core * key_rows, key_rows), key_rows)
     for step in range(low):
+        place = lo ^ step
         total = jnp.zeros((half_rows, columns), jnp.float32)
-        for piece in pieces[step::low]:
-            terms = piece[key_rows:].astype(jnp.float32)
+        for k in range(2):
+            piece = pieces[k * low + step]
+            at = ((hi ^ core ^ k) * low + place) * key_rows
+            key_ref[pl.ds(pl.multiple_of(at, key_rows), key_rows)] = piece[mine]
+            terms = piece[2 * key_rows :].astype(jnp.float32)
             total = total + terms[:half_rows] + terms[half_rows:]
         for i in range(half_rows):
             for j in range(wide):
-                at = pl.ds(((place_ref[1] ^ step) * half_rows + i) * wide + j, 1)
+                at = pl.ds((place * half_rows + i) * wide + j, 1)
                 sums = total[i : i + 1, j * LANES : (j + 1) * LANES]
                 gain_ref[at] = sums * factor / norm_ref[at]
 
 
-def gather_pieces(pieces, norm_gain, chip, key_rows, factor):
-    places = jnp.stack([chip, lax.axis_index("lo")]).astype(jnp.int32)
+def gather_pieces(pieces, norm_gain, key_rows, factor):
     key_width, width = pieces[0].shape[1], norm_gain.shape[0]
     return pl.pallas_call(
         functools.partial(gather_kernel, key_rows, factor),
@@ -208,10 +209,10 @@
             jax.ShapeDtypeStruct((len(pieces) * key_rows, key_width), jnp.bfloat16),
             jax.ShapeDtypeStruct((width // LANES, LANES), jnp.float32),
         ],
-        in_specs=[pl.BlockSpec(memory_space=pltpu.SMEM)]
-        + [pl.BlockSpec(memory_space=pltpu.VMEM)] * (len(pieces) + 1),
+        in_specs=[pl.BlockSpec(memory_space=pltpu.VMEM)] * (len(pieces) + 1),
         out_specs=[pl.BlockSpec(memory_space=pltpu.VMEM)] * 2,
-    )(places, *pieces, norm_gain.reshape(width // LANES, LANES))
+        compiler_params=pltpu.CompilerParams(vmem_limit_bytes=4 * 1024 * 1024),
+    )(*pieces, norm_gain.reshape(width // LANES, LANES))
 
 
 def on_device(hidden_rows, norm_gain, key_weight, cotangent, accepted_counts, destination):
@@ -287,44 +288,53 @@
     ).astype(jnp.bfloat16)
     key_slots = select(key_slots, by_core)
 
-    key_slots = key_slots.reshape(halves * low, cores, capacity, key_width)
-    mine = lax.dynamic_index_in_dim(key_slots, core, 1, keepdims=False)
-    other = swap_core(lax.dynamic_index_in_dim(key_slots, 1 - core, 1, keepdims=False))
-    mine, other = jnp.where(core == 0, mine, other), jnp.where(core == 0, other, mine)
+    whole_slots = key_slots.reshape(replicas, capacity, key_width)
+    key_slots = key_slots.reshape(halves, low, cores, capacity, key_width)
+    stay = lax.dynamic_index_in_dim(key_slots, hi ^ core, 0, keepdims=False)
+    come = swap_core(lax.dynamic_index_in_dim(key_slots, hi ^ 1 ^ core, 0, keepdims=False))
+    stay, come = jnp.where(core == 0, stay, come), jnp.where(core == 0, come, stay)
     gain_part = gain_part + swap_core(gain_part)
     upper = lax.reduce_precision(gain_part, 8, 7)
     terms = jnp.concatenate([upper, gain_part - upper]).astype(jnp.bfloat16)
     extra = -(-2 * part // (8 * key_width)) * 8
     terms = jnp.pad(terms, (0, extra * key_width - 2 * part)).reshape(1, extra, key_width)
+    key_rows = cores * capacity
     routed = jnp.concatenate(
-        [mine, other, jnp.broadcast_to(terms, (halves * low, extra, key_width))], axis=1
-    )
-    late, grad_terms = lax.optimization_barrier((routed, grad_terms))
-    grad_weight = sum_terms(grad_terms, factor)
-    if low <= FEW:
-        pieces = [
-            lax.ppermute(
-                lax.dynamic_index_in_dim(
-                    routed if step < EARLY else late, (hi * low + lo) ^ step, 0, keepdims=False
-                ),
-                ("hi", "lo"),
-                [(j, j ^ step) for j in range(halves * low)],
-            )
-            for step in range(1, halves * low)
-        ]
-        own = lax.dynamic_index_in_dim(routed, hi * low + lo, 0, keepdims=False)
-        key_out, grad_gain = gather_pieces(
-            [own] + pieces, norm_gain, hi * low + lo, cores * capacity, factor
-        )
+        [
+            jnp.stack([stay, come], axis=2).reshape(low, cores * key_rows, key_width),
+            jnp.broadcast_to(terms, (low, extra, key_width)),
+        ],
+        axis=1,
+    )
+    if low == FEW:
+        pieces = [lax.dynamic_index_in_dim(routed, lo ^ s, 0, keepdims=False) for s in range(low)]
+        own = pieces[0]
+        pieces[PIN], grad_terms = lax.optimization_barrier((pieces[PIN], grad_terms))
+        for step in range(low):
+            pairs = [
+                ((h * low + j) * cores + c, ((h ^ c) * low + (j ^ step)) * cores + c)
+                for h in range(halves)
+                for j in range(low)
+                for c in range(cores)
+                if step or c
+            ]
+            pieces[step] = lax.ppermute(pieces[step], DP, pairs)
+        pieces[0] = jnp.where(core == 0, own, pieces[0])
+        pieces += [swap_core(piece) for piece in pieces]
+        key_out, grad_gain = gather_pieces(pieces, norm_gain, key_rows, factor)
         grad_gain = grad_gain.reshape(width)
     else:
-        routed = lax.all_to_all(routed, ("hi", "lo"), split_axis=0, concat_axis=0, tiled=True)
-        key_out = routed[:, : cores * capacity].reshape(replicas * capacity, key_width)
-        gain_sums = routed[:, cores * capacity :].reshape(halves, low, extra * key_width)
-        gain_sums = gain_sums[:, :, : 2 * part].astype(jnp.float32)
-        gain_sums = jnp.sum(gain_sums.reshape(halves, low, 2, part), axis=(0, 2))
+        routed = lax.all_to_all(
+            jnp.concatenate(
+                [whole_slots, jnp.broadcast_to(terms, (replicas, extra, key_width))], axis=1
+            ),
+            DP, split_axis=0, concat_axis=0, tiled=True)
+        key_out = routed[:, :capacity].reshape(replicas * capacity, key_width)
+        gain_sums = routed[:, capacity:].reshape(replicas, extra * key_width)[:, : 2 * part]
+        gain_sums = gain_sums.astype(jnp.float32).reshape(halves, low, cores, 2, part)
+        gain_sums = jnp.sum(gain_sums[:, :, 0], axis=(0, 2))
         grad_gain = gain_sums.reshape(width) * factor / norm_gain
-    return (key_out[None], grad_weight, grad_gain)
+    return (key_out[None], sum_terms(grad_terms, factor), grad_gain)
 
 
 def solution(mesh):

time: 100 us -> 95.8 us (0.958)
  waiting for transfers between devices: 44.4 us -> 51.6 us
  starting transfers between devices: 38.4 us -> 31.7 us
  Pallas kernels: 7.8 us -> 5.86 us
  local copies, waits for them, and re-layouts: 3.2 us -> 1.28 us
    ppermute x7 -> x4, starting transfers between devices: 12.4 us -> 5.2 us  [on_device(): pieces[step] = lax.ppermute(pieces[step], DP, pairs)]
    all_to_all x1, waiting for transfers between devices: 10.5 us -> 15.6 us  [on_device(): lax.all_to_all(grad_part.reshape(halves * low, owned, part), ('hi', 'lo')...]
    ppermute x7 -> x4, waiting for transfers between devices: 0.89 us -> 2.33 us  [on_device(): pieces[step] = lax.ppermute(pieces[step], DP, pairs)]
    pallas_call x1, Pallas kernels: 5.1 us -> 4.05 us  [products(): pl.pallas_call(functools.partial(products_kernel, pieces, owned, low, cor...]
    ppermute x7 -> x11, waiting for transfers between devices: 3.32 us -> 3.93 us  [swap_core(): return lax.ppermute(value, 'core', SWAP)]
  transfers between devices with their start and end apart: 28 -> 29, of which waited for: 10 -> 11; matrix products, arithmetic and copies ran while one was open for 5% -> 3% of each run, Pallas kernels for 1% -> 1%
where the time goes in v5:
time: 95.8 us; the launch traced here: 95.4 us
  waiting for transfers between devices  51.6 us (54%)
  starting transfers between devices  31.7 us (33%)
  Pallas kernels  5.86 us (6%)
  other arithmetic  2.45 us (3%)
  between operations  1.63 us (2%)
  local copies, waits for them, and re-layouts  1.28 us (1%)
    ppermute x6, waiting for transfers between devices, swap_lo(): pieces.append(lax.ppermute(block(me ^ step), 'lo', pairs))  23 us
    all_to_all x1, waiting for transfers between devices, on_device(): lax.all_to_all(grad_part.reshape(halves * low, owned, part), ('hi', 'lo')...  15.6 us
    ppermute x6, starting transfers between devices, swap_lo(): pieces.append(lax.ppermute(block(me ^ step), 'lo', pairs))  7.11 us
    all_to_all x1, starting transfers between devices, on_device(): lax.all_to_all(cotangent[0], DP, split_axis=0, concat_axis=0, tiled=True)  5.94 us
    ppermute x4, starting transfers between devices, on_device(): pieces[step] = lax.ppermute(pieces[step], DP, pairs)  5.2 us
    ppermute x2, waiting for transfers between devices, reduce_tensor(): return value + lax.ppermute(value, 'tensor', SWAP)  4.43 us
    pallas_call x1, Pallas kernels, products(): pl.pallas_call(functools.partial(products_kernel, pieces, owned, low, cor...  4.05 us
    ppermute x11, waiting for transfers between devices, swap_core(): return lax.ppermute(value, 'core', SWAP)  3.93 us
  transfers between devices with their start and end apart: 29, of which 11 were waited for; matrix products, arithmetic and copies ran while one was open for 3% of the time, Pallas kernels for 1%

profile of v5, /device:TPU:0, one launch (start us, length us, event | category | flops | bytes accessed | tf_op | source)
XLA Modules:
  0.0 95.4 jit_solution(4676164328530506432)
XLA Ops:
  0.7 1.6 %fusion = f32[64]{0:T(128)S(1)} fusion(bf16[64,8192]{1,0:T(8,128)(2,1)} %param.6), kind=kLoop, calls=%fused_computation.2 | loop fusion | flops 1572800 | bytes 1048832 | tf_op jit(solution)/shard_map/reduce_sum | solution.py:250
  2.3 3.0 %collective-permute-start = (f32[64]{0:T(128)S(1)}, f32[64]{0:T(128)S(1)}, u32[]{:S(2)}, u32[]{:S(2)}) collective-permute-start(f32[64]{0:T(128)S(1)} %fusion), channel_id=1, source_target_pairs={{0,1},{1,0},{2,3},{3,2},{4,5},{5,4},{6,7},{7,6},{8,9},{9,8},{10,11... | collective-permute-start | bytes 776 | tf_op jit(solution)/shard_map/ppermute | solution.py:36
  5.3 5.9 %all-to-all-start = ((bf16[16,8,512]{2,1,0:T(8,128)(2,1)}), bf16[16,8,512]{2,1,0:T(8,128)(2,1)S(1)}, u32[]{:S(2)}, u32[]{:S(2)}) async-start(bf16[16,8,512]{2,1,0:T(8,128)(2,1)} %bitcast.48), calls=%async_computation | async-start | bytes 262144 | tf_op jit(solution)/shard_map/all_to_all | solution.py:236
  11.3 1.1 %constant_dynamic-slice_fusion.3 = (bf16[32,2048]{1,0:T(8,128)(2,1)S(1)}, bf16[32,2048]{1,0:T(8,128)(2,1)S(1)}, bf16[32,2048]{1,0:T(8,128)(2,1)S(1)}, bf16[32,2048]{1,0:T(8,128)(2,1)S(1)}) fusion(bf16[32,8192]{1,0:T(8,128)(2,1)} %param.8, s32[]{:T(128)S(6)} %select_n.103, s32[]{:T(128)S(6)} %select_n.108, s32[]{:T(128)S(6)} %select_n.110, s32[]{:T(128)S(6)} %select_n.109), kind=kLoop, calls=%fused_computation.62 | loop fusion | bytes 1048592 | tf_op jit(solution)/shard_map/dynamic_slice | solution.py:231
  12.4 2.9 %collective-permute-start.10 = (bf16[32,2048]{1,0:T(8,128)(2,1)S(1)}, bf16[32,2048]{1,0:T(8,128)(2,1)S(1)}, u32[]{:S(2)}, u32[]{:S(2)}) collective-permute-start(bf16[32,2048]{1,0:T(8,128)(2,1)S(1)} %get-tuple-element.29), channel_id=1, source_target_pairs={{0,12},{4,8},{8,4},{12,0},{1,13},{5,9},{9,5},{13,1},{2,14},{6,10},... | collective-permute-start | bytes 393224 | tf_op jit(solution)/shard_map/ppermute | solution.py:50
  15.3 0.6 collective-permute-start.8
  15.8 0.2 collective-permute-start.9
  16.7 0.2 convert_reduce_fusion
  16.9 0.0 collective-permute-done
  16.9 0.4 fusion.3
  17.3 0.1 constant_dynamic-slice_fusion.4
  17.4 2.3 %all-to-all-done = bf16[16,8,512]{2,1,0:T(8,128)(2,1)S(1)} async-done(((bf16[16,8,512]{2,1,0:T(8,128)(2,1)}), bf16[16,8,512]{2,1,0:T(8,128)(2,1)S(1)}, u32[]{:S(2)}, u32[]{:S(2)}) %all-to-all-start) | async-done | bytes 131104 | tf_op jit(solution)/shard_map/all_to_all | solution.py:236
  19.7 0.4 convolution_convert_fusion.2
  20.1 0.1 pad_maximum_fusion
  20.2 0.1 collective-permute-start.1
  20.3 1.0 %collective-permute-start.2 = (bf16[64,2560]{1,0:T(8,128)(2,1)S(1)}, bf16[64,2560]{1,0:T(8,128)(2,1)S(1)}, u32[]{:S(2)}, u32[]{:S(2)}) collective-permute-start(bf16[64,2560]{1,0:T(8,128)(2,1)S(1)} %get-tuple-element.41), channel_id=1, source_target_pairs={{0,8},{4,12},{8,0},{12,4},{1,9},{5,13},{9,1},{13,5},{2,10},{6,14},... | collective-permute-start | bytes 983048 | tf_op jit(solution)/shard_map/ppermute | solution.py:50
  21.3 0.0 collective-permute-done.10
  21.3 2.5 %collective-permute-start.3 = (bf16[64,2560]{1,0:T(8,128)(2,1)S(1)}, bf16[64,2560]{1,0:T(8,128)(2,1)S(1)}, u32[]{:S(2)}, u32[]{:S(2)}) collective-permute-start(bf16[64,2560]{1,0:T(8,128)(2,1)S(1)} %get-tuple-element.39), channel_id=1, source_target_pairs={{0,12},{4,8},{8,4},{12,0},{1,13},{5,9},{9,5},{13,1},{2,14},{6,10},... | collective-permute-start | bytes 983048 | tf_op jit(solution)/shard_map/ppermute | solution.py:50
  23.8 0.0 collective-permute-done.8
  23.8 0.0 collective-permute-done.9
  23.8 1.7 %collective-permute-start.11 = (bf16[128,2048]{1,0:T(8,128)(2,1)S(1)}, bf16[128,2048]{1,0:T(8,128)(2,1)S(1)}, u32[]{:S(2)}, u32[]{:S(2)}) collective-permute-start(bf16[128,2048]{1,0:T(8,128)(2,1)S(1)} %pad_maximum_fusion.4.refs_8_), channel_id=1, source_target_pairs={{0,16},{16,0},{1,17},{17,1},{2,18},{18,2},{3,19},{19,3},{4,20},{20... | collective-permute-start | bytes 1572872 | tf_op jit(solution)/shard_map/ppermute | solution.py:234
  25.5 0.0 collective-permute-start.4
  25.5 4.5 %collective-permute-done.1.refs_1_ = bf16[64,2560]{1,0:T(8,128)(2,1)S(1)} collective-permute-done((bf16[64,2560]{1,0:T(8,128)(2,1)S(1)}, bf16[64,2560]{1,0:T(8,128)(2,1)S(1)}, u32[]{:S(2)}, u32[]{:S(2)}) %collective-permute-start.1) | collective-permute-done | bytes 327712 | tf_op jit(solution)/shard_map/ppermute | solution.py:50
  30.0 0.0 collective-permute-start.5
  30.0 12.3 %collective-permute-done.2.refs_2_ = bf16[64,2560]{1,0:T(8,128)(2,1)S(1)} collective-permute-done((bf16[64,2560]{1,0:T(8,128)(2,1)S(1)}, bf16[64,2560]{1,0:T(8,128)(2,1)S(1)}, u32[]{:S(2)}, u32[]{:S(2)}) %collective-permute-start.2) | collective-permute-done | bytes 327712 | tf_op jit(solution)/shard_map/ppermute | solution.py:50
  42.2 0.0 collective-permute-start.6
  42.2 6.2 %collective-permute-done.3.refs_3_ = bf16[64,2560]{1,0:T(8,128)(2,1)S(1)} collective-permute-done((bf16[64,2560]{1,0:T(8,128)(2,1)S(1)}, bf16[64,2560]{1,0:T(8,128)(2,1)S(1)}, u32[]{:S(2)}, u32[]{:S(2)}) %collective-permute-start.3) | collective-permute-done | bytes 327712 | tf_op jit(solution)/shard_map/ppermute | solution.py:50
  48.5 0.0 collective-permute-start.7
  48.5 0.0 collective-permute-done.4.refs_4_
  48.5 0.0 collective-permute-done.11.refs_9_
  48.5 0.0 collective-permute-done.5.refs_5_
  48.5 1.6 %collective-permute-done.7.refs_7_ = bf16[64,2560]{1,0:T(8,128)(2,1)S(1)} collective-permute-done((bf16[64,2560]{1,0:T(8,128)(2,1)S(1)}, bf16[64,2560]{1,0:T(8,128)(2,1)S(1)}, u32[]{:S(2)}, u32[]{:S(2)}) %collective-permute-start.7) | collective-permute-done | bytes 327712 | tf_op jit(solution)/shard_map/ppermute | solution.py:41
  50.1 4.0 %shard_map.85 = (bf16[256,2048]{1,0:T(8,128)(2,1)}, f32[1,2048]{1,0:T(1,128)S(1)}, bf16[2,64,256]{2,1,0:T(8,128)(2,1)S(1)}, bf16[2,64,256]{2,1,0:T(8,128)(2,1)S(...) custom-call(bf16[64,2560]{1,0:T(8,128)(2,1)S(1)} %get-tuple-element.42.refs_0_, ...), custom_call_target="tpu_custom_call" | custom-call | flops 1073741824 | bytes 6815744 | tf_op jit(solution)/shard_map/pallas_call | solution.py:133
  54.1 1.2 %collective-permute-start.12 = (bf16[2,64,256]{2,1,0:T(8,128)(2,1)S(1)}, bf16[2,64,256]{2,1,0:T(8,128)(2,1)S(1)}, u32[]{:S(2)}, u32[]{:S(2)}) collective-permute-start(bf16[2,64,256]{2,1,0:T(8,128)(2,1)S(1)} %get-tuple-element.14), channel_id=1, source_target_pairs={{0,4},{4,0},{8,12},{12,8},{1,5},{5,1},{9,13},{13,9},{2,6},{6,2},{1... | collective-permute-start | bytes 196616 | tf_op jit(solution)/shard_map/ppermute | solution.py:269
  55.3 2.4 %collective-permute-start.14 = (bf16[2,64,256]{2,1,0:T(8,128)(2,1)S(1)}, bf16[2,64,256]{2,1,0:T(8,128)(2,1)S(1)}, u32[]{:S(2)}, u32[]{:S(2)}) collective-permute-start(bf16[2,64,256]{2,1,0:T(8,128)(2,1)S(1)} %get-tuple-element.16), channel_id=1, source_target_pairs={{0,12},{4,8},{8,4},{12,0},{1,13},{5,9},{9,5},{13,1},{2,14},{6,10},... | collective-permute-start | bytes 196616 | tf_op jit(solution)/shard_map/ppermute | solution.py:269
  57.7 3.7 %all-to-all-start.1 = ((bf16[8,32,2048]{2,1,0:T(8,128)(2,1)}), bf16[8,32,2048]{2,1,0:T(8,128)(2,1)S(1)}, u32[]{:S(2)}, u32[]{:S(2)}) async-start(bf16[8,32,2048]{2,1,0:T(8,128)(2,1)} %bitcast.15), calls=%async_computation.1 | async-start | bytes 2097152 | tf_op jit(solution)/shard_map/all_to_all | solution.py:276
  61.4 0.0 collective-permute-done.13
  61.4 0.0 collective-permute-done.14
  61.4 0.6 collective-permute-start.15
  62.0 0.0 collective-permute-start.18
  62.0 4.4 %collective-permute-done.15 = f32[2,64,256]{2,1,0:T(8,128)S(1)} collective-permute-done((f32[2,64,256]{2,1,0:T(8,128)S(1)}, f32[2,64,256]{2,1,0:T(8,128)S(1)}, u32[]{:S(2)}, u32[]{:S(2)}) %collective-permute-start.15) | collective-permute-done | bytes 131104 | tf_op jit(solution)/shard_map/ppermute | solution.py:36
  66.5 0.1 collective-permute-start.16
  66.6 0.0 collective-permute-done.18
  66.6 1.1 %collective-permute-done.16 = bf16[64,256]{1,0:T(8,128)(2,1)S(1)} collective-permute-done((bf16[64,256]{1,0:T(8,128)(2,1)S(1)}, bf16[64,256]{1,0:T(8,128)(2,1)S(1)}, u32[]{:S(2)}, u32[]{:S(2)}) %collective-permute-start.16) | collective-permute-done | bytes 32800 | tf_op jit(solution)/shard_map/ppermute | solution.py:41
  67.8 0.5 convolution_convert_fusion
  68.3 0.2 collective-permute-start.17
  68.5 1.1 %collective-permute-done.17 = bf16[4,2,8,512]{3,2,1,0:T(8,128)(2,1)S(1)} collective-permute-done((bf16[4,2,8,512]{3,2,1,0:T(8,128)(2,1)S(1)}, bf16[4,2,8,512]{3,2,1,0:T(8,128)(2,1)S(1)}, u32[]{:S(2)}, u32[]{:S(2)}) %collective-permute-start.17) | collective-permute-done | bytes 65568 | tf_op jit(solution)/shard_map/ppermute | solution.py:41
  69.7 0.7 collective-permute-start.19
  70.3 2.1 %collective-permute-start.21 = (bf16[40,512]{1,0:T(8,128)(2,1)S(1)}, bf16[40,512]{1,0:T(8,128)(2,1)S(1)}, u32[]{:S(2)}, u32[]{:S(2)}) collective-permute-start(bf16[40,512]{1,0:T(8,128)(2,1)S(1)} %get-tuple-element.36), channel_id=1, source_target_pairs={{0,8},{2,26},{4,12},{6,30},{8,0},{10,18},{12,4},{14,22},{16,24},{1... | collective-permute-start | bytes 122888 | tf_op jit(solution)/shard_map/ppermute | solution.py:321
  72.4 1.5 %collective-permute-start.22 = (bf16[40,512]{1,0:T(8,128)(2,1)S(1)}, bf16[40,512]{1,0:T(8,128)(2,1)S(1)}, u32[]{:S(2)}, u32[]{:S(2)}) collective-permute-start(bf16[40,512]{1,0:T(8,128)(2,1)S(1)} %get-tuple-element.33), channel_id=1, source_target_pairs={{0,12},{2,30},{4,8},{6,26},{8,4},{10,22},{12,0},{14,18},{16,28},{1... | collective-permute-start | bytes 122888 | tf_op jit(solution)/shard_map/ppermute | solution.py:321
  73.9 15.6 %all-to-all-done.1 = bf16[8,32,2048]{2,1,0:T(8,128)(2,1)S(1)} async-done(((bf16[8,32,2048]{2,1,0:T(8,128)(2,1)}), bf16[8,32,2048]{2,1,0:T(8,128)(2,1)S(1)}, u32[]{:S(2)}, u32[]{:S(2)}) %all-to-all-start.1) | async-done | bytes 1048608 | tf_op jit(solution)/shard_map/all_to_all | solution.py:276
  89.5 1.0 %collective-permute-start.20 = (bf16[40,512]{1,0:T(8,128)(2,1)S(1)}, bf16[40,512]{1,0:T(8,128)(2,1)S(1)}, u32[]{:S(2)}, u32[]{:S(2)}) collective-permute-start(bf16[40,512]{1,0:T(8,128)(2,1)S(1)} %get-tuple-element.19), channel_id=1, source_target_pairs={{0,4},{2,22},{4,0},{6,18},{8,12},{10,30},{12,8},{14,26},{16,20},{1... | collective-permute-start | bytes 122888 | tf_op jit(solution)/shard_map/ppermute | solution.py:321
  90.5 0.0 collective-permute-done.19
  90.5 0.1 collective-permute-start.23
  90.6 0.0 collective-permute-done.21.refs_2_
  90.6 0.5 collective-permute-start.25
  91.1 0.0 collective-permute-done.22.refs_3_
  91.1 0.1 collective-permute-start.26
  91.2 2.3 %collective-permute-done.20.refs_1_ = bf16[40,512]{1,0:T(8,128)(2,1)S(1)} collective-permute-done((bf16[40,512]{1,0:T(8,128)(2,1)S(1)}, bf16[40,512]{1,0:T(8,128)(2,1)S(1)}, u32[]{:S(2)}, u32[]{:S(2)}) %collective-permute-start.20) | collective-permute-done | bytes 40992 | tf_op jit(solution)/shard_map/ppermute | solution.py:321
  93.5 1.1 %shard_map.87 = f32[32,8192]{1,0:T(8,128)} custom-call(bf16[2,4,32,2048]{3,2,1,0:T(8,128)(2,1)S(1)} %bitcast.43), custom_call_target="tpu_custom_call" | custom-call | flops 1048576 | bytes 2097152 | tf_op jit(solution)/shard_map/pallas_call | solution.py:170
  94.6 0.0 collective-permute-done.25.refs_6_
  94.6 0.0 collective-permute-done.26.refs_7_
  94.6 0.1 collective-permute-done.24.refs_5_
  94.7 0.7 shard_map.86
  (29 shorter events, 0.3 us)
Async XLA Ops:
  0.6 16.2 %copy-start.1 = (bf16[64,8192]{1,0:T(8,128)(2,1)S(1)}, bf16[64,8192]{1,0:T(8,128)(2,1)}, u32[]{:S(2)}) copy-start(bf16[64,8192]{1,0:T(8,128)(2,1)} %param.6) | copy-start | bytes 3145732
  0.6 16.0 %copy-start.2 = (s32[64]{0:T(128)S(1)}, s32[64]{0:T(128)}, u32[]{:S(2)}) copy-start(s32[64]{0:T(128)} %param.11) | copy-start | bytes 772
  0.7 16.2 %copy-start = (f32[8192]{0:T(1024)S(1)}, f32[8192]{0:T(1024)}, u32[]{:S(2)}) copy-start(f32[8192]{0:T(1024)} %param.7) | copy-start | bytes 98308
  2.3 14.6 %collective-permute-start = (f32[64]{0:T(128)S(1)}, f32[64]{0:T(128)S(1)}, u32[]{:S(2)}, u32[]{:S(2)}) collective-permute-start(f32[64]{0:T(128)S(1)} %fusion), channel_id=1, source_target_pairs={{0,1},{1,0},{2,3},{3,2},{4,5},{5,4},{6,7},{7,6},{8,9},{9,8},{10,11... | collective-permute-start | bytes 776 | tf_op jit(solution)/shard_map/ppermute | solution.py:36
  5.3 14.4 %all-to-all-start = ((bf16[16,8,512]{2,1,0:T(8,128)(2,1)}), bf16[16,8,512]{2,1,0:T(8,128)(2,1)S(1)}, u32[]{:S(2)}, u32[]{:S(2)}) async-start(bf16[16,8,512]{2,1,0:T(8,128)(2,1)} %bitcast.48), calls=%async_computation | async-start | bytes 262144 | tf_op jit(solution)/shard_map/all_to_all | solution.py:236
  12.4 8.9 %collective-permute-start.10 = (bf16[32,2048]{1,0:T(8,128)(2,1)S(1)}, bf16[32,2048]{1,0:T(8,128)(2,1)S(1)}, u32[]{:S(2)}, u32[]{:S(2)}) collective-permute-start(bf16[32,2048]{1,0:T(8,128)(2,1)S(1)} %get-tuple-element.29), channel_id=1, source_target_pairs={{0,12},{4,8},{8,4},{12,0},{1,13},{5,9},{9,5},{13,1},{2,14},{6,10},... | collective-permute-start | bytes 393224 | tf_op jit(solution)/shard_map/ppermute | solution.py:50
  15.3 8.5 %collective-permute-start.8 = (bf16[32,2048]{1,0:T(8,128)(2,1)S(1)}, bf16[32,2048]{1,0:T(8,128)(2,1)S(1)}, u32[]{:S(2)}, u32[]{:S(2)}) collective-permute-start(bf16[32,2048]{1,0:T(8,128)(2,1)S(1)} %get-tuple-element.28), channel_id=1, source_target_pairs={{0,4},{4,0},{8,12},{12,8},{1,5},{5,1},{9,13},{13,9},{2,6},{6,2},{1... | collective-permute-start | bytes 393224 | tf_op jit(solution)/shard_map/ppermute | solution.py:50
  15.8 8.0 %collective-permute-start.9 = (bf16[32,2048]{1,0:T(8,128)(2,1)S(1)}, bf16[32,2048]{1,0:T(8,128)(2,1)S(1)}, u32[]{:S(2)}, u32[]{:S(2)}) collective-permute-start(bf16[32,2048]{1,0:T(8,128)(2,1)S(1)} %get-tuple-element.30), channel_id=1, source_target_pairs={{0,8},{4,12},{8,0},{12,4},{1,9},{5,13},{9,1},{13,5},{2,10},{6,14},... | collective-permute-start | bytes 393224 | tf_op jit(solution)/shard_map/ppermute | solution.py:50
  20.2 9.8 %collective-permute-start.1 = (bf16[64,2560]{1,0:T(8,128)(2,1)S(1)}, bf16[64,2560]{1,0:T(8,128)(2,1)S(1)}, u32[]{:S(2)}, u32[]{:S(2)}) collective-permute-start(bf16[64,2560]{1,0:T(8,128)(2,1)S(1)} %get-tuple-element.40), channel_id=1, source_target_pairs={{0,4},{4,0},{8,12},{12,8},{1,5},{5,1},{9,13},{13,9},{2,6},{6,2},{1... | collective-permute-start | bytes 983048 | tf_op jit(solution)/shard_map/ppermute | solution.py:50
  20.3 21.9 %collective-permute-start.2 = (bf16[64,2560]{1,0:T(8,128)(2,1)S(1)}, bf16[64,2560]{1,0:T(8,128)(2,1)S(1)}, u32[]{:S(2)}, u32[]{:S(2)}) collective-permute-start(bf16[64,2560]{1,0:T(8,128)(2,1)S(1)} %get-tuple-element.41), channel_id=1, source_target_pairs={{0,8},{4,12},{8,0},{12,4},{1,9},{5,13},{9,1},{13,5},{2,10},{6,14},... | collective-permute-start | bytes 983048 | tf_op jit(solution)/shard_map/ppermute | solution.py:50
  21.3 27.2 %collective-permute-start.3 = (bf16[64,2560]{1,0:T(8,128)(2,1)S(1)}, bf16[64,2560]{1,0:T(8,128)(2,1)S(1)}, u32[]{:S(2)}, u32[]{:S(2)}) collective-permute-start(bf16[64,2560]{1,0:T(8,128)(2,1)S(1)} %get-tuple-element.39), channel_id=1, source_target_pairs={{0,12},{4,8},{8,4},{12,0},{1,13},{5,9},{9,5},{13,1},{2,14},{6,10},... | collective-permute-start | bytes 983048 | tf_op jit(solution)/shard_map/ppermute | solution.py:50
  23.8 24.6 %collective-permute-start.11 = (bf16[128,2048]{1,0:T(8,128)(2,1)S(1)}, bf16[128,2048]{1,0:T(8,128)(2,1)S(1)}, u32[]{:S(2)}, u32[]{:S(2)}) collective-permute-start(bf16[128,2048]{1,0:T(8,128)(2,1)S(1)} %pad_maximum_fusion.4.refs_8_), channel_id=1, source_target_pairs={{0,16},{16,0},{1,17},{17,1},{2,18},{18,2},{3,19},{19,3},{4,20},{20... | collective-permute-start | bytes 1572872 | tf_op jit(solution)/shard_map/ppermute | solution.py:234
  25.5 23.0 %collective-permute-start.4 = (bf16[64,2560]{1,0:T(8,128)(2,1)S(1)}, bf16[64,2560]{1,0:T(8,128)(2,1)S(1)}, u32[]{:S(2)}, u32[]{:S(2)}) collective-permute-start(bf16[64,2560]{1,0:T(8,128)(2,1)S(1)} %get-tuple-element.42.refs_0_), channel_id=1, source_target_pairs={{0,2},{2,0},{1,3},{3,1},{4,6},{6,4},{5,7},{7,5},{8,10},{10,8},{9,1... | collective-permute-start | bytes 983048 | tf_op jit(solution)/shard_map/ppermute | solution.py:41
  30.0 18.5 %collective-permute-start.5 = (bf16[64,2560]{1,0:T(8,128)(2,1)S(1)}, bf16[64,2560]{1,0:T(8,128)(2,1)S(1)}, u32[]{:S(2)}, u32[]{:S(2)}) collective-permute-start(bf16[64,2560]{1,0:T(8,128)(2,1)S(1)} %collective-permute-done.1.refs_1_), channel_id=1, source_target_pairs={{0,2},{2,0},{1,3},{3,1},{4,6},{6,4},{5,7},{7,5},{8,10},{10,8},{9,1... | collective-permute-start | bytes 983048 | tf_op jit(solution)/shard_map/ppermute | solution.py:41
  42.2 6.2 %collective-permute-start.6 = (bf16[64,2560]{1,0:T(8,128)(2,1)S(1)}, bf16[64,2560]{1,0:T(8,128)(2,1)S(1)}, u32[]{:S(2)}, u32[]{:S(2)}) collective-permute-start(bf16[64,2560]{1,0:T(8,128)(2,1)S(1)} %collective-permute-done.2.refs_2_), channel_id=1, source_target_pairs={{0,2},{2,0},{1,3},{3,1},{4,6},{6,4},{5,7},{7,5},{8,10},{10,8},{9,1... | collective-permute-start | bytes 983048 | tf_op jit(solution)/shard_map/ppermute | solution.py:41
  48.5 1.6 %collective-permute-start.7 = (bf16[64,2560]{1,0:T(8,128)(2,1)S(1)}, bf16[64,2560]{1,0:T(8,128)(2,1)S(1)}, u32[]{:S(2)}, u32[]{:S(2)}) collective-permute-start(bf16[64,2560]{1,0:T(8,128)(2,1)S(1)} %collective-permute-done.3.refs_3_), channel_id=1, source_target_pairs={{0,2},{2,0},{1,3},{3,1},{4,6},{6,4},{5,7},{7,5},{8,10},{10,8},{9,1... | collective-permute-start | bytes 983048 | tf_op jit(solution)/shard_map/ppermute | solution.py:41
  54.1 7.2 %collective-permute-start.12 = (bf16[2,64,256]{2,1,0:T(8,128)(2,1)S(1)}, bf16[2,64,256]{2,1,0:T(8,128)(2,1)S(1)}, u32[]{:S(2)}, u32[]{:S(2)}) collective-permute-start(bf16[2,64,256]{2,1,0:T(8,128)(2,1)S(1)} %get-tuple-element.14), channel_id=1, source_target_pairs={{0,4},{4,0},{8,12},{12,8},{1,5},{5,1},{9,13},{13,9},{2,6},{6,2},{1... | collective-permute-start | bytes 196616 | tf_op jit(solution)/shard_map/ppermute | solution.py:269
  55.3 6.0 %collective-permute-start.13 = (bf16[2,64,256]{2,1,0:T(8,128)(2,1)S(1)}, bf16[2,64,256]{2,1,0:T(8,128)(2,1)S(1)}, u32[]{:S(2)}, u32[]{:S(2)}) collective-permute-start(bf16[2,64,256]{2,1,0:T(8,128)(2,1)S(1)} %get-tuple-element.15), channel_id=1, source_target_pairs={{0,8},{4,12},{8,0},{12,4},{1,9},{5,13},{9,1},{13,5},{2,10},{6,14},... | collective-permute-start | bytes 196616 | tf_op jit(solution)/shard_map/ppermute | solution.py:269
  55.3 6.0 %collective-permute-start.14 = (bf16[2,64,256]{2,1,0:T(8,128)(2,1)S(1)}, bf16[2,64,256]{2,1,0:T(8,128)(2,1)S(1)}, u32[]{:S(2)}, u32[]{:S(2)}) collective-permute-start(bf16[2,64,256]{2,1,0:T(8,128)(2,1)S(1)} %get-tuple-element.16), channel_id=1, source_target_pairs={{0,12},{4,8},{8,4},{12,0},{1,13},{5,9},{9,5},{13,1},{2,14},{6,10},... | collective-permute-start | bytes 196616 | tf_op jit(solution)/shard_map/ppermute | solution.py:269
  57.7 31.8 %all-to-all-start.1 = ((bf16[8,32,2048]{2,1,0:T(8,128)(2,1)}), bf16[8,32,2048]{2,1,0:T(8,128)(2,1)S(1)}, u32[]{:S(2)}, u32[]{:S(2)}) async-start(bf16[8,32,2048]{2,1,0:T(8,128)(2,1)} %bitcast.15), calls=%async_computation.1 | async-start | bytes 2097152 | tf_op jit(solution)/shard_map/all_to_all | solution.py:276
  61.4 5.0 %collective-permute-start.15 = (f32[2,64,256]{2,1,0:T(8,128)S(1)}, f32[2,64,256]{2,1,0:T(8,128)S(1)}, u32[]{:S(2)}, u32[]{:S(2)}) collective-permute-start(f32[2,64,256]{2,1,0:T(8,128)S(1)} %convert_add_fusion), channel_id=1, source_target_pairs={{0,1},{1,0},{2,3},{3,2},{4,5},{5,4},{6,7},{7,6},{8,9},{9,8},{10,11... | collective-permute-start | bytes 393224 | tf_op jit(solution)/shard_map/ppermute | solution.py:36
  62.0 4.6 %collective-permute-start.18 = (f32[2048]{0:T(1024)S(1)}, f32[2048]{0:T(1024)S(1)}, u32[]{:S(2)}, u32[]{:S(2)}) collective-permute-start(f32[2048]{0:T(1024)S(1)} %bitcast.45), channel_id=1, source_target_pairs={{0,2},{2,0},{1,3},{3,1},{4,6},{6,4},{5,7},{7,5},{8,10},{10,8},{9,1... | collective-permute-start | bytes 24584 | tf_op jit(solution)/shard_map/ppermute | solution.py:41
  66.5 1.3 %collective-permute-start.16 = (bf16[64,256]{1,0:T(8,128)(2,1)S(1)}, bf16[64,256]{1,0:T(8,128)(2,1)S(1)}, u32[]{:S(2)}, u32[]{:S(2)}) collective-permute-start(bf16[64,256]{1,0:T(8,128)(2,1)S(1)} %get-tuple-element.38), channel_id=1, source_target_pairs={{0,2},{2,0},{1,3},{3,1},{4,6},{6,4},{5,7},{7,5},{8,10},{10,8},{9,1... | collective-permute-start | bytes 98312 | tf_op jit(solution)/shard_map/ppermute | solution.py:41
  68.3 1.3 %collective-permute-start.17 = (bf16[4,2,8,512]{3,2,1,0:T(8,128)(2,1)S(1)}, bf16[4,2,8,512]{3,2,1,0:T(8,128)(2,1)S(1)}, u32[]{:S(2)}, u32[]{:S(2)}) collective-permute-start(bf16[4,2,8,512]{3,2,1,0:T(8,128)(2,1)S(1)} %dynamic-slice_bitcast_fusion), channel_id=1, source_target_pairs={{0,2},{2,0},{1,3},{3,1},{4,6},{6,4},{5,7},{7,5},{8,10},{10,8},{9,1... | collective-permute-start | bytes 196616 | tf_op jit(solution)/shard_map/ppermute | solution.py:41
  69.7 20.8 %collective-permute-start.19 = (bf16[40,512]{1,0:T(8,128)(2,1)S(1)}, bf16[40,512]{1,0:T(8,128)(2,1)S(1)}, u32[]{:S(2)}, u32[]{:S(2)}) collective-permute-start(bf16[40,512]{1,0:T(8,128)(2,1)S(1)} %get-tuple-element.34), channel_id=1, source_target_pairs={{2,18},{6,22},{10,26},{14,30},{18,2},{22,6},{26,10},{30,14},{3,19}... | collective-permute-start | bytes 122888 | tf_op jit(solution)/shard_map/ppermute | solution.py:321
  70.3 20.3 %collective-permute-start.21 = (bf16[40,512]{1,0:T(8,128)(2,1)S(1)}, bf16[40,512]{1,0:T(8,128)(2,1)S(1)}, u32[]{:S(2)}, u32[]{:S(2)}) collective-permute-start(bf16[40,512]{1,0:T(8,128)(2,1)S(1)} %get-tuple-element.36), channel_id=1, source_target_pairs={{0,8},{2,26},{4,12},{6,30},{8,0},{10,18},{12,4},{14,22},{16,24},{1... | collective-permute-start | bytes 122888 | tf_op jit(solution)/shard_map/ppermute | solution.py:321
  72.4 18.7 %collective-permute-start.22 = (bf16[40,512]{1,0:T(8,128)(2,1)S(1)}, bf16[40,512]{1,0:T(8,128)(2,1)S(1)}, u32[]{:S(2)}, u32[]{:S(2)}) collective-permute-start(bf16[40,512]{1,0:T(8,128)(2,1)S(1)} %get-tuple-element.33), channel_id=1, source_target_pairs={{0,12},{2,30},{4,8},{6,26},{8,4},{10,22},{12,0},{14,18},{16,28},{1... | collective-permute-start | bytes 122888 | tf_op jit(solution)/shard_map/ppermute | solution.py:321
  89.5 4.0 %collective-permute-start.20 = (bf16[40,512]{1,0:T(8,128)(2,1)S(1)}, bf16[40,512]{1,0:T(8,128)(2,1)S(1)}, u32[]{:S(2)}, u32[]{:S(2)}) collective-permute-start(bf16[40,512]{1,0:T(8,128)(2,1)S(1)} %get-tuple-element.19), channel_id=1, source_target_pairs={{0,4},{2,22},{4,0},{6,18},{8,12},{10,30},{12,8},{14,26},{16,20},{1... | collective-permute-start | bytes 122888 | tf_op jit(solution)/shard_map/ppermute | solution.py:321
  90.5 4.1 %collective-permute-start.23 = (bf16[40,512]{1,0:T(8,128)(2,1)S(1)}, bf16[40,512]{1,0:T(8,128)(2,1)S(1)}, u32[]{:S(2)}, u32[]{:S(2)}) collective-permute-start(bf16[40,512]{1,0:T(8,128)(2,1)S(1)} %broadcast_select_fusion.refs_0_), channel_id=1, source_target_pairs={{0,2},{2,0},{1,3},{3,1},{4,6},{6,4},{5,7},{7,5},{8,10},{10,8},{9,1... | collective-permute-start | bytes 122888 | tf_op jit(solution)/shard_map/ppermute | solution.py:41
  90.6 4.0 %collective-permute-start.25 = (bf16[40,512]{1,0:T(8,128)(2,1)S(1)}, bf16[40,512]{1,0:T(8,128)(2,1)S(1)}, u32[]{:S(2)}, u32[]{:S(2)}) collective-permute-start(bf16[40,512]{1,0:T(8,128)(2,1)S(1)} %collective-permute-done.21.refs_2_), channel_id=1, source_target_pairs={{0,2},{2,0},{1,3},{3,1},{4,6},{6,4},{5,7},{7,5},{8,10},{10,8},{9,1... | collective-permute-start | bytes 122888 | tf_op jit(solution)/shard_map/ppermute | solution.py:41
  91.1 3.5 %collective-permute-start.26 = (bf16[40,512]{1,0:T(8,128)(2,1)S(1)}, bf16[40,512]{1,0:T(8,128)(2,1)S(1)}, u32[]{:S(2)}, u32[]{:S(2)}) collective-permute-start(bf16[40,512]{1,0:T(8,128)(2,1)S(1)} %collective-permute-done.22.refs_3_), channel_id=1, source_target_pairs={{0,2},{2,0},{1,3},{3,1},{4,6},{6,4},{5,7},{7,5},{8,10},{10,8},{9,1... | collective-permute-start | bytes 122888 | tf_op jit(solution)/shard_map/ppermute | solution.py:41
  93.5 1.2 %collective-permute-start.24 = (bf16[40,512]{1,0:T(8,128)(2,1)S(1)}, bf16[40,512]{1,0:T(8,128)(2,1)S(1)}, u32[]{:S(2)}, u32[]{:S(2)}) collective-permute-start(bf16[40,512]{1,0:T(8,128)(2,1)S(1)} %collective-permute-done.20.refs_1_), channel_id=1, source_target_pairs={{0,2},{2,0},{1,3},{3,1},{4,6},{6,4},{5,7},{7,5},{8,10},{10,8},{9,1... | collective-permute-start | bytes 122888 | tf_op jit(solution)/shard_map/ppermute | solution.py:41

commit v6 on v5

--- a/solution.py
+++ b/solution.py
@@ -65,7 +65,7 @@
     return accepted, one_hot(position, shards * capacity)
 
 
-def products_kernel(pieces, owned, low, core_keys, part, chunk, *refs):
+def products_kernel(pieces, owned, core_keys, part, chunk, *refs):
     row_refs, weight_refs = refs[: 2 * pieces], refs[2 * pieces : 2 * pieces + 2]
     grad_ref, gain_ref = refs[2 * pieces + 2 : 2 * pieces + 4]
     key_refs = refs[2 * pieces + 4 : 3 * pieces + 4]
@@ -74,7 +74,6 @@
     ]
     piece_rows = row_refs[0].shape[0]
     half_keys = core_keys // 2
-    key_width = 2 * core_keys
 
     copies = []
     for j, ref in enumerate(row_refs):
@@ -125,14 +124,13 @@
             ref[k] = sums_ref[first : first + piece_rows].astype(jnp.bfloat16)
 
 
-def products(rows_here, rows_there, weights, places, core_keys, part, owned):
-    pieces, low = len(rows_here), lax.axis_size("lo")
+def products(rows_here, rows_there, weights, core_keys, part, owned):
+    pieces = len(rows_here)
     piece_rows, columns = rows_here[0].shape
-    half_keys = core_keys // 2
     total = 2 * pieces * piece_rows
     return pl.pallas_call(
         functools.partial(
-            products_kernel, pieces, owned, low, core_keys, part, min(CHUNK, part)
+            products_kernel, pieces, owned, core_keys, part, min(CHUNK, part)
         ),
         out_shape=[
             jax.ShapeDtypeStruct((core_keys, part), jnp.bfloat16),
@@ -182,7 +180,8 @@
 def gather_kernel(key_rows, factor, *refs):
     pieces, norm_ref, key_ref, gain_ref = refs[:-3], refs[-3], refs[-2], refs[-1]
     low, columns = len(pieces) // 2, key_ref.shape[1]
-    half_rows, wide = (pieces[0].shape[0] - 2 * key_rows) // 2, columns // LANES
+    wide = columns // LANES
+    half_rows = gain_ref.shape[0] // (low * wide)
     hi, lo, core = (lax.axis_index(name) for name in DP)
     mine = pl.ds(pl.multiple_of(core * key_rows, key_rows), key_rows)
     for step in range(low):
@@ -193,7 +192,7 @@
             at = ((hi ^ core ^ k) * low + place) * key_rows
             key_ref[pl.ds(pl.multiple_of(at, key_rows), key_rows)] = piece[mine]
             terms = piece[2 * key_rows :].astype(jnp.float32)
-            total = total + terms[:half_rows] + terms[half_rows:]
+            total = total + terms[:half_rows] + terms[half_rows : 2 * half_rows]
         for i in range(half_rows):
             for j in range(wide):
                 at = pl.ds((place * half_rows + i) * wide + j, 1)
@@ -223,7 +222,7 @@
     model_width = width * lax.axis_size("tensor")
     owned, key_width = key_weight.shape[0], cotangent.shape[2]
     part = width // low
-    core_keys, half_keys = key_width // cores, low * owned
+    core_keys = key_width // cores
     capacity = cotangent.shape[1] // replicas
     factor = 1.0 / math.sqrt(rows * replicas)
 
@@ -260,7 +259,7 @@
     )
     rows_there = [swap_core(piece) for piece in rows_here]
     grad_part, gain_part, *key_parts = products(
-        rows_here, rows_there, (weight_here, weight_there), places, core_keys, part, owned
+        rows_here, rows_there, (weight_here, weight_there), core_keys, part, owned
     )
     gain_part = gain_part[0]
 
@@ -296,7 +295,7 @@
     gain_part = gain_part + swap_core(gain_part)
     upper = lax.reduce_precision(gain_part, 8, 7)
     terms = jnp.concatenate([upper, gain_part - upper]).astype(jnp.bfloat16)
-    extra = -(-2 * part // (8 * key_width)) * 8
+    extra = -(-2 * part // (16 * key_width)) * 16
     terms = jnp.pad(terms, (0, extra * key_width - 2 * part)).reshape(1, extra, key_width)
     key_rows = cores * capacity
     routed = jnp.concatenate(

time: 95.8 us -> 96.4 us (level)
  no operation moved by 1% of the time
where the time goes in v6:
time: 96.4 us; the launch traced here: 96.1 us
  waiting for transfers between devices  52.5 us (54%)
  starting transfers between devices  31.5 us (33%)
  Pallas kernels  5.86 us (6%)
  other arithmetic  2.45 us (3%)
  between operations  1.63 us (2%)
  local copies, waits for them, and re-layouts  1.29 us (1%)
    ppermute x6, waiting for transfers between devices, swap_lo(): pieces.append(lax.ppermute(block(me ^ step), 'lo', pairs))  23 us
    all_to_all x1, waiting for transfers between devices, on_device(): lax.all_to_all(grad_part.reshape(halves * low, owned, part), ('hi', 'lo')...  16.1 us
    ppermute x6, starting transfers between devices, swap_lo(): pieces.append(lax.ppermute(block(me ^ step), 'lo', pairs))  7.11 us
    all_to_all x1, starting transfers between devices, on_device(): lax.all_to_all(cotangent[0], DP, split_axis=0, concat_axis=0, tiled=True)  5.94 us
    ppermute x4, starting transfers between devices, on_device(): pieces[step] = lax.ppermute(pieces[step], DP, pairs)  4.94 us
    ppermute x2, waiting for transfers between devices, reduce_tensor(): return value + lax.ppermute(value, 'tensor', SWAP)  4.43 us
    pallas_call x1, Pallas kernels, products(): pl.pallas_call(functools.partial(products_kernel, pieces, owned, core_key...  4.05 us
    ppermute x11, waiting for transfers between devices, swap_core(): return lax.ppermute(value, 'core', SWAP)  3.94 us
  transfers between devices with their start and end apart: 29, of which 11 were waited for; matrix products, arithmetic and copies ran while one was open for 3% of the time, Pallas kernels for 1%

profile of v6, /device:TPU:0, one launch (start us, length us, event | category | flops | bytes accessed | tf_op | source)
XLA Modules:
  0.0 96.1 jit_solution(6743452846860153763)
XLA Ops:
  0.7 1.6 %fusion = f32[64]{0:T(128)S(1)} fusion(bf16[64,8192]{1,0:T(8,128)(2,1)} %param.6), kind=kLoop, calls=%fused_computation.2 | loop fusion | flops 1572800 | bytes 1048832 | tf_op jit(solution)/shard_map/reduce_sum | solution.py:249
  2.3 3.0 %collective-permute-start = (f32[64]{0:T(128)S(1)}, f32[64]{0:T(128)S(1)}, u32[]{:S(2)}, u32[]{:S(2)}) collective-permute-start(f32[64]{0:T(128)S(1)} %fusion), channel_id=1, source_target_pairs={{0,1},{1,0},{2,3},{3,2},{4,5},{5,4},{6,7},{7,6},{8,9},{9,8},{10,11... | collective-permute-start | bytes 776 | tf_op jit(solution)/shard_map/ppermute | solution.py:36
  5.3 5.9 %all-to-all-start = ((bf16[16,8,512]{2,1,0:T(8,128)(2,1)}), bf16[16,8,512]{2,1,0:T(8,128)(2,1)S(1)}, u32[]{:S(2)}, u32[]{:S(2)}) async-start(bf16[16,8,512]{2,1,0:T(8,128)(2,1)} %bitcast.48), calls=%async_computation | async-start | bytes 262144 | tf_op jit(solution)/shard_map/all_to_all | solution.py:235
  11.3 1.1 %constant_dynamic-slice_fusion.3 = (bf16[32,2048]{1,0:T(8,128)(2,1)S(1)}, bf16[32,2048]{1,0:T(8,128)(2,1)S(1)}, bf16[32,2048]{1,0:T(8,128)(2,1)S(1)}, bf16[32,2048]{1,0:T(8,128)(2,1)S(1)}) fusion(bf16[32,8192]{1,0:T(8,128)(2,1)} %param.8, s32[]{:T(128)S(6)} %select_n.103, s32[]{:T(128)S(6)} %select_n.108, s32[]{:T(128)S(6)} %select_n.110, s32[]{:T(128)S(6)} %select_n.109), kind=kLoop, calls=%fused_computation.65 | loop fusion | bytes 1048592 | tf_op jit(solution)/shard_map/dynamic_slice | solution.py:230
  12.4 2.9 %collective-permute-start.10 = (bf16[32,2048]{1,0:T(8,128)(2,1)S(1)}, bf16[32,2048]{1,0:T(8,128)(2,1)S(1)}, u32[]{:S(2)}, u32[]{:S(2)}) collective-permute-start(bf16[32,2048]{1,0:T(8,128)(2,1)S(1)} %get-tuple-element.29), channel_id=1, source_target_pairs={{0,12},{4,8},{8,4},{12,0},{1,13},{5,9},{9,5},{13,1},{2,14},{6,10},... | collective-permute-start | bytes 393224 | tf_op jit(solution)/shard_map/ppermute | solution.py:50
  15.3 0.6 collective-permute-start.8
  15.8 0.2 collective-permute-start.9
  16.7 0.2 convert_reduce_fusion
  16.9 0.0 collective-permute-done
  16.9 0.4 fusion.3
  17.3 0.1 constant_dynamic-slice_fusion.4
  17.4 2.3 %all-to-all-done = bf16[16,8,512]{2,1,0:T(8,128)(2,1)S(1)} async-done(((bf16[16,8,512]{2,1,0:T(8,128)(2,1)}), bf16[16,8,512]{2,1,0:T(8,128)(2,1)S(1)}, u32[]{:S(2)}, u32[]{:S(2)}) %all-to-all-start) | async-done | bytes 131104 | tf_op jit(solution)/shard_map/all_to_all | solution.py:235
  19.7 0.4 convolution_convert_fusion.2
  20.1 0.1 pad_maximum_fusion
  20.2 0.1 collective-permute-start.1
  20.3 1.0 %collective-permute-start.2 = (bf16[64,2560]{1,0:T(8,128)(2,1)S(1)}, bf16[64,2560]{1,0:T(8,128)(2,1)S(1)}, u32[]{:S(2)}, u32[]{:S(2)}) collective-permute-start(bf16[64,2560]{1,0:T(8,128)(2,1)S(1)} %get-tuple-element.41), channel_id=1, source_target_pairs={{0,8},{4,12},{8,0},{12,4},{1,9},{5,13},{9,1},{13,5},{2,10},{6,14},... | collective-permute-start | bytes 983048 | tf_op jit(solution)/shard_map/ppermute | solution.py:50
  21.3 0.0 collective-permute-done.10
  21.3 2.5 %collective-permute-start.3 = (bf16[64,2560]{1,0:T(8,128)(2,1)S(1)}, bf16[64,2560]{1,0:T(8,128)(2,1)S(1)}, u32[]{:S(2)}, u32[]{:S(2)}) collective-permute-start(bf16[64,2560]{1,0:T(8,128)(2,1)S(1)} %get-tuple-element.39), channel_id=1, source_target_pairs={{0,12},{4,8},{8,4},{12,0},{1,13},{5,9},{9,5},{13,1},{2,14},{6,10},... | collective-permute-start | bytes 983048 | tf_op jit(solution)/shard_map/ppermute | solution.py:50
  23.8 0.0 collective-permute-done.8
  23.8 0.0 collective-permute-done.9
  23.8 1.7 %collective-permute-start.11 = (bf16[128,2048]{1,0:T(8,128)(2,1)S(1)}, bf16[128,2048]{1,0:T(8,128)(2,1)S(1)}, u32[]{:S(2)}, u32[]{:S(2)}) collective-permute-start(bf16[128,2048]{1,0:T(8,128)(2,1)S(1)} %pad_maximum_fusion.4.refs_8_), channel_id=1, source_target_pairs={{0,16},{16,0},{1,17},{17,1},{2,18},{18,2},{3,19},{19,3},{4,20},{20... | collective-permute-start | bytes 1572872 | tf_op jit(solution)/shard_map/ppermute | solution.py:233
  25.5 0.0 collective-permute-start.4
  25.5 4.5 %collective-permute-done.1.refs_1_ = bf16[64,2560]{1,0:T(8,128)(2,1)S(1)} collective-permute-done((bf16[64,2560]{1,0:T(8,128)(2,1)S(1)}, bf16[64,2560]{1,0:T(8,128)(2,1)S(1)}, u32[]{:S(2)}, u32[]{:S(2)}) %collective-permute-start.1) | collective-permute-done | bytes 327712 | tf_op jit(solution)/shard_map/ppermute | solution.py:50
  30.0 0.0 collective-permute-start.5
  30.0 12.3 %collective-permute-done.2.refs_2_ = bf16[64,2560]{1,0:T(8,128)(2,1)S(1)} collective-permute-done((bf16[64,2560]{1,0:T(8,128)(2,1)S(1)}, bf16[64,2560]{1,0:T(8,128)(2,1)S(1)}, u32[]{:S(2)}, u32[]{:S(2)}) %collective-permute-start.2) | collective-permute-done | bytes 327712 | tf_op jit(solution)/shard_map/ppermute | solution.py:50
  42.2 0.0 collective-permute-start.6
  42.2 6.2 %collective-permute-done.3.refs_3_ = bf16[64,2560]{1,0:T(8,128)(2,1)S(1)} collective-permute-done((bf16[64,2560]{1,0:T(8,128)(2,1)S(1)}, bf16[64,2560]{1,0:T(8,128)(2,1)S(1)}, u32[]{:S(2)}, u32[]{:S(2)}) %collective-permute-start.3) | collective-permute-done | bytes 327712 | tf_op jit(solution)/shard_map/ppermute | solution.py:50
  48.5 0.0 collective-permute-start.7
  48.5 0.0 collective-permute-done.4.refs_4_
  48.5 0.0 collective-permute-done.11.refs_9_
  48.5 0.0 collective-permute-done.5.refs_5_
  48.5 0.0 collective-permute-done.6.refs_6_
  48.5 1.6 %collective-permute-done.7.refs_7_ = bf16[64,2560]{1,0:T(8,128)(2,1)S(1)} collective-permute-done((bf16[64,2560]{1,0:T(8,128)(2,1)S(1)}, bf16[64,2560]{1,0:T(8,128)(2,1)S(1)}, u32[]{:S(2)}, u32[]{:S(2)}) %collective-permute-start.7) | collective-permute-done | bytes 327712 | tf_op jit(solution)/shard_map/ppermute | solution.py:41
  50.1 4.0 %shard_map.85 = (bf16[256,2048]{1,0:T(8,128)(2,1)}, f32[1,2048]{1,0:T(1,128)S(1)}, bf16[2,64,256]{2,1,0:T(8,128)(2,1)S(1)}, bf16[2,64,256]{2,1,0:T(8,128)(2,1)S(...) custom-call(bf16[64,2560]{1,0:T(8,128)(2,1)S(1)} %get-tuple-element.42.refs_0_, ...), custom_call_target="tpu_custom_call" | custom-call | flops 1073741824 | bytes 6815744 | tf_op jit(solution)/shard_map/pallas_call | solution.py:131
  54.1 1.2 %collective-permute-start.12 = (bf16[2,64,256]{2,1,0:T(8,128)(2,1)S(1)}, bf16[2,64,256]{2,1,0:T(8,128)(2,1)S(1)}, u32[]{:S(2)}, u32[]{:S(2)}) collective-permute-start(bf16[2,64,256]{2,1,0:T(8,128)(2,1)S(1)} %get-tuple-element.14), channel_id=1, source_target_pairs={{0,4},{4,0},{8,12},{12,8},{1,5},{5,1},{9,13},{13,9},{2,6},{6,2},{1... | collective-permute-start | bytes 196616 | tf_op jit(solution)/shard_map/ppermute | solution.py:268
  55.3 0.0 collective-permute-start.13
  55.3 2.4 %collective-permute-start.14 = (bf16[2,64,256]{2,1,0:T(8,128)(2,1)S(1)}, bf16[2,64,256]{2,1,0:T(8,128)(2,1)S(1)}, u32[]{:S(2)}, u32[]{:S(2)}) collective-permute-start(bf16[2,64,256]{2,1,0:T(8,128)(2,1)S(1)} %get-tuple-element.16), channel_id=1, source_target_pairs={{0,12},{4,8},{8,4},{12,0},{1,13},{5,9},{9,5},{13,1},{2,14},{6,10},... | collective-permute-start | bytes 196616 | tf_op jit(solution)/shard_map/ppermute | solution.py:268
  57.7 3.7 %all-to-all-start.1 = ((bf16[8,32,2048]{2,1,0:T(8,128)(2,1)}), bf16[8,32,2048]{2,1,0:T(8,128)(2,1)S(1)}, u32[]{:S(2)}, u32[]{:S(2)}) async-start(bf16[8,32,2048]{2,1,0:T(8,128)(2,1)} %bitcast.15), calls=%async_computation.1 | async-start | bytes 2097152 | tf_op jit(solution)/shard_map/all_to_all | solution.py:275
  61.4 0.0 collective-permute-done.12
  61.4 0.0 collective-permute-done.13
  61.4 0.0 collective-permute-done.14
  61.4 0.6 collective-permute-start.15
  62.0 0.0 collective-permute-start.18
  62.0 4.4 %collective-permute-done.15 = f32[2,64,256]{2,1,0:T(8,128)S(1)} collective-permute-done((f32[2,64,256]{2,1,0:T(8,128)S(1)}, f32[2,64,256]{2,1,0:T(8,128)S(1)}, u32[]{:S(2)}, u32[]{:S(2)}) %collective-permute-start.15) | collective-permute-done | bytes 131104 | tf_op jit(solution)/shard_map/ppermute | solution.py:36
  66.5 0.1 collective-permute-start.16
  66.6 0.0 collective-permute-done.18
  66.6 1.2 %collective-permute-done.16 = bf16[64,256]{1,0:T(8,128)(2,1)S(1)} collective-permute-done((bf16[64,256]{1,0:T(8,128)(2,1)S(1)}, bf16[64,256]{1,0:T(8,128)(2,1)S(1)}, u32[]{:S(2)}, u32[]{:S(2)}) %collective-permute-start.16) | collective-permute-done | bytes 32800 | tf_op jit(solution)/shard_map/ppermute | solution.py:41
  67.8 0.5 convolution_convert_fusion
  68.3 0.2 collective-permute-start.17
  68.5 1.1 %collective-permute-done.17 = bf16[4,2,8,512]{3,2,1,0:T(8,128)(2,1)S(1)} collective-permute-done((bf16[4,2,8,512]{3,2,1,0:T(8,128)(2,1)S(1)}, bf16[4,2,8,512]{3,2,1,0:T(8,128)(2,1)S(1)}, u32[]{:S(2)}, u32[]{:S(2)}) %collective-permute-start.17) | collective-permute-done | bytes 65568 | tf_op jit(solution)/shard_map/ppermute | solution.py:41
  69.7 0.7 collective-permute-start.19
  70.3 2.1 %collective-permute-start.21 = (bf16[48,512]{1,0:T(8,128)(2,1)S(1)}, bf16[48,512]{1,0:T(8,128)(2,1)S(1)}, u32[]{:S(2)}, u32[]{:S(2)}) collective-permute-start(bf16[48,512]{1,0:T(8,128)(2,1)S(1)} %get-tuple-element.34), channel_id=1, source_target_pairs={{0,8},{2,26},{4,12},{6,30},{8,0},{10,18},{12,4},{14,22},{16,24},{1... | collective-permute-start | bytes 147464 | tf_op jit(solution)/shard_map/ppermute | solution.py:320
  72.4 1.5 %collective-permute-start.22 = (bf16[48,512]{1,0:T(8,128)(2,1)S(1)}, bf16[48,512]{1,0:T(8,128)(2,1)S(1)}, u32[]{:S(2)}, u32[]{:S(2)}) collective-permute-start(bf16[48,512]{1,0:T(8,128)(2,1)S(1)} %get-tuple-element.31), channel_id=1, source_target_pairs={{0,12},{2,30},{4,8},{6,26},{8,4},{10,22},{12,0},{14,18},{16,28},{1... | collective-permute-start | bytes 147464 | tf_op jit(solution)/shard_map/ppermute | solution.py:320
  73.9 16.1 %all-to-all-done.1 = bf16[8,32,2048]{2,1,0:T(8,128)(2,1)S(1)} async-done(((bf16[8,32,2048]{2,1,0:T(8,128)(2,1)}), bf16[8,32,2048]{2,1,0:T(8,128)(2,1)S(1)}, u32[]{:S(2)}, u32[]{:S(2)}) %all-to-all-start.1) | async-done | bytes 1048608 | tf_op jit(solution)/shard_map/all_to_all | solution.py:275
  90.0 0.7 collective-permute-start.20
  90.8 0.1 collective-permute-start.23
  90.9 0.0 collective-permute-done.21.refs_2_
  90.9 0.5 collective-permute-start.25
  91.4 0.0 collective-permute-done.22.refs_3_
  91.4 0.1 collective-permute-start.26
  91.5 2.7 %collective-permute-done.20.refs_1_ = bf16[48,512]{1,0:T(8,128)(2,1)S(1)} collective-permute-done((bf16[48,512]{1,0:T(8,128)(2,1)S(1)}, bf16[48,512]{1,0:T(8,128)(2,1)S(1)}, u32[]{:S(2)}, u32[]{:S(2)}) %collective-permute-start.20) | collective-permute-done | bytes 49184 | tf_op jit(solution)/shard_map/ppermute | solution.py:320
  94.1 1.1 %shard_map.87 = f32[32,8192]{1,0:T(8,128)} custom-call(bf16[2,4,32,2048]{3,2,1,0:T(8,128)(2,1)S(1)} %bitcast.43), custom_call_target="tpu_custom_call" | custom-call | flops 1048576 | bytes 2097152 | tf_op jit(solution)/shard_map/pallas_call | solution.py:168
  95.3 0.1 collective-permute-done.24.refs_5_
  95.4 0.7 shard_map.86
  (28 shorter events, 0.3 us)
Async XLA Ops:
  0.6 16.2 %copy-start.1 = (bf16[64,8192]{1,0:T(8,128)(2,1)S(1)}, bf16[64,8192]{1,0:T(8,128)(2,1)}, u32[]{:S(2)}) copy-start(bf16[64,8192]{1,0:T(8,128)(2,1)} %param.6) | copy-start | bytes 3145732
  0.6 16.0 %copy-start.2 = (s32[64]{0:T(128)S(1)}, s32[64]{0:T(128)}, u32[]{:S(2)}) copy-start(s32[64]{0:T(128)} %param.11) | copy-start | bytes 772
  0.7 16.2 %copy-start = (f32[8192]{0:T(1024)S(1)}, f32[8192]{0:T(1024)}, u32[]{:S(2)}) copy-start(f32[8192]{0:T(1024)} %param.7) | copy-start | bytes 98308
  2.3 14.6 %collective-permute-start = (f32[64]{0:T(128)S(1)}, f32[64]{0:T(128)S(1)}, u32[]{:S(2)}, u32[]{:S(2)}) collective-permute-start(f32[64]{0:T(128)S(1)} %fusion), channel_id=1, source_target_pairs={{0,1},{1,0},{2,3},{3,2},{4,5},{5,4},{6,7},{7,6},{8,9},{9,8},{10,11... | collective-permute-start | bytes 776 | tf_op jit(solution)/shard_map/ppermute | solution.py:36
  5.3 14.4 %all-to-all-start = ((bf16[16,8,512]{2,1,0:T(8,128)(2,1)}), bf16[16,8,512]{2,1,0:T(8,128)(2,1)S(1)}, u32[]{:S(2)}, u32[]{:S(2)}) async-start(bf16[16,8,512]{2,1,0:T(8,128)(2,1)} %bitcast.48), calls=%async_computation | async-start | bytes 262144 | tf_op jit(solution)/shard_map/all_to_all | solution.py:235
  12.4 8.9 %collective-permute-start.10 = (bf16[32,2048]{1,0:T(8,128)(2,1)S(1)}, bf16[32,2048]{1,0:T(8,128)(2,1)S(1)}, u32[]{:S(2)}, u32[]{:S(2)}) collective-permute-start(bf16[32,2048]{1,0:T(8,128)(2,1)S(1)} %get-tuple-element.29), channel_id=1, source_target_pairs={{0,12},{4,8},{8,4},{12,0},{1,13},{5,9},{9,5},{13,1},{2,14},{6,10},... | collective-permute-start | bytes 393224 | tf_op jit(solution)/shard_map/ppermute | solution.py:50
  15.3 8.5 %collective-permute-start.8 = (bf16[32,2048]{1,0:T(8,128)(2,1)S(1)}, bf16[32,2048]{1,0:T(8,128)(2,1)S(1)}, u32[]{:S(2)}, u32[]{:S(2)}) collective-permute-start(bf16[32,2048]{1,0:T(8,128)(2,1)S(1)} %get-tuple-element.28), channel_id=1, source_target_pairs={{0,4},{4,0},{8,12},{12,8},{1,5},{5,1},{9,13},{13,9},{2,6},{6,2},{1... | collective-permute-start | bytes 393224 | tf_op jit(solution)/shard_map/ppermute | solution.py:50
  15.8 8.0 %collective-permute-start.9 = (bf16[32,2048]{1,0:T(8,128)(2,1)S(1)}, bf16[32,2048]{1,0:T(8,128)(2,1)S(1)}, u32[]{:S(2)}, u32[]{:S(2)}) collective-permute-start(bf16[32,2048]{1,0:T(8,128)(2,1)S(1)} %get-tuple-element.30), channel_id=1, source_target_pairs={{0,8},{4,12},{8,0},{12,4},{1,9},{5,13},{9,1},{13,5},{2,10},{6,14},... | collective-permute-start | bytes 393224 | tf_op jit(solution)/shard_map/ppermute | solution.py:50
  20.2 9.8 %collective-permute-start.1 = (bf16[64,2560]{1,0:T(8,128)(2,1)S(1)}, bf16[64,2560]{1,0:T(8,128)(2,1)S(1)}, u32[]{:S(2)}, u32[]{:S(2)}) collective-permute-start(bf16[64,2560]{1,0:T(8,128)(2,1)S(1)} %get-tuple-element.40), channel_id=1, source_target_pairs={{0,4},{4,0},{8,12},{12,8},{1,5},{5,1},{9,13},{13,9},{2,6},{6,2},{1... | collective-permute-start | bytes 983048 | tf_op jit(solution)/shard_map/ppermute | solution.py:50
  20.3 21.9 %collective-permute-start.2 = (bf16[64,2560]{1,0:T(8,128)(2,1)S(1)}, bf16[64,2560]{1,0:T(8,128)(2,1)S(1)}, u32[]{:S(2)}, u32[]{:S(2)}) collective-permute-start(bf16[64,2560]{1,0:T(8,128)(2,1)S(1)} %get-tuple-element.41), channel_id=1, source_target_pairs={{0,8},{4,12},{8,0},{12,4},{1,9},{5,13},{9,1},{13,5},{2,10},{6,14},... | collective-permute-start | bytes 983048 | tf_op jit(solution)/shard_map/ppermute | solution.py:50
  21.3 27.2 %collective-permute-start.3 = (bf16[64,2560]{1,0:T(8,128)(2,1)S(1)}, bf16[64,2560]{1,0:T(8,128)(2,1)S(1)}, u32[]{:S(2)}, u32[]{:S(2)}) collective-permute-start(bf16[64,2560]{1,0:T(8,128)(2,1)S(1)} %get-tuple-element.39), channel_id=1, source_target_pairs={{0,12},{4,8},{8,4},{12,0},{1,13},{5,9},{9,5},{13,1},{2,14},{6,10},... | collective-permute-start | bytes 983048 | tf_op jit(solution)/shard_map/ppermute | solution.py:50
  23.8 24.6 %collective-permute-start.11 = (bf16[128,2048]{1,0:T(8,128)(2,1)S(1)}, bf16[128,2048]{1,0:T(8,128)(2,1)S(1)}, u32[]{:S(2)}, u32[]{:S(2)}) collective-permute-start(bf16[128,2048]{1,0:T(8,128)(2,1)S(1)} %pad_maximum_fusion.4.refs_8_), channel_id=1, source_target_pairs={{0,16},{16,0},{1,17},{17,1},{2,18},{18,2},{3,19},{19,3},{4,20},{20... | collective-permute-start | bytes 1572872 | tf_op jit(solution)/shard_map/ppermute | solution.py:233
  25.5 23.0 %collective-permute-start.4 = (bf16[64,2560]{1,0:T(8,128)(2,1)S(1)}, bf16[64,2560]{1,0:T(8,128)(2,1)S(1)}, u32[]{:S(2)}, u32[]{:S(2)}) collective-permute-start(bf16[64,2560]{1,0:T(8,128)(2,1)S(1)} %get-tuple-element.42.refs_0_), channel_id=1, source_target_pairs={{0,2},{2,0},{1,3},{3,1},{4,6},{6,4},{5,7},{7,5},{8,10},{10,8},{9,1... | collective-permute-start | bytes 983048 | tf_op jit(solution)/shard_map/ppermute | solution.py:41
  30.0 18.5 %collective-permute-start.5 = (bf16[64,2560]{1,0:T(8,128)(2,1)S(1)}, bf16[64,2560]{1,0:T(8,128)(2,1)S(1)}, u32[]{:S(2)}, u32[]{:S(2)}) collective-permute-start(bf16[64,2560]{1,0:T(8,128)(2,1)S(1)} %collective-permute-done.1.refs_1_), channel_id=1, source_target_pairs={{0,2},{2,0},{1,3},{3,1},{4,6},{6,4},{5,7},{7,5},{8,10},{10,8},{9,1... | collective-permute-start | bytes 983048 | tf_op jit(solution)/shard_map/ppermute | solution.py:41
  42.2 6.2 %collective-permute-start.6 = (bf16[64,2560]{1,0:T(8,128)(2,1)S(1)}, bf16[64,2560]{1,0:T(8,128)(2,1)S(1)}, u32[]{:S(2)}, u32[]{:S(2)}) collective-permute-start(bf16[64,2560]{1,0:T(8,128)(2,1)S(1)} %collective-permute-done.2.refs_2_), channel_id=1, source_target_pairs={{0,2},{2,0},{1,3},{3,1},{4,6},{6,4},{5,7},{7,5},{8,10},{10,8},{9,1... | collective-permute-start | bytes 983048 | tf_op jit(solution)/shard_map/ppermute | solution.py:41
  48.5 1.6 %collective-permute-start.7 = (bf16[64,2560]{1,0:T(8,128)(2,1)S(1)}, bf16[64,2560]{1,0:T(8,128)(2,1)S(1)}, u32[]{:S(2)}, u32[]{:S(2)}) collective-permute-start(bf16[64,2560]{1,0:T(8,128)(2,1)S(1)} %collective-permute-done.3.refs_3_), channel_id=1, source_target_pairs={{0,2},{2,0},{1,3},{3,1},{4,6},{6,4},{5,7},{7,5},{8,10},{10,8},{9,1... | collective-permute-start | bytes 983048 | tf_op jit(solution)/shard_map/ppermute | solution.py:41
  54.1 7.2 %collective-permute-start.12 = (bf16[2,64,256]{2,1,0:T(8,128)(2,1)S(1)}, bf16[2,64,256]{2,1,0:T(8,128)(2,1)S(1)}, u32[]{:S(2)}, u32[]{:S(2)}) collective-permute-start(bf16[2,64,256]{2,1,0:T(8,128)(2,1)S(1)} %get-tuple-element.14), channel_id=1, source_target_pairs={{0,4},{4,0},{8,12},{12,8},{1,5},{5,1},{9,13},{13,9},{2,6},{6,2},{1... | collective-permute-start | bytes 196616 | tf_op jit(solution)/shard_map/ppermute | solution.py:268
  55.3 6.0 %collective-permute-start.13 = (bf16[2,64,256]{2,1,0:T(8,128)(2,1)S(1)}, bf16[2,64,256]{2,1,0:T(8,128)(2,1)S(1)}, u32[]{:S(2)}, u32[]{:S(2)}) collective-permute-start(bf16[2,64,256]{2,1,0:T(8,128)(2,1)S(1)} %get-tuple-element.15), channel_id=1, source_target_pairs={{0,8},{4,12},{8,0},{12,4},{1,9},{5,13},{9,1},{13,5},{2,10},{6,14},... | collective-permute-start | bytes 196616 | tf_op jit(solution)/shard_map/ppermute | solution.py:268
  55.3 6.0 %collective-permute-start.14 = (bf16[2,64,256]{2,1,0:T(8,128)(2,1)S(1)}, bf16[2,64,256]{2,1,0:T(8,128)(2,1)S(1)}, u32[]{:S(2)}, u32[]{:S(2)}) collective-permute-start(bf16[2,64,256]{2,1,0:T(8,128)(2,1)S(1)} %get-tuple-element.16), channel_id=1, source_target_pairs={{0,12},{4,8},{8,4},{12,0},{1,13},{5,9},{9,5},{13,1},{2,14},{6,10},... | collective-permute-start | bytes 196616 | tf_op jit(solution)/shard_map/ppermute | solution.py:268
  57.7 32.3 %all-to-all-start.1 = ((bf16[8,32,2048]{2,1,0:T(8,128)(2,1)}), bf16[8,32,2048]{2,1,0:T(8,128)(2,1)S(1)}, u32[]{:S(2)}, u32[]{:S(2)}) async-start(bf16[8,32,2048]{2,1,0:T(8,128)(2,1)} %bitcast.15), calls=%async_computation.1 | async-start | bytes 2097152 | tf_op jit(solution)/shard_map/all_to_all | solution.py:275
  61.4 5.0 %collective-permute-start.15 = (f32[2,64,256]{2,1,0:T(8,128)S(1)}, f32[2,64,256]{2,1,0:T(8,128)S(1)}, u32[]{:S(2)}, u32[]{:S(2)}) collective-permute-start(f32[2,64,256]{2,1,0:T(8,128)S(1)} %convert_add_fusion), channel_id=1, source_target_pairs={{0,1},{1,0},{2,3},{3,2},{4,5},{5,4},{6,7},{7,6},{8,9},{9,8},{10,11... | collective-permute-start | bytes 393224 | tf_op jit(solution)/shard_map/ppermute | solution.py:36
  62.0 4.6 %collective-permute-start.18 = (f32[2048]{0:T(1024)S(1)}, f32[2048]{0:T(1024)S(1)}, u32[]{:S(2)}, u32[]{:S(2)}) collective-permute-start(f32[2048]{0:T(1024)S(1)} %bitcast.45), channel_id=1, source_target_pairs={{0,2},{2,0},{1,3},{3,1},{4,6},{6,4},{5,7},{7,5},{8,10},{10,8},{9,1... | collective-permute-start | bytes 24584 | tf_op jit(solution)/shard_map/ppermute | solution.py:41
  66.5 1.3 %collective-permute-start.16 = (bf16[64,256]{1,0:T(8,128)(2,1)S(1)}, bf16[64,256]{1,0:T(8,128)(2,1)S(1)}, u32[]{:S(2)}, u32[]{:S(2)}) collective-permute-start(bf16[64,256]{1,0:T(8,128)(2,1)S(1)} %get-tuple-element.38), channel_id=1, source_target_pairs={{0,2},{2,0},{1,3},{3,1},{4,6},{6,4},{5,7},{7,5},{8,10},{10,8},{9,1... | collective-permute-start | bytes 98312 | tf_op jit(solution)/shard_map/ppermute | solution.py:41
  68.3 1.3 %collective-permute-start.17 = (bf16[4,2,8,512]{3,2,1,0:T(8,128)(2,1)S(1)}, bf16[4,2,8,512]{3,2,1,0:T(8,128)(2,1)S(1)}, u32[]{:S(2)}, u32[]{:S(2)}) collective-permute-start(bf16[4,2,8,512]{3,2,1,0:T(8,128)(2,1)S(1)} %dynamic-slice_bitcast_fusion), channel_id=1, source_target_pairs={{0,2},{2,0},{1,3},{3,1},{4,6},{6,4},{5,7},{7,5},{8,10},{10,8},{9,1... | collective-permute-start | bytes 196616 | tf_op jit(solution)/shard_map/ppermute | solution.py:41
  69.7 21.1 %collective-permute-start.19 = (bf16[48,512]{1,0:T(8,128)(2,1)S(1)}, bf16[48,512]{1,0:T(8,128)(2,1)S(1)}, u32[]{:S(2)}, u32[]{:S(2)}) collective-permute-start(bf16[48,512]{1,0:T(8,128)(2,1)S(1)} %get-tuple-element.32), channel_id=1, source_target_pairs={{2,18},{6,22},{10,26},{14,30},{18,2},{22,6},{26,10},{30,14},{3,19}... | collective-permute-start | bytes 147464 | tf_op jit(solution)/shard_map/ppermute | solution.py:320
  70.3 20.5 %collective-permute-start.21 = (bf16[48,512]{1,0:T(8,128)(2,1)S(1)}, bf16[48,512]{1,0:T(8,128)(2,1)S(1)}, u32[]{:S(2)}, u32[]{:S(2)}) collective-permute-start(bf16[48,512]{1,0:T(8,128)(2,1)S(1)} %get-tuple-element.34), channel_id=1, source_target_pairs={{0,8},{2,26},{4,12},{6,30},{8,0},{10,18},{12,4},{14,22},{16,24},{1... | collective-permute-start | bytes 147464 | tf_op jit(solution)/shard_map/ppermute | solution.py:320
  72.4 18.9 %collective-permute-start.22 = (bf16[48,512]{1,0:T(8,128)(2,1)S(1)}, bf16[48,512]{1,0:T(8,128)(2,1)S(1)}, u32[]{:S(2)}, u32[]{:S(2)}) collective-permute-start(bf16[48,512]{1,0:T(8,128)(2,1)S(1)} %get-tuple-element.31), channel_id=1, source_target_pairs={{0,12},{2,30},{4,8},{6,26},{8,4},{10,22},{12,0},{14,18},{16,28},{1... | collective-permute-start | bytes 147464 | tf_op jit(solution)/shard_map/ppermute | solution.py:320
  90.0 4.1 %collective-permute-start.20 = (bf16[48,512]{1,0:T(8,128)(2,1)S(1)}, bf16[48,512]{1,0:T(8,128)(2,1)S(1)}, u32[]{:S(2)}, u32[]{:S(2)}) collective-permute-start(bf16[48,512]{1,0:T(8,128)(2,1)S(1)} %get-tuple-element.19), channel_id=1, source_target_pairs={{0,4},{2,22},{4,0},{6,18},{8,12},{10,30},{12,8},{14,26},{16,20},{1... | collective-permute-start | bytes 147464 | tf_op jit(solution)/shard_map/ppermute | solution.py:320
  90.8 4.5 %collective-permute-start.23 = (bf16[48,512]{1,0:T(8,128)(2,1)S(1)}, bf16[48,512]{1,0:T(8,128)(2,1)S(1)}, u32[]{:S(2)}, u32[]{:S(2)}) collective-permute-start(bf16[48,512]{1,0:T(8,128)(2,1)S(1)} %broadcast_select_fusion.refs_0_), channel_id=1, source_target_pairs={{0,2},{2,0},{1,3},{3,1},{4,6},{6,4},{5,7},{7,5},{8,10},{10,8},{9,1... | collective-permute-start | bytes 147464 | tf_op jit(solution)/shard_map/ppermute | solution.py:41
  90.9 4.4 %collective-permute-start.25 = (bf16[48,512]{1,0:T(8,128)(2,1)S(1)}, bf16[48,512]{1,0:T(8,128)(2,1)S(1)}, u32[]{:S(2)}, u32[]{:S(2)}) collective-permute-start(bf16[48,512]{1,0:T(8,128)(2,1)S(1)} %collective-permute-done.21.refs_2_), channel_id=1, source_target_pairs={{0,2},{2,0},{1,3},{3,1},{4,6},{6,4},{5,7},{7,5},{8,10},{10,8},{9,1... | collective-permute-start | bytes 147464 | tf_op jit(solution)/shard_map/ppermute | solution.py:41
  91.4 3.9 %collective-permute-start.26 = (bf16[48,512]{1,0:T(8,128)(2,1)S(1)}, bf16[48,512]{1,0:T(8,128)(2,1)S(1)}, u32[]{:S(2)}, u32[]{:S(2)}) collective-permute-start(bf16[48,512]{1,0:T(8,128)(2,1)S(1)} %collective-permute-done.22.refs_3_), channel_id=1, source_target_pairs={{0,2},{2,0},{1,3},{3,1},{4,6},{6,4},{5,7},{7,5},{8,10},{10,8},{9,1... | collective-permute-start | bytes 147464 | tf_op jit(solution)/shard_map/ppermute | solution.py:41
  94.1 1.2 %collective-permute-start.24 = (bf16[48,512]{1,0:T(8,128)(2,1)S(1)}, bf16[48,512]{1,0:T(8,128)(2,1)S(1)}, u32[]{:S(2)}, u32[]{:S(2)}) collective-permute-start(bf16[48,512]{1,0:T(8,128)(2,1)S(1)} %collective-permute-done.20.refs_1_), channel_id=1, source_target_pairs={{0,2},{2,0},{1,3},{3,1},{4,6},{6,4},{5,7},{7,5},{8,10},{10,8},{9,1... | collective-permute-start | bytes 147464 | tf_op jit(solution)/shard_map/ppermute | solution.py:41

commit v7 on v6

--- a/solution.py
+++ b/solution.py
@@ -14,9 +14,9 @@
 DP = ("hi", "lo", "core")
 SWAP = [(0, 1), (1, 0)]
 FEW = 4
-PIN = 1
+PIN = 0
 LANES = 128
-CHUNK = 512
+CHUNK = 2048
 
 
 def iota2(shape, dim):

time: 96.4 us -> 94.4 us (0.979)
  waiting for transfers between devices: 52.5 us -> 50.3 us
    ppermute x4, waiting for transfers between devices: 2.68 us -> 0.01 us  [on_device(): pieces[step] = lax.ppermute(pieces[step], DP, pairs)]
    ppermute x11, starting transfers between devices: 0.97 us -> 2.32 us  [swap_core(): return lax.ppermute(value, 'core', SWAP)]
  transfers between devices with their start and end apart: 29 -> 29, of which waited for: 11 -> 9; matrix products, arithmetic and copies ran while one was open for 3% -> 3% of each run, Pallas kernels for 1% -> 1%
where the time goes in v7:
time: 94.4 us; the launch traced here: 94.1 us
  waiting for transfers between devices  50.3 us (53%)
  starting transfers between devices  32.1 us (34%)
  Pallas kernels  5.34 us (6%)
  other arithmetic  2.45 us (3%)
  between operations  1.65 us (2%)
  local copies, waits for them, and re-layouts  1.29 us (1%)
    ppermute x6, waiting for transfers between devices, swap_lo(): pieces.append(lax.ppermute(block(me ^ step), 'lo', pairs))  23 us
    all_to_all x1, waiting for transfers between devices, on_device(): lax.all_to_all(grad_part.reshape(halves * low, owned, part), ('hi', 'lo')...  16.8 us
    ppermute x6, starting transfers between devices, swap_lo(): pieces.append(lax.ppermute(block(me ^ step), 'lo', pairs))  7.11 us
    all_to_all x1, starting transfers between devices, on_device(): lax.all_to_all(cotangent[0], DP, split_axis=0, concat_axis=0, tiled=True)  5.94 us
    ppermute x2, waiting for transfers between devices, reduce_tensor(): return value + lax.ppermute(value, 'tensor', SWAP)  4.43 us
    ppermute x4, starting transfers between devices, on_device(): pieces[step] = lax.ppermute(pieces[step], DP, pairs)  4.27 us
    ppermute x11, waiting for transfers between devices, swap_core(): return lax.ppermute(value, 'core', SWAP)  3.84 us
    all_to_all x1, starting transfers between devices, on_device(): lax.all_to_all(grad_part.reshape(halves * low, owned, part), ('hi', 'lo')...  3.64 us
  transfers between devices with their start and end apart: 29, of which 9 were waited for; matrix products, arithmetic and copies ran while one was open for 3% of the time, Pallas kernels for 1%

profile of v7, /device:TPU:0, one launch (start us, length us, event | category | flops | bytes accessed | tf_op | source)
XLA Modules:
  0.0 94.1 jit_solution(5143117828304119750)
XLA Ops:
  0.7 1.6 %fusion = f32[64]{0:T(128)S(1)} fusion(bf16[64,8192]{1,0:T(8,128)(2,1)} %param.6), kind=kLoop, calls=%fused_computation.2 | loop fusion | flops 1572800 | bytes 1048832 | tf_op jit(solution)/shard_map/reduce_sum | solution.py:249
  2.3 3.0 %collective-permute-start = (f32[64]{0:T(128)S(1)}, f32[64]{0:T(128)S(1)}, u32[]{:S(2)}, u32[]{:S(2)}) collective-permute-start(f32[64]{0:T(128)S(1)} %fusion), channel_id=1, source_target_pairs={{0,1},{1,0},{2,3},{3,2},{4,5},{5,4},{6,7},{7,6},{8,9},{9,8},{10,11... | collective-permute-start | bytes 776 | tf_op jit(solution)/shard_map/ppermute | solution.py:36
  5.3 5.9 %all-to-all-start = ((bf16[16,8,512]{2,1,0:T(8,128)(2,1)}), bf16[16,8,512]{2,1,0:T(8,128)(2,1)S(1)}, u32[]{:S(2)}, u32[]{:S(2)}) async-start(bf16[16,8,512]{2,1,0:T(8,128)(2,1)} %bitcast.48), calls=%async_computation | async-start | bytes 262144 | tf_op jit(solution)/shard_map/all_to_all | solution.py:235
  11.3 1.1 %constant_dynamic-slice_fusion.3 = (bf16[32,2048]{1,0:T(8,128)(2,1)S(1)}, bf16[32,2048]{1,0:T(8,128)(2,1)S(1)}, bf16[32,2048]{1,0:T(8,128)(2,1)S(1)}, bf16[32,2048]{1,0:T(8,128)(2,1)S(1)}) fusion(bf16[32,8192]{1,0:T(8,128)(2,1)} %param.8, s32[]{:T(128)S(6)} %select_n.103, s32[]{:T(128)S(6)} %select_n.108, s32[]{:T(128)S(6)} %select_n.110, s32[]{:T(128)S(6)} %select_n.109), kind=kLoop, calls=%fused_computation.65 | loop fusion | bytes 1048592 | tf_op jit(solution)/shard_map/dynamic_slice | solution.py:230
  12.4 2.9 %collective-permute-start.10 = (bf16[32,2048]{1,0:T(8,128)(2,1)S(1)}, bf16[32,2048]{1,0:T(8,128)(2,1)S(1)}, u32[]{:S(2)}, u32[]{:S(2)}) collective-permute-start(bf16[32,2048]{1,0:T(8,128)(2,1)S(1)} %get-tuple-element.29), channel_id=1, source_target_pairs={{0,12},{4,8},{8,4},{12,0},{1,13},{5,9},{9,5},{13,1},{2,14},{6,10},... | collective-permute-start | bytes 393224 | tf_op jit(solution)/shard_map/ppermute | solution.py:50
  15.3 0.6 collective-permute-start.8
  15.8 0.2 collective-permute-start.9
  16.7 0.2 convert_reduce_fusion
  16.9 0.0 collective-permute-done
  16.9 0.4 fusion.3
  17.3 0.1 constant_dynamic-slice_fusion.4
  17.4 2.3 %all-to-all-done = bf16[16,8,512]{2,1,0:T(8,128)(2,1)S(1)} async-done(((bf16[16,8,512]{2,1,0:T(8,128)(2,1)}), bf16[16,8,512]{2,1,0:T(8,128)(2,1)S(1)}, u32[]{:S(2)}, u32[]{:S(2)}) %all-to-all-start) | async-done | bytes 131104 | tf_op jit(solution)/shard_map/all_to_all | solution.py:235
  19.7 0.4 convolution_convert_fusion.2
  20.1 0.1 pad_maximum_fusion
  20.2 0.1 collective-permute-start.1
  20.3 1.0 %collective-permute-start.2 = (bf16[64,2560]{1,0:T(8,128)(2,1)S(1)}, bf16[64,2560]{1,0:T(8,128)(2,1)S(1)}, u32[]{:S(2)}, u32[]{:S(2)}) collective-permute-start(bf16[64,2560]{1,0:T(8,128)(2,1)S(1)} %get-tuple-element.41), channel_id=1, source_target_pairs={{0,8},{4,12},{8,0},{12,4},{1,9},{5,13},{9,1},{13,5},{2,10},{6,14},... | collective-permute-start | bytes 983048 | tf_op jit(solution)/shard_map/ppermute | solution.py:50
  21.3 0.0 collective-permute-done.10
  21.3 2.5 %collective-permute-start.3 = (bf16[64,2560]{1,0:T(8,128)(2,1)S(1)}, bf16[64,2560]{1,0:T(8,128)(2,1)S(1)}, u32[]{:S(2)}, u32[]{:S(2)}) collective-permute-start(bf16[64,2560]{1,0:T(8,128)(2,1)S(1)} %get-tuple-element.39), channel_id=1, source_target_pairs={{0,12},{4,8},{8,4},{12,0},{1,13},{5,9},{9,5},{13,1},{2,14},{6,10},... | collective-permute-start | bytes 983048 | tf_op jit(solution)/shard_map/ppermute | solution.py:50
  23.8 0.0 collective-permute-done.8
  23.8 0.0 collective-permute-done.9
  23.8 1.7 %collective-permute-start.11 = (bf16[128,2048]{1,0:T(8,128)(2,1)S(1)}, bf16[128,2048]{1,0:T(8,128)(2,1)S(1)}, u32[]{:S(2)}, u32[]{:S(2)}) collective-permute-start(bf16[128,2048]{1,0:T(8,128)(2,1)S(1)} %pad_maximum_fusion.4.refs_8_), channel_id=1, source_target_pairs={{0,16},{16,0},{1,17},{17,1},{2,18},{18,2},{3,19},{19,3},{4,20},{20... | collective-permute-start | bytes 1572872 | tf_op jit(solution)/shard_map/ppermute | solution.py:233
  25.5 0.0 collective-permute-start.4
  25.5 4.5 %collective-permute-done.1.refs_1_ = bf16[64,2560]{1,0:T(8,128)(2,1)S(1)} collective-permute-done((bf16[64,2560]{1,0:T(8,128)(2,1)S(1)}, bf16[64,2560]{1,0:T(8,128)(2,1)S(1)}, u32[]{:S(2)}, u32[]{:S(2)}) %collective-permute-start.1) | collective-permute-done | bytes 327712 | tf_op jit(solution)/shard_map/ppermute | solution.py:50
  30.0 0.0 collective-permute-start.5
  30.0 12.3 %collective-permute-done.2.refs_2_ = bf16[64,2560]{1,0:T(8,128)(2,1)S(1)} collective-permute-done((bf16[64,2560]{1,0:T(8,128)(2,1)S(1)}, bf16[64,2560]{1,0:T(8,128)(2,1)S(1)}, u32[]{:S(2)}, u32[]{:S(2)}) %collective-permute-start.2) | collective-permute-done | bytes 327712 | tf_op jit(solution)/shard_map/ppermute | solution.py:50
  42.2 0.0 collective-permute-start.6
  42.2 6.2 %collective-permute-done.3.refs_3_ = bf16[64,2560]{1,0:T(8,128)(2,1)S(1)} collective-permute-done((bf16[64,2560]{1,0:T(8,128)(2,1)S(1)}, bf16[64,2560]{1,0:T(8,128)(2,1)S(1)}, u32[]{:S(2)}, u32[]{:S(2)}) %collective-permute-start.3) | collective-permute-done | bytes 327712 | tf_op jit(solution)/shard_map/ppermute | solution.py:50
  48.5 0.0 collective-permute-start.7
  48.5 0.0 collective-permute-done.4.refs_4_
  48.5 0.0 collective-permute-done.11.refs_9_
  48.5 0.0 collective-permute-done.5.refs_5_
  48.5 1.6 %collective-permute-done.7.refs_7_ = bf16[64,2560]{1,0:T(8,128)(2,1)S(1)} collective-permute-done((bf16[64,2560]{1,0:T(8,128)(2,1)S(1)}, bf16[64,2560]{1,0:T(8,128)(2,1)S(1)}, u32[]{:S(2)}, u32[]{:S(2)}) %collective-permute-start.7) | collective-permute-done | bytes 327712 | tf_op jit(solution)/shard_map/ppermute | solution.py:41
  50.1 3.5 %shard_map.85 = (bf16[256,2048]{1,0:T(8,128)(2,1)}, f32[1,2048]{1,0:T(1,128)S(1)}, bf16[2,64,256]{2,1,0:T(8,128)(2,1)S(1)}, bf16[2,64,256]{2,1,0:T(8,128)(2,1)S(...) custom-call(bf16[64,2560]{1,0:T(8,128)(2,1)S(1)} %get-tuple-element.42.refs_0_, ...), custom_call_target="tpu_custom_call" | custom-call | flops 1073741824 | bytes 6815744 | tf_op jit(solution)/shard_map/pallas_call | solution.py:131
  53.6 1.2 %collective-permute-start.12 = (bf16[2,64,256]{2,1,0:T(8,128)(2,1)S(1)}, bf16[2,64,256]{2,1,0:T(8,128)(2,1)S(1)}, u32[]{:S(2)}, u32[]{:S(2)}) collective-permute-start(bf16[2,64,256]{2,1,0:T(8,128)(2,1)S(1)} %get-tuple-element.14), channel_id=1, source_target_pairs={{0,4},{4,0},{8,12},{12,8},{1,5},{5,1},{9,13},{13,9},{2,6},{6,2},{1... | collective-permute-start | bytes 196616 | tf_op jit(solution)/shard_map/ppermute | solution.py:268
  54.8 0.0 collective-permute-start.13
  54.8 2.4 %collective-permute-start.14 = (bf16[2,64,256]{2,1,0:T(8,128)(2,1)S(1)}, bf16[2,64,256]{2,1,0:T(8,128)(2,1)S(1)}, u32[]{:S(2)}, u32[]{:S(2)}) collective-permute-start(bf16[2,64,256]{2,1,0:T(8,128)(2,1)S(1)} %get-tuple-element.16), channel_id=1, source_target_pairs={{0,12},{4,8},{8,4},{12,0},{1,13},{5,9},{9,5},{13,1},{2,14},{6,10},... | collective-permute-start | bytes 196616 | tf_op jit(solution)/shard_map/ppermute | solution.py:268
  57.2 3.6 %all-to-all-start.1 = ((bf16[8,32,2048]{2,1,0:T(8,128)(2,1)}), bf16[8,32,2048]{2,1,0:T(8,128)(2,1)S(1)}, u32[]{:S(2)}, u32[]{:S(2)}) async-start(bf16[8,32,2048]{2,1,0:T(8,128)(2,1)} %bitcast.14), calls=%async_computation.1 | async-start | bytes 2097152 | tf_op jit(solution)/shard_map/all_to_all | solution.py:275
  60.8 0.0 collective-permute-done.13
  60.9 0.6 collective-permute-start.15
  61.5 0.0 collective-permute-start.18
  61.5 4.4 %collective-permute-done.15 = f32[2,64,256]{2,1,0:T(8,128)S(1)} collective-permute-done((f32[2,64,256]{2,1,0:T(8,128)S(1)}, f32[2,64,256]{2,1,0:T(8,128)S(1)}, u32[]{:S(2)}, u32[]{:S(2)}) %collective-permute-start.15) | collective-permute-done | bytes 131104 | tf_op jit(solution)/shard_map/ppermute | solution.py:36
  66.0 0.1 collective-permute-start.16
  66.0 0.0 collective-permute-done.18
  66.1 1.2 %collective-permute-done.16 = bf16[64,256]{1,0:T(8,128)(2,1)S(1)} collective-permute-done((bf16[64,256]{1,0:T(8,128)(2,1)S(1)}, bf16[64,256]{1,0:T(8,128)(2,1)S(1)}, u32[]{:S(2)}, u32[]{:S(2)}) %collective-permute-start.16) | collective-permute-done | bytes 32800 | tf_op jit(solution)/shard_map/ppermute | solution.py:41
  67.2 0.5 convolution_convert_fusion
  67.7 0.2 collective-permute-start.17
  68.0 1.1 %collective-permute-done.17 = bf16[4,2,8,512]{3,2,1,0:T(8,128)(2,1)S(1)} collective-permute-done((bf16[4,2,8,512]{3,2,1,0:T(8,128)(2,1)S(1)}, bf16[4,2,8,512]{3,2,1,0:T(8,128)(2,1)S(1)}, u32[]{:S(2)}, u32[]{:S(2)}) %collective-permute-start.17) | collective-permute-done | bytes 65568 | tf_op jit(solution)/shard_map/ppermute | solution.py:41
  69.1 2.1 %collective-permute-start.20 = (bf16[48,512]{1,0:T(8,128)(2,1)S(1)}, bf16[48,512]{1,0:T(8,128)(2,1)S(1)}, u32[]{:S(2)}, u32[]{:S(2)}) collective-permute-start(bf16[48,512]{1,0:T(8,128)(2,1)S(1)} %get-tuple-element.33), channel_id=1, source_target_pairs={{0,4},{2,22},{4,0},{6,18},{8,12},{10,30},{12,8},{14,26},{16,20},{1... | collective-permute-start | bytes 147464 | tf_op jit(solution)/shard_map/ppermute | solution.py:320
  71.2 1.5 %collective-permute-start.21 = (bf16[48,512]{1,0:T(8,128)(2,1)S(1)}, bf16[48,512]{1,0:T(8,128)(2,1)S(1)}, u32[]{:S(2)}, u32[]{:S(2)}) collective-permute-start(bf16[48,512]{1,0:T(8,128)(2,1)S(1)} %get-tuple-element.34), channel_id=1, source_target_pairs={{0,8},{2,26},{4,12},{6,30},{8,0},{10,18},{12,4},{14,22},{16,24},{1... | collective-permute-start | bytes 147464 | tf_op jit(solution)/shard_map/ppermute | solution.py:320
  72.7 0.1 collective-permute-start.22
  72.8 16.8 %all-to-all-done.1 = bf16[8,32,2048]{2,1,0:T(8,128)(2,1)S(1)} async-done(((bf16[8,32,2048]{2,1,0:T(8,128)(2,1)}), bf16[8,32,2048]{2,1,0:T(8,128)(2,1)S(1)}, u32[]{:S(2)}, u32[]{:S(2)}) %all-to-all-start.1) | async-done | bytes 1048608 | tf_op jit(solution)/shard_map/all_to_all | solution.py:275
  89.5 0.7 collective-permute-start.19
  90.2 0.0 collective-permute-done.20.refs_1_
  90.2 0.1 collective-permute-start.24
  90.3 0.0 collective-permute-done.21.refs_2_
  90.3 0.5 collective-permute-start.25
  90.8 0.1 collective-permute-start.26
  90.8 0.0 collective-permute-done.19
  90.9 1.4 %collective-permute-start.23 = (bf16[48,512]{1,0:T(8,128)(2,1)S(1)}, bf16[48,512]{1,0:T(8,128)(2,1)S(1)}, u32[]{:S(2)}, u32[]{:S(2)}) collective-permute-start(bf16[48,512]{1,0:T(8,128)(2,1)S(1)} %broadcast_select_fusion.refs_0_), channel_id=1, source_target_pairs={{0,2},{2,0},{1,3},{3,1},{4,6},{6,4},{5,7},{7,5},{8,10},{10,8},{9,1... | collective-permute-start | bytes 147464 | tf_op jit(solution)/shard_map/ppermute | solution.py:41
  92.2 1.1 %shard_map.87 = f32[32,8192]{1,0:T(8,128)} custom-call(bf16[2,4,32,2048]{3,2,1,0:T(8,128)(2,1)S(1)} %bitcast.43), custom_call_target="tpu_custom_call" | custom-call | flops 1048576 | bytes 2097152 | tf_op jit(solution)/shard_map/pallas_call | solution.py:168
  93.3 0.0 collective-permute-done.24.refs_5_
  93.3 0.0 collective-permute-done.25.refs_6_
  93.3 0.0 collective-permute-done.23.refs_4_
  93.3 0.7 shard_map.86
  (28 shorter events, 0.3 us)
Async XLA Ops:
  0.6 16.2 %copy-start.1 = (bf16[64,8192]{1,0:T(8,128)(2,1)S(1)}, bf16[64,8192]{1,0:T(8,128)(2,1)}, u32[]{:S(2)}) copy-start(bf16[64,8192]{1,0:T(8,128)(2,1)} %param.6) | copy-start | bytes 3145732
  0.6 16.0 %copy-start.2 = (s32[64]{0:T(128)S(1)}, s32[64]{0:T(128)}, u32[]{:S(2)}) copy-start(s32[64]{0:T(128)} %param.11) | copy-start | bytes 772
  0.7 16.2 %copy-start = (f32[8192]{0:T(1024)S(1)}, f32[8192]{0:T(1024)}, u32[]{:S(2)}) copy-start(f32[8192]{0:T(1024)} %param.7) | copy-start | bytes 98308
  2.3 14.6 %collective-permute-start = (f32[64]{0:T(128)S(1)}, f32[64]{0:T(128)S(1)}, u32[]{:S(2)}, u32[]{:S(2)}) collective-permute-start(f32[64]{0:T(128)S(1)} %fusion), channel_id=1, source_target_pairs={{0,1},{1,0},{2,3},{3,2},{4,5},{5,4},{6,7},{7,6},{8,9},{9,8},{10,11... | collective-permute-start | bytes 776 | tf_op jit(solution)/shard_map/ppermute | solution.py:36
  5.3 14.4 %all-to-all-start = ((bf16[16,8,512]{2,1,0:T(8,128)(2,1)}), bf16[16,8,512]{2,1,0:T(8,128)(2,1)S(1)}, u32[]{:S(2)}, u32[]{:S(2)}) async-start(bf16[16,8,512]{2,1,0:T(8,128)(2,1)} %bitcast.48), calls=%async_computation | async-start | bytes 262144 | tf_op jit(solution)/shard_map/all_to_all | solution.py:235
  12.4 8.9 %collective-permute-start.10 = (bf16[32,2048]{1,0:T(8,128)(2,1)S(1)}, bf16[32,2048]{1,0:T(8,128)(2,1)S(1)}, u32[]{:S(2)}, u32[]{:S(2)}) collective-permute-start(bf16[32,2048]{1,0:T(8,128)(2,1)S(1)} %get-tuple-element.29), channel_id=1, source_target_pairs={{0,12},{4,8},{8,4},{12,0},{1,13},{5,9},{9,5},{13,1},{2,14},{6,10},... | collective-permute-start | bytes 393224 | tf_op jit(solution)/shard_map/ppermute | solution.py:50
  15.3 8.5 %collective-permute-start.8 = (bf16[32,2048]{1,0:T(8,128)(2,1)S(1)}, bf16[32,2048]{1,0:T(8,128)(2,1)S(1)}, u32[]{:S(2)}, u32[]{:S(2)}) collective-permute-start(bf16[32,2048]{1,0:T(8,128)(2,1)S(1)} %get-tuple-element.28), channel_id=1, source_target_pairs={{0,4},{4,0},{8,12},{12,8},{1,5},{5,1},{9,13},{13,9},{2,6},{6,2},{1... | collective-permute-start | bytes 393224 | tf_op jit(solution)/shard_map/ppermute | solution.py:50
  15.8 8.0 %collective-permute-start.9 = (bf16[32,2048]{1,0:T(8,128)(2,1)S(1)}, bf16[32,2048]{1,0:T(8,128)(2,1)S(1)}, u32[]{:S(2)}, u32[]{:S(2)}) collective-permute-start(bf16[32,2048]{1,0:T(8,128)(2,1)S(1)} %get-tuple-element.30), channel_id=1, source_target_pairs={{0,8},{4,12},{8,0},{12,4},{1,9},{5,13},{9,1},{13,5},{2,10},{6,14},... | collective-permute-start | bytes 393224 | tf_op jit(solution)/shard_map/ppermute | solution.py:50
  20.2 9.8 %collective-permute-start.1 = (bf16[64,2560]{1,0:T(8,128)(2,1)S(1)}, bf16[64,2560]{1,0:T(8,128)(2,1)S(1)}, u32[]{:S(2)}, u32[]{:S(2)}) collective-permute-start(bf16[64,2560]{1,0:T(8,128)(2,1)S(1)} %get-tuple-element.40), channel_id=1, source_target_pairs={{0,4},{4,0},{8,12},{12,8},{1,5},{5,1},{9,13},{13,9},{2,6},{6,2},{1... | collective-permute-start | bytes 983048 | tf_op jit(solution)/shard_map/ppermute | solution.py:50
  20.3 21.9 %collective-permute-start.2 = (bf16[64,2560]{1,0:T(8,128)(2,1)S(1)}, bf16[64,2560]{1,0:T(8,128)(2,1)S(1)}, u32[]{:S(2)}, u32[]{:S(2)}) collective-permute-start(bf16[64,2560]{1,0:T(8,128)(2,1)S(1)} %get-tuple-element.41), channel_id=1, source_target_pairs={{0,8},{4,12},{8,0},{12,4},{1,9},{5,13},{9,1},{13,5},{2,10},{6,14},... | collective-permute-start | bytes 983048 | tf_op jit(solution)/shard_map/ppermute | solution.py:50
  21.3 27.2 %collective-permute-start.3 = (bf16[64,2560]{1,0:T(8,128)(2,1)S(1)}, bf16[64,2560]{1,0:T(8,128)(2,1)S(1)}, u32[]{:S(2)}, u32[]{:S(2)}) collective-permute-start(bf16[64,2560]{1,0:T(8,128)(2,1)S(1)} %get-tuple-element.39), channel_id=1, source_target_pairs={{0,12},{4,8},{8,4},{12,0},{1,13},{5,9},{9,5},{13,1},{2,14},{6,10},... | collective-permute-start | bytes 983048 | tf_op jit(solution)/shard_map/ppermute | solution.py:50
  23.8 24.6 %collective-permute-start.11 = (bf16[128,2048]{1,0:T(8,128)(2,1)S(1)}, bf16[128,2048]{1,0:T(8,128)(2,1)S(1)}, u32[]{:S(2)}, u32[]{:S(2)}) collective-permute-start(bf16[128,2048]{1,0:T(8,128)(2,1)S(1)} %pad_maximum_fusion.4.refs_8_), channel_id=1, source_target_pairs={{0,16},{16,0},{1,17},{17,1},{2,18},{18,2},{3,19},{19,3},{4,20},{20... | collective-permute-start | bytes 1572872 | tf_op jit(solution)/shard_map/ppermute | solution.py:233
  25.5 23.0 %collective-permute-start.4 = (bf16[64,2560]{1,0:T(8,128)(2,1)S(1)}, bf16[64,2560]{1,0:T(8,128)(2,1)S(1)}, u32[]{:S(2)}, u32[]{:S(2)}) collective-permute-start(bf16[64,2560]{1,0:T(8,128)(2,1)S(1)} %get-tuple-element.42.refs_0_), channel_id=1, source_target_pairs={{0,2},{2,0},{1,3},{3,1},{4,6},{6,4},{5,7},{7,5},{8,10},{10,8},{9,1... | collective-permute-start | bytes 983048 | tf_op jit(solution)/shard_map/ppermute | solution.py:41
  30.0 18.5 %collective-permute-start.5 = (bf16[64,2560]{1,0:T(8,128)(2,1)S(1)}, bf16[64,2560]{1,0:T(8,128)(2,1)S(1)}, u32[]{:S(2)}, u32[]{:S(2)}) collective-permute-start(bf16[64,2560]{1,0:T(8,128)(2,1)S(1)} %collective-permute-done.1.refs_1_), channel_id=1, source_target_pairs={{0,2},{2,0},{1,3},{3,1},{4,6},{6,4},{5,7},{7,5},{8,10},{10,8},{9,1... | collective-permute-start | bytes 983048 | tf_op jit(solution)/shard_map/ppermute | solution.py:41
  42.2 6.2 %collective-permute-start.6 = (bf16[64,2560]{1,0:T(8,128)(2,1)S(1)}, bf16[64,2560]{1,0:T(8,128)(2,1)S(1)}, u32[]{:S(2)}, u32[]{:S(2)}) collective-permute-start(bf16[64,2560]{1,0:T(8,128)(2,1)S(1)} %collective-permute-done.2.refs_2_), channel_id=1, source_target_pairs={{0,2},{2,0},{1,3},{3,1},{4,6},{6,4},{5,7},{7,5},{8,10},{10,8},{9,1... | collective-permute-start | bytes 983048 | tf_op jit(solution)/shard_map/ppermute | solution.py:41
  48.5 1.6 %collective-permute-start.7 = (bf16[64,2560]{1,0:T(8,128)(2,1)S(1)}, bf16[64,2560]{1,0:T(8,128)(2,1)S(1)}, u32[]{:S(2)}, u32[]{:S(2)}) collective-permute-start(bf16[64,2560]{1,0:T(8,128)(2,1)S(1)} %collective-permute-done.3.refs_3_), channel_id=1, source_target_pairs={{0,2},{2,0},{1,3},{3,1},{4,6},{6,4},{5,7},{7,5},{8,10},{10,8},{9,1... | collective-permute-start | bytes 983048 | tf_op jit(solution)/shard_map/ppermute | solution.py:41
  53.6 7.2 %collective-permute-start.12 = (bf16[2,64,256]{2,1,0:T(8,128)(2,1)S(1)}, bf16[2,64,256]{2,1,0:T(8,128)(2,1)S(1)}, u32[]{:S(2)}, u32[]{:S(2)}) collective-permute-start(bf16[2,64,256]{2,1,0:T(8,128)(2,1)S(1)} %get-tuple-element.14), channel_id=1, source_target_pairs={{0,4},{4,0},{8,12},{12,8},{1,5},{5,1},{9,13},{13,9},{2,6},{6,2},{1... | collective-permute-start | bytes 196616 | tf_op jit(solution)/shard_map/ppermute | solution.py:268
  54.8 6.0 %collective-permute-start.13 = (bf16[2,64,256]{2,1,0:T(8,128)(2,1)S(1)}, bf16[2,64,256]{2,1,0:T(8,128)(2,1)S(1)}, u32[]{:S(2)}, u32[]{:S(2)}) collective-permute-start(bf16[2,64,256]{2,1,0:T(8,128)(2,1)S(1)} %get-tuple-element.15), channel_id=1, source_target_pairs={{0,8},{4,12},{8,0},{12,4},{1,9},{5,13},{9,1},{13,5},{2,10},{6,14},... | collective-permute-start | bytes 196616 | tf_op jit(solution)/shard_map/ppermute | solution.py:268
  54.8 6.0 %collective-permute-start.14 = (bf16[2,64,256]{2,1,0:T(8,128)(2,1)S(1)}, bf16[2,64,256]{2,1,0:T(8,128)(2,1)S(1)}, u32[]{:S(2)}, u32[]{:S(2)}) collective-permute-start(bf16[2,64,256]{2,1,0:T(8,128)(2,1)S(1)} %get-tuple-element.16), channel_id=1, source_target_pairs={{0,12},{4,8},{8,4},{12,0},{1,13},{5,9},{9,5},{13,1},{2,14},{6,10},... | collective-permute-start | bytes 196616 | tf_op jit(solution)/shard_map/ppermute | solution.py:268
  57.2 32.3 %all-to-all-start.1 = ((bf16[8,32,2048]{2,1,0:T(8,128)(2,1)}), bf16[8,32,2048]{2,1,0:T(8,128)(2,1)S(1)}, u32[]{:S(2)}, u32[]{:S(2)}) async-start(bf16[8,32,2048]{2,1,0:T(8,128)(2,1)} %bitcast.14), calls=%async_computation.1 | async-start | bytes 2097152 | tf_op jit(solution)/shard_map/all_to_all | solution.py:275
  60.9 5.0 %collective-permute-start.15 = (f32[2,64,256]{2,1,0:T(8,128)S(1)}, f32[2,64,256]{2,1,0:T(8,128)S(1)}, u32[]{:S(2)}, u32[]{:S(2)}) collective-permute-start(f32[2,64,256]{2,1,0:T(8,128)S(1)} %convert_add_fusion), channel_id=1, source_target_pairs={{0,1},{1,0},{2,3},{3,2},{4,5},{5,4},{6,7},{7,6},{8,9},{9,8},{10,11... | collective-permute-start | bytes 393224 | tf_op jit(solution)/shard_map/ppermute | solution.py:36
  61.5 4.5 %collective-permute-start.18 = (f32[2048]{0:T(1024)S(1)}, f32[2048]{0:T(1024)S(1)}, u32[]{:S(2)}, u32[]{:S(2)}) collective-permute-start(f32[2048]{0:T(1024)S(1)} %bitcast.45), channel_id=1, source_target_pairs={{0,2},{2,0},{1,3},{3,1},{4,6},{6,4},{5,7},{7,5},{8,10},{10,8},{9,1... | collective-permute-start | bytes 24584 | tf_op jit(solution)/shard_map/ppermute | solution.py:41
  66.0 1.3 %collective-permute-start.16 = (bf16[64,256]{1,0:T(8,128)(2,1)S(1)}, bf16[64,256]{1,0:T(8,128)(2,1)S(1)}, u32[]{:S(2)}, u32[]{:S(2)}) collective-permute-start(bf16[64,256]{1,0:T(8,128)(2,1)S(1)} %get-tuple-element.38), channel_id=1, source_target_pairs={{0,2},{2,0},{1,3},{3,1},{4,6},{6,4},{5,7},{7,5},{8,10},{10,8},{9,1... | collective-permute-start | bytes 98312 | tf_op jit(solution)/shard_map/ppermute | solution.py:41
  67.7 1.3 %collective-permute-start.17 = (bf16[4,2,8,512]{3,2,1,0:T(8,128)(2,1)S(1)}, bf16[4,2,8,512]{3,2,1,0:T(8,128)(2,1)S(1)}, u32[]{:S(2)}, u32[]{:S(2)}) collective-permute-start(bf16[4,2,8,512]{3,2,1,0:T(8,128)(2,1)S(1)} %dynamic-slice_bitcast_fusion), channel_id=1, source_target_pairs={{0,2},{2,0},{1,3},{3,1},{4,6},{6,4},{5,7},{7,5},{8,10},{10,8},{9,1... | collective-permute-start | bytes 196616 | tf_op jit(solution)/shard_map/ppermute | solution.py:41
  69.1 21.0 %collective-permute-start.20 = (bf16[48,512]{1,0:T(8,128)(2,1)S(1)}, bf16[48,512]{1,0:T(8,128)(2,1)S(1)}, u32[]{:S(2)}, u32[]{:S(2)}) collective-permute-start(bf16[48,512]{1,0:T(8,128)(2,1)S(1)} %get-tuple-element.33), channel_id=1, source_target_pairs={{0,4},{2,22},{4,0},{6,18},{8,12},{10,30},{12,8},{14,26},{16,20},{1... | collective-permute-start | bytes 147464 | tf_op jit(solution)/shard_map/ppermute | solution.py:320
  71.2 19.0 %collective-permute-start.21 = (bf16[48,512]{1,0:T(8,128)(2,1)S(1)}, bf16[48,512]{1,0:T(8,128)(2,1)S(1)}, u32[]{:S(2)}, u32[]{:S(2)}) collective-permute-start(bf16[48,512]{1,0:T(8,128)(2,1)S(1)} %get-tuple-element.34), channel_id=1, source_target_pairs={{0,8},{2,26},{4,12},{6,30},{8,0},{10,18},{12,4},{14,22},{16,24},{1... | collective-permute-start | bytes 147464 | tf_op jit(solution)/shard_map/ppermute | solution.py:320
  72.7 18.1 %collective-permute-start.22 = (bf16[48,512]{1,0:T(8,128)(2,1)S(1)}, bf16[48,512]{1,0:T(8,128)(2,1)S(1)}, u32[]{:S(2)}, u32[]{:S(2)}) collective-permute-start(bf16[48,512]{1,0:T(8,128)(2,1)S(1)} %get-tuple-element.31), channel_id=1, source_target_pairs={{0,12},{2,30},{4,8},{6,26},{8,4},{10,22},{12,0},{14,18},{16,28},{1... | collective-permute-start | bytes 147464 | tf_op jit(solution)/shard_map/ppermute | solution.py:320
  89.5 1.3 %collective-permute-start.19 = (bf16[48,512]{1,0:T(8,128)(2,1)S(1)}, bf16[48,512]{1,0:T(8,128)(2,1)S(1)}, u32[]{:S(2)}, u32[]{:S(2)}) collective-permute-start(bf16[48,512]{1,0:T(8,128)(2,1)S(1)} %get-tuple-element.19), channel_id=1, source_target_pairs={{2,18},{6,22},{10,26},{14,30},{18,2},{22,6},{26,10},{30,14},{3,19}... | collective-permute-start | bytes 147464 | tf_op jit(solution)/shard_map/ppermute | solution.py:320
  90.2 3.2 %collective-permute-start.24 = (bf16[48,512]{1,0:T(8,128)(2,1)S(1)}, bf16[48,512]{1,0:T(8,128)(2,1)S(1)}, u32[]{:S(2)}, u32[]{:S(2)}) collective-permute-start(bf16[48,512]{1,0:T(8,128)(2,1)S(1)} %collective-permute-done.20.refs_1_), channel_id=1, source_target_pairs={{0,2},{2,0},{1,3},{3,1},{4,6},{6,4},{5,7},{7,5},{8,10},{10,8},{9,1... | collective-permute-start | bytes 147464 | tf_op jit(solution)/shard_map/ppermute | solution.py:41
  90.3 3.1 %collective-permute-start.25 = (bf16[48,512]{1,0:T(8,128)(2,1)S(1)}, bf16[48,512]{1,0:T(8,128)(2,1)S(1)}, u32[]{:S(2)}, u32[]{:S(2)}) collective-permute-start(bf16[48,512]{1,0:T(8,128)(2,1)S(1)} %collective-permute-done.21.refs_2_), channel_id=1, source_target_pairs={{0,2},{2,0},{1,3},{3,1},{4,6},{6,4},{5,7},{7,5},{8,10},{10,8},{9,1... | collective-permute-start | bytes 147464 | tf_op jit(solution)/shard_map/ppermute | solution.py:41
  90.8 2.6 %collective-permute-start.26 = (bf16[48,512]{1,0:T(8,128)(2,1)S(1)}, bf16[48,512]{1,0:T(8,128)(2,1)S(1)}, u32[]{:S(2)}, u32[]{:S(2)}) collective-permute-start(bf16[48,512]{1,0:T(8,128)(2,1)S(1)} %collective-permute-done.22.refs_3_), channel_id=1, source_target_pairs={{0,2},{2,0},{1,3},{3,1},{4,6},{6,4},{5,7},{7,5},{8,10},{10,8},{9,1... | collective-permute-start | bytes 147464 | tf_op jit(solution)/shard_map/ppermute | solution.py:41
  90.9 2.5 %collective-permute-start.23 = (bf16[48,512]{1,0:T(8,128)(2,1)S(1)}, bf16[48,512]{1,0:T(8,128)(2,1)S(1)}, u32[]{:S(2)}, u32[]{:S(2)}) collective-permute-start(bf16[48,512]{1,0:T(8,128)(2,1)S(1)} %broadcast_select_fusion.refs_0_), channel_id=1, source_target_pairs={{0,2},{2,0},{1,3},{3,1},{4,6},{6,4},{5,7},{7,5},{8,10},{10,8},{9,1... | collective-permute-start | bytes 147464 | tf_op jit(solution)/shard_map/ppermute | solution.py:41

commit v8 on v7

--- a/solution.py
+++ b/solution.py
@@ -147,7 +147,7 @@
             pltpu.SemaphoreType.DMA((2 * pieces,)),
             pltpu.SemaphoreType.DMA((2 * pieces,)),
         ],
-        compiler_params=pltpu.CompilerParams(vmem_limit_bytes=16 * 1024 * 1024),
+        compiler_params=pltpu.CompilerParams(vmem_limit_bytes=24 * 1024 * 1024),
         cost_estimate=pl.CostEstimate(
             flops=4 * total * core_keys * part,
             bytes_accessed=2 * total * columns + 8 * core_keys * part,
@@ -170,7 +170,7 @@
         out_shape=jax.ShapeDtypeStruct((owned, low * part), jnp.float32),
         in_specs=[pl.BlockSpec(memory_space=pltpu.VMEM)],
         out_specs=pl.BlockSpec(memory_space=pltpu.VMEM),
-        compiler_params=pltpu.CompilerParams(vmem_limit_bytes=8 * 1024 * 1024),
+        compiler_params=pltpu.CompilerParams(vmem_limit_bytes=4 * 1024 * 1024),
         cost_estimate=pl.CostEstimate(
             flops=2 * terms.size, bytes_accessed=4 * terms.size, transcendentals=0
         ),

time: 94.4 us -> 94.4 us (level)
  no operation moved by 1% of the time
where the time goes in v8:
time: 94.4 us; the launch traced here: 94.1 us
  waiting for transfers between devices  50.3 us (53%)
  starting transfers between devices  32.1 us (34%)
  Pallas kernels  5.34 us (6%)
  other arithmetic  2.45 us (3%)
  between operations  1.65 us (2%)
  local copies, waits for them, and re-layouts  1.29 us (1%)
    ppermute x6, waiting for transfers between devices, swap_lo(): pieces.append(lax.ppermute(block(me ^ step), 'lo', pairs))  23 us
    all_to_all x1, waiting for transfers between devices, on_device(): lax.all_to_all(grad_part.reshape(halves * low, owned, part), ('hi', 'lo')...  16.8 us
    ppermute x6, starting transfers between devices, swap_lo(): pieces.append(lax.ppermute(block(me ^ step), 'lo', pairs))  7.11 us
    all_to_all x1, starting transfers between devices, on_device(): lax.all_to_all(cotangent[0], DP, split_axis=0, concat_axis=0, tiled=True)  5.94 us
    ppermute x2, waiting for transfers between devices, reduce_tensor(): return value + lax.ppermute(value, 'tensor', SWAP)  4.43 us
    ppermute x4, starting transfers between devices, on_device(): pieces[step] = lax.ppermute(pieces[step], DP, pairs)  4.27 us
    ppermute x11, waiting for transfers between devices, swap_core(): return lax.ppermute(value, 'core', SWAP)  3.84 us
    all_to_all x1, starting transfers between devices, on_device(): lax.all_to_all(grad_part.reshape(halves * low, owned, part), ('hi', 'lo')...  3.64 us
  transfers between devices with their start and end apart: 29, of which 9 were waited for; matrix products, arithmetic and copies ran while one was open for 3% of the time, Pallas kernels for 1%

profile of v8, /device:TPU:0, one launch (start us, length us, event | category | flops | bytes accessed | tf_op | source)
XLA Modules:
  0.0 94.1 jit_solution(8614355627641784683)
XLA Ops:
  0.7 1.6 %fusion = f32[64]{0:T(128)S(1)} fusion(bf16[64,8192]{1,0:T(8,128)(2,1)} %param.6), kind=kLoop, calls=%fused_computation.2 | loop fusion | flops 1572800 | bytes 1048832 | tf_op jit(solution)/shard_map/reduce_sum | solution.py:249
  2.3 3.0 %collective-permute-start = (f32[64]{0:T(128)S(1)}, f32[64]{0:T(128)S(1)}, u32[]{:S(2)}, u32[]{:S(2)}) collective-permute-start(f32[64]{0:T(128)S(1)} %fusion), channel_id=1, source_target_pairs={{0,1},{1,0},{2,3},{3,2},{4,5},{5,4},{6,7},{7,6},{8,9},{9,8},{10,11... | collective-permute-start | bytes 776 | tf_op jit(solution)/shard_map/ppermute | solution.py:36
  5.3 5.9 %all-to-all-start = ((bf16[16,8,512]{2,1,0:T(8,128)(2,1)}), bf16[16,8,512]{2,1,0:T(8,128)(2,1)S(1)}, u32[]{:S(2)}, u32[]{:S(2)}) async-start(bf16[16,8,512]{2,1,0:T(8,128)(2,1)} %bitcast.48), calls=%async_computation | async-start | bytes 262144 | tf_op jit(solution)/shard_map/all_to_all | solution.py:235
  11.3 1.1 %constant_dynamic-slice_fusion.3 = (bf16[32,2048]{1,0:T(8,128)(2,1)S(1)}, bf16[32,2048]{1,0:T(8,128)(2,1)S(1)}, bf16[32,2048]{1,0:T(8,128)(2,1)S(1)}, bf16[32,2048]{1,0:T(8,128)(2,1)S(1)}) fusion(bf16[32,8192]{1,0:T(8,128)(2,1)} %param.8, s32[]{:T(128)S(6)} %select_n.103, s32[]{:T(128)S(6)} %select_n.108, s32[]{:T(128)S(6)} %select_n.110, s32[]{:T(128)S(6)} %select_n.109), kind=kLoop, calls=%fused_computation.65 | loop fusion | bytes 1048592 | tf_op jit(solution)/shard_map/dynamic_slice | solution.py:230
  12.4 2.9 %collective-permute-start.10 = (bf16[32,2048]{1,0:T(8,128)(2,1)S(1)}, bf16[32,2048]{1,0:T(8,128)(2,1)S(1)}, u32[]{:S(2)}, u32[]{:S(2)}) collective-permute-start(bf16[32,2048]{1,0:T(8,128)(2,1)S(1)} %get-tuple-element.29), channel_id=1, source_target_pairs={{0,12},{4,8},{8,4},{12,0},{1,13},{5,9},{9,5},{13,1},{2,14},{6,10},... | collective-permute-start | bytes 393224 | tf_op jit(solution)/shard_map/ppermute | solution.py:50
  15.3 0.6 collective-permute-start.8
  15.8 0.2 collective-permute-start.9
  16.7 0.2 convert_reduce_fusion
  16.9 0.0 collective-permute-done
  16.9 0.4 fusion.3
  17.3 0.1 constant_dynamic-slice_fusion.4
  17.4 2.3 %all-to-all-done = bf16[16,8,512]{2,1,0:T(8,128)(2,1)S(1)} async-done(((bf16[16,8,512]{2,1,0:T(8,128)(2,1)}), bf16[16,8,512]{2,1,0:T(8,128)(2,1)S(1)}, u32[]{:S(2)}, u32[]{:S(2)}) %all-to-all-start) | async-done | bytes 131104 | tf_op jit(solution)/shard_map/all_to_all | solution.py:235
  19.7 0.4 convolution_convert_fusion.2
  20.1 0.1 pad_maximum_fusion
  20.2 0.1 collective-permute-start.1
  20.3 1.0 %collective-permute-start.2 = (bf16[64,2560]{1,0:T(8,128)(2,1)S(1)}, bf16[64,2560]{1,0:T(8,128)(2,1)S(1)}, u32[]{:S(2)}, u32[]{:S(2)}) collective-permute-start(bf16[64,2560]{1,0:T(8,128)(2,1)S(1)} %get-tuple-element.41), channel_id=1, source_target_pairs={{0,8},{4,12},{8,0},{12,4},{1,9},{5,13},{9,1},{13,5},{2,10},{6,14},... | collective-permute-start | bytes 983048 | tf_op jit(solution)/shard_map/ppermute | solution.py:50
  21.3 0.0 collective-permute-done.10
  21.3 2.5 %collective-permute-start.3 = (bf16[64,2560]{1,0:T(8,128)(2,1)S(1)}, bf16[64,2560]{1,0:T(8,128)(2,1)S(1)}, u32[]{:S(2)}, u32[]{:S(2)}) collective-permute-start(bf16[64,2560]{1,0:T(8,128)(2,1)S(1)} %get-tuple-element.39), channel_id=1, source_target_pairs={{0,12},{4,8},{8,4},{12,0},{1,13},{5,9},{9,5},{13,1},{2,14},{6,10},... | collective-permute-start | bytes 983048 | tf_op jit(solution)/shard_map/ppermute | solution.py:50
  23.8 0.0 collective-permute-done.8
  23.8 0.0 collective-permute-done.9
  23.8 1.7 %collective-permute-start.11 = (bf16[128,2048]{1,0:T(8,128)(2,1)S(1)}, bf16[128,2048]{1,0:T(8,128)(2,1)S(1)}, u32[]{:S(2)}, u32[]{:S(2)}) collective-permute-start(bf16[128,2048]{1,0:T(8,128)(2,1)S(1)} %pad_maximum_fusion.4.refs_8_), channel_id=1, source_target_pairs={{0,16},{16,0},{1,17},{17,1},{2,18},{18,2},{3,19},{19,3},{4,20},{20... | collective-permute-start | bytes 1572872 | tf_op jit(solution)/shard_map/ppermute | solution.py:233
  25.5 0.0 collective-permute-start.4
  25.5 4.5 %collective-permute-done.1.refs_1_ = bf16[64,2560]{1,0:T(8,128)(2,1)S(1)} collective-permute-done((bf16[64,2560]{1,0:T(8,128)(2,1)S(1)}, bf16[64,2560]{1,0:T(8,128)(2,1)S(1)}, u32[]{:S(2)}, u32[]{:S(2)}) %collective-permute-start.1) | collective-permute-done | bytes 327712 | tf_op jit(solution)/shard_map/ppermute | solution.py:50
  30.0 0.0 collective-permute-start.5
  30.0 12.3 %collective-permute-done.2.refs_2_ = bf16[64,2560]{1,0:T(8,128)(2,1)S(1)} collective-permute-done((bf16[64,2560]{1,0:T(8,128)(2,1)S(1)}, bf16[64,2560]{1,0:T(8,128)(2,1)S(1)}, u32[]{:S(2)}, u32[]{:S(2)}) %collective-permute-start.2) | collective-permute-done | bytes 327712 | tf_op jit(solution)/shard_map/ppermute | solution.py:50
  42.2 0.0 collective-permute-start.6
  42.2 6.2 %collective-permute-done.3.refs_3_ = bf16[64,2560]{1,0:T(8,128)(2,1)S(1)} collective-permute-done((bf16[64,2560]{1,0:T(8,128)(2,1)S(1)}, bf16[64,2560]{1,0:T(8,128)(2,1)S(1)}, u32[]{:S(2)}, u32[]{:S(2)}) %collective-permute-start.3) | collective-permute-done | bytes 327712 | tf_op jit(solution)/shard_map/ppermute | solution.py:50
  48.5 0.0 collective-permute-start.7
  48.5 0.0 collective-permute-done.4.refs_4_
  48.5 0.0 collective-permute-done.11.refs_9_
  48.5 0.0 collective-permute-done.5.refs_5_
  48.5 1.6 %collective-permute-done.7.refs_7_ = bf16[64,2560]{1,0:T(8,128)(2,1)S(1)} collective-permute-done((bf16[64,2560]{1,0:T(8,128)(2,1)S(1)}, bf16[64,2560]{1,0:T(8,128)(2,1)S(1)}, u32[]{:S(2)}, u32[]{:S(2)}) %collective-permute-start.7) | collective-permute-done | bytes 327712 | tf_op jit(solution)/shard_map/ppermute | solution.py:41
  50.1 3.5 %shard_map.85 = (bf16[256,2048]{1,0:T(8,128)(2,1)}, f32[1,2048]{1,0:T(1,128)S(1)}, bf16[2,64,256]{2,1,0:T(8,128)(2,1)S(1)}, bf16[2,64,256]{2,1,0:T(8,128)(2,1)S(...) custom-call(bf16[64,2560]{1,0:T(8,128)(2,1)S(1)} %get-tuple-element.42.refs_0_, ...), custom_call_target="tpu_custom_call" | custom-call | flops 1073741824 | bytes 6815744 | tf_op jit(solution)/shard_map/pallas_call | solution.py:131
  53.6 1.2 %collective-permute-start.12 = (bf16[2,64,256]{2,1,0:T(8,128)(2,1)S(1)}, bf16[2,64,256]{2,1,0:T(8,128)(2,1)S(1)}, u32[]{:S(2)}, u32[]{:S(2)}) collective-permute-start(bf16[2,64,256]{2,1,0:T(8,128)(2,1)S(1)} %get-tuple-element.14), channel_id=1, source_target_pairs={{0,4},{4,0},{8,12},{12,8},{1,5},{5,1},{9,13},{13,9},{2,6},{6,2},{1... | collective-permute-start | bytes 196616 | tf_op jit(solution)/shard_map/ppermute | solution.py:268
  54.8 0.0 collective-permute-start.13
  54.8 2.4 %collective-permute-start.14 = (bf16[2,64,256]{2,1,0:T(8,128)(2,1)S(1)}, bf16[2,64,256]{2,1,0:T(8,128)(2,1)S(1)}, u32[]{:S(2)}, u32[]{:S(2)}) collective-permute-start(bf16[2,64,256]{2,1,0:T(8,128)(2,1)S(1)} %get-tuple-element.16), channel_id=1, source_target_pairs={{0,12},{4,8},{8,4},{12,0},{1,13},{5,9},{9,5},{13,1},{2,14},{6,10},... | collective-permute-start | bytes 196616 | tf_op jit(solution)/shard_map/ppermute | solution.py:268
  57.2 3.6 %all-to-all-start.1 = ((bf16[8,32,2048]{2,1,0:T(8,128)(2,1)}), bf16[8,32,2048]{2,1,0:T(8,128)(2,1)S(1)}, u32[]{:S(2)}, u32[]{:S(2)}) async-start(bf16[8,32,2048]{2,1,0:T(8,128)(2,1)} %bitcast.14), calls=%async_computation.1 | async-start | bytes 2097152 | tf_op jit(solution)/shard_map/all_to_all | solution.py:275
  60.8 0.0 collective-permute-done.13
  60.9 0.6 collective-permute-start.15
  61.5 0.0 collective-permute-start.18
  61.5 4.4 %collective-permute-done.15 = f32[2,64,256]{2,1,0:T(8,128)S(1)} collective-permute-done((f32[2,64,256]{2,1,0:T(8,128)S(1)}, f32[2,64,256]{2,1,0:T(8,128)S(1)}, u32[]{:S(2)}, u32[]{:S(2)}) %collective-permute-start.15) | collective-permute-done | bytes 131104 | tf_op jit(solution)/shard_map/ppermute | solution.py:36
  66.0 0.1 collective-permute-start.16
  66.0 0.0 collective-permute-done.18
  66.1 1.2 %collective-permute-done.16 = bf16[64,256]{1,0:T(8,128)(2,1)S(1)} collective-permute-done((bf16[64,256]{1,0:T(8,128)(2,1)S(1)}, bf16[64,256]{1,0:T(8,128)(2,1)S(1)}, u32[]{:S(2)}, u32[]{:S(2)}) %collective-permute-start.16) | collective-permute-done | bytes 32800 | tf_op jit(solution)/shard_map/ppermute | solution.py:41
  67.2 0.5 convolution_convert_fusion
  67.7 0.2 collective-permute-start.17
  68.0 1.1 %collective-permute-done.17 = bf16[4,2,8,512]{3,2,1,0:T(8,128)(2,1)S(1)} collective-permute-done((bf16[4,2,8,512]{3,2,1,0:T(8,128)(2,1)S(1)}, bf16[4,2,8,512]{3,2,1,0:T(8,128)(2,1)S(1)}, u32[]{:S(2)}, u32[]{:S(2)}) %collective-permute-start.17) | collective-permute-done | bytes 65568 | tf_op jit(solution)/shard_map/ppermute | solution.py:41
  69.1 2.1 %collective-permute-start.20 = (bf16[48,512]{1,0:T(8,128)(2,1)S(1)}, bf16[48,512]{1,0:T(8,128)(2,1)S(1)}, u32[]{:S(2)}, u32[]{:S(2)}) collective-permute-start(bf16[48,512]{1,0:T(8,128)(2,1)S(1)} %get-tuple-element.33), channel_id=1, source_target_pairs={{0,4},{2,22},{4,0},{6,18},{8,12},{10,30},{12,8},{14,26},{16,20},{1... | collective-permute-start | bytes 147464 | tf_op jit(solution)/shard_map/ppermute | solution.py:320
  71.2 1.5 %collective-permute-start.21 = (bf16[48,512]{1,0:T(8,128)(2,1)S(1)}, bf16[48,512]{1,0:T(8,128)(2,1)S(1)}, u32[]{:S(2)}, u32[]{:S(2)}) collective-permute-start(bf16[48,512]{1,0:T(8,128)(2,1)S(1)} %get-tuple-element.34), channel_id=1, source_target_pairs={{0,8},{2,26},{4,12},{6,30},{8,0},{10,18},{12,4},{14,22},{16,24},{1... | collective-permute-start | bytes 147464 | tf_op jit(solution)/shard_map/ppermute | solution.py:320
  72.7 0.1 collective-permute-start.22
  72.8 16.8 %all-to-all-done.1 = bf16[8,32,2048]{2,1,0:T(8,128)(2,1)S(1)} async-done(((bf16[8,32,2048]{2,1,0:T(8,128)(2,1)}), bf16[8,32,2048]{2,1,0:T(8,128)(2,1)S(1)}, u32[]{:S(2)}, u32[]{:S(2)}) %all-to-all-start.1) | async-done | bytes 1048608 | tf_op jit(solution)/shard_map/all_to_all | solution.py:275
  89.5 0.7 collective-permute-start.19
  90.2 0.0 collective-permute-done.20.refs_1_
  90.2 0.1 collective-permute-start.24
  90.3 0.0 collective-permute-done.21.refs_2_
  90.3 0.5 collective-permute-start.25
  90.8 0.1 collective-permute-start.26
  90.8 0.0 collective-permute-done.19
  90.9 1.4 %collective-permute-start.23 = (bf16[48,512]{1,0:T(8,128)(2,1)S(1)}, bf16[48,512]{1,0:T(8,128)(2,1)S(1)}, u32[]{:S(2)}, u32[]{:S(2)}) collective-permute-start(bf16[48,512]{1,0:T(8,128)(2,1)S(1)} %broadcast_select_fusion.refs_0_), channel_id=1, source_target_pairs={{0,2},{2,0},{1,3},{3,1},{4,6},{6,4},{5,7},{7,5},{8,10},{10,8},{9,1... | collective-permute-start | bytes 147464 | tf_op jit(solution)/shard_map/ppermute | solution.py:41
  92.2 1.1 %shard_map.87 = f32[32,8192]{1,0:T(8,128)} custom-call(bf16[2,4,32,2048]{3,2,1,0:T(8,128)(2,1)S(1)} %bitcast.43), custom_call_target="tpu_custom_call" | custom-call | flops 1048576 | bytes 2097152 | tf_op jit(solution)/shard_map/pallas_call | solution.py:168
  93.3 0.0 collective-permute-done.24.refs_5_
  93.3 0.0 collective-permute-done.25.refs_6_
  93.3 0.0 collective-permute-done.23.refs_4_
  93.3 0.7 shard_map.86
  (28 shorter events, 0.3 us)
Async XLA Ops:
  0.6 16.2 %copy-start.1 = (bf16[64,8192]{1,0:T(8,128)(2,1)S(1)}, bf16[64,8192]{1,0:T(8,128)(2,1)}, u32[]{:S(2)}) copy-start(bf16[64,8192]{1,0:T(8,128)(2,1)} %param.6) | copy-start | bytes 3145732
  0.6 16.0 %copy-start.2 = (s32[64]{0:T(128)S(1)}, s32[64]{0:T(128)}, u32[]{:S(2)}) copy-start(s32[64]{0:T(128)} %param.11) | copy-start | bytes 772
  0.7 16.2 %copy-start = (f32[8192]{0:T(1024)S(1)}, f32[8192]{0:T(1024)}, u32[]{:S(2)}) copy-start(f32[8192]{0:T(1024)} %param.7) | copy-start | bytes 98308
  2.3 14.6 %collective-permute-start = (f32[64]{0:T(128)S(1)}, f32[64]{0:T(128)S(1)}, u32[]{:S(2)}, u32[]{:S(2)}) collective-permute-start(f32[64]{0:T(128)S(1)} %fusion), channel_id=1, source_target_pairs={{0,1},{1,0},{2,3},{3,2},{4,5},{5,4},{6,7},{7,6},{8,9},{9,8},{10,11... | collective-permute-start | bytes 776 | tf_op jit(solution)/shard_map/ppermute | solution.py:36
  5.3 14.4 %all-to-all-start = ((bf16[16,8,512]{2,1,0:T(8,128)(2,1)}), bf16[16,8,512]{2,1,0:T(8,128)(2,1)S(1)}, u32[]{:S(2)}, u32[]{:S(2)}) async-start(bf16[16,8,512]{2,1,0:T(8,128)(2,1)} %bitcast.48), calls=%async_computation | async-start | bytes 262144 | tf_op jit(solution)/shard_map/all_to_all | solution.py:235
  12.4 8.9 %collective-permute-start.10 = (bf16[32,2048]{1,0:T(8,128)(2,1)S(1)}, bf16[32,2048]{1,0:T(8,128)(2,1)S(1)}, u32[]{:S(2)}, u32[]{:S(2)}) collective-permute-start(bf16[32,2048]{1,0:T(8,128)(2,1)S(1)} %get-tuple-element.29), channel_id=1, source_target_pairs={{0,12},{4,8},{8,4},{12,0},{1,13},{5,9},{9,5},{13,1},{2,14},{6,10},... | collective-permute-start | bytes 393224 | tf_op jit(solution)/shard_map/ppermute | solution.py:50
  15.3 8.5 %collective-permute-start.8 = (bf16[32,2048]{1,0:T(8,128)(2,1)S(1)}, bf16[32,2048]{1,0:T(8,128)(2,1)S(1)}, u32[]{:S(2)}, u32[]{:S(2)}) collective-permute-start(bf16[32,2048]{1,0:T(8,128)(2,1)S(1)} %get-tuple-element.28), channel_id=1, source_target_pairs={{0,4},{4,0},{8,12},{12,8},{1,5},{5,1},{9,13},{13,9},{2,6},{6,2},{1... | collective-permute-start | bytes 393224 | tf_op jit(solution)/shard_map/ppermute | solution.py:50
  15.8 8.0 %collective-permute-start.9 = (bf16[32,2048]{1,0:T(8,128)(2,1)S(1)}, bf16[32,2048]{1,0:T(8,128)(2,1)S(1)}, u32[]{:S(2)}, u32[]{:S(2)}) collective-permute-start(bf16[32,2048]{1,0:T(8,128)(2,1)S(1)} %get-tuple-element.30), channel_id=1, source_target_pairs={{0,8},{4,12},{8,0},{12,4},{1,9},{5,13},{9,1},{13,5},{2,10},{6,14},... | collective-permute-start | bytes 393224 | tf_op jit(solution)/shard_map/ppermute | solution.py:50
  20.2 9.8 %collective-permute-start.1 = (bf16[64,2560]{1,0:T(8,128)(2,1)S(1)}, bf16[64,2560]{1,0:T(8,128)(2,1)S(1)}, u32[]{:S(2)}, u32[]{:S(2)}) collective-permute-start(bf16[64,2560]{1,0:T(8,128)(2,1)S(1)} %get-tuple-element.40), channel_id=1, source_target_pairs={{0,4},{4,0},{8,12},{12,8},{1,5},{5,1},{9,13},{13,9},{2,6},{6,2},{1... | collective-permute-start | bytes 983048 | tf_op jit(solution)/shard_map/ppermute | solution.py:50
  20.3 21.9 %collective-permute-start.2 = (bf16[64,2560]{1,0:T(8,128)(2,1)S(1)}, bf16[64,2560]{1,0:T(8,128)(2,1)S(1)}, u32[]{:S(2)}, u32[]{:S(2)}) collective-permute-start(bf16[64,2560]{1,0:T(8,128)(2,1)S(1)} %get-tuple-element.41), channel_id=1, source_target_pairs={{0,8},{4,12},{8,0},{12,4},{1,9},{5,13},{9,1},{13,5},{2,10},{6,14},... | collective-permute-start | bytes 983048 | tf_op jit(solution)/shard_map/ppermute | solution.py:50
  21.3 27.2 %collective-permute-start.3 = (bf16[64,2560]{1,0:T(8,128)(2,1)S(1)}, bf16[64,2560]{1,0:T(8,128)(2,1)S(1)}, u32[]{:S(2)}, u32[]{:S(2)}) collective-permute-start(bf16[64,2560]{1,0:T(8,128)(2,1)S(1)} %get-tuple-element.39), channel_id=1, source_target_pairs={{0,12},{4,8},{8,4},{12,0},{1,13},{5,9},{9,5},{13,1},{2,14},{6,10},... | collective-permute-start | bytes 983048 | tf_op jit(solution)/shard_map/ppermute | solution.py:50
  23.8 24.6 %collective-permute-start.11 = (bf16[128,2048]{1,0:T(8,128)(2,1)S(1)}, bf16[128,2048]{1,0:T(8,128)(2,1)S(1)}, u32[]{:S(2)}, u32[]{:S(2)}) collective-permute-start(bf16[128,2048]{1,0:T(8,128)(2,1)S(1)} %pad_maximum_fusion.4.refs_8_), channel_id=1, source_target_pairs={{0,16},{16,0},{1,17},{17,1},{2,18},{18,2},{3,19},{19,3},{4,20},{20... | collective-permute-start | bytes 1572872 | tf_op jit(solution)/shard_map/ppermute | solution.py:233
  25.5 23.0 %collective-permute-start.4 = (bf16[64,2560]{1,0:T(8,128)(2,1)S(1)}, bf16[64,2560]{1,0:T(8,128)(2,1)S(1)}, u32[]{:S(2)}, u32[]{:S(2)}) collective-permute-start(bf16[64,2560]{1,0:T(8,128)(2,1)S(1)} %get-tuple-element.42.refs_0_), channel_id=1, source_target_pairs={{0,2},{2,0},{1,3},{3,1},{4,6},{6,4},{5,7},{7,5},{8,10},{10,8},{9,1... | collective-permute-start | bytes 983048 | tf_op jit(solution)/shard_map/ppermute | solution.py:41
  30.0 18.5 %collective-permute-start.5 = (bf16[64,2560]{1,0:T(8,128)(2,1)S(1)}, bf16[64,2560]{1,0:T(8,128)(2,1)S(1)}, u32[]{:S(2)}, u32[]{:S(2)}) collective-permute-start(bf16[64,2560]{1,0:T(8,128)(2,1)S(1)} %collective-permute-done.1.refs_1_), channel_id=1, source_target_pairs={{0,2},{2,0},{1,3},{3,1},{4,6},{6,4},{5,7},{7,5},{8,10},{10,8},{9,1... | collective-permute-start | bytes 983048 | tf_op jit(solution)/shard_map/ppermute | solution.py:41
  42.2 6.2 %collective-permute-start.6 = (bf16[64,2560]{1,0:T(8,128)(2,1)S(1)}, bf16[64,2560]{1,0:T(8,128)(2,1)S(1)}, u32[]{:S(2)}, u32[]{:S(2)}) collective-permute-start(bf16[64,2560]{1,0:T(8,128)(2,1)S(1)} %collective-permute-done.2.refs_2_), channel_id=1, source_target_pairs={{0,2},{2,0},{1,3},{3,1},{4,6},{6,4},{5,7},{7,5},{8,10},{10,8},{9,1... | collective-permute-start | bytes 983048 | tf_op jit(solution)/shard_map/ppermute | solution.py:41
  48.5 1.6 %collective-permute-start.7 = (bf16[64,2560]{1,0:T(8,128)(2,1)S(1)}, bf16[64,2560]{1,0:T(8,128)(2,1)S(1)}, u32[]{:S(2)}, u32[]{:S(2)}) collective-permute-start(bf16[64,2560]{1,0:T(8,128)(2,1)S(1)} %collective-permute-done.3.refs_3_), channel_id=1, source_target_pairs={{0,2},{2,0},{1,3},{3,1},{4,6},{6,4},{5,7},{7,5},{8,10},{10,8},{9,1... | collective-permute-start | bytes 983048 | tf_op jit(solution)/shard_map/ppermute | solution.py:41
  53.6 7.2 %collective-permute-start.12 = (bf16[2,64,256]{2,1,0:T(8,128)(2,1)S(1)}, bf16[2,64,256]{2,1,0:T(8,128)(2,1)S(1)}, u32[]{:S(2)}, u32[]{:S(2)}) collective-permute-start(bf16[2,64,256]{2,1,0:T(8,128)(2,1)S(1)} %get-tuple-element.14), channel_id=1, source_target_pairs={{0,4},{4,0},{8,12},{12,8},{1,5},{5,1},{9,13},{13,9},{2,6},{6,2},{1... | collective-permute-start | bytes 196616 | tf_op jit(solution)/shard_map/ppermute | solution.py:268
  54.8 6.0 %collective-permute-start.13 = (bf16[2,64,256]{2,1,0:T(8,128)(2,1)S(1)}, bf16[2,64,256]{2,1,0:T(8,128)(2,1)S(1)}, u32[]{:S(2)}, u32[]{:S(2)}) collective-permute-start(bf16[2,64,256]{2,1,0:T(8,128)(2,1)S(1)} %get-tuple-element.15), channel_id=1, source_target_pairs={{0,8},{4,12},{8,0},{12,4},{1,9},{5,13},{9,1},{13,5},{2,10},{6,14},... | collective-permute-start | bytes 196616 | tf_op jit(solution)/shard_map/ppermute | solution.py:268
  54.8 6.0 %collective-permute-start.14 = (bf16[2,64,256]{2,1,0:T(8,128)(2,1)S(1)}, bf16[2,64,256]{2,1,0:T(8,128)(2,1)S(1)}, u32[]{:S(2)}, u32[]{:S(2)}) collective-permute-start(bf16[2,64,256]{2,1,0:T(8,128)(2,1)S(1)} %get-tuple-element.16), channel_id=1, source_target_pairs={{0,12},{4,8},{8,4},{12,0},{1,13},{5,9},{9,5},{13,1},{2,14},{6,10},... | collective-permute-start | bytes 196616 | tf_op jit(solution)/shard_map/ppermute | solution.py:268
  57.2 32.3 %all-to-all-start.1 = ((bf16[8,32,2048]{2,1,0:T(8,128)(2,1)}), bf16[8,32,2048]{2,1,0:T(8,128)(2,1)S(1)}, u32[]{:S(2)}, u32[]{:S(2)}) async-start(bf16[8,32,2048]{2,1,0:T(8,128)(2,1)} %bitcast.14), calls=%async_computation.1 | async-start | bytes 2097152 | tf_op jit(solution)/shard_map/all_to_all | solution.py:275
  60.9 5.0 %collective-permute-start.15 = (f32[2,64,256]{2,1,0:T(8,128)S(1)}, f32[2,64,256]{2,1,0:T(8,128)S(1)}, u32[]{:S(2)}, u32[]{:S(2)}) collective-permute-start(f32[2,64,256]{2,1,0:T(8,128)S(1)} %convert_add_fusion), channel_id=1, source_target_pairs={{0,1},{1,0},{2,3},{3,2},{4,5},{5,4},{6,7},{7,6},{8,9},{9,8},{10,11... | collective-permute-start | bytes 393224 | tf_op jit(solution)/shard_map/ppermute | solution.py:36
  61.5 4.5 %collective-permute-start.18 = (f32[2048]{0:T(1024)S(1)}, f32[2048]{0:T(1024)S(1)}, u32[]{:S(2)}, u32[]{:S(2)}) collective-permute-start(f32[2048]{0:T(1024)S(1)} %bitcast.45), channel_id=1, source_target_pairs={{0,2},{2,0},{1,3},{3,1},{4,6},{6,4},{5,7},{7,5},{8,10},{10,8},{9,1... | collective-permute-start | bytes 24584 | tf_op jit(solution)/shard_map/ppermute | solution.py:41
  66.0 1.3 %collective-permute-start.16 = (bf16[64,256]{1,0:T(8,128)(2,1)S(1)}, bf16[64,256]{1,0:T(8,128)(2,1)S(1)}, u32[]{:S(2)}, u32[]{:S(2)}) collective-permute-start(bf16[64,256]{1,0:T(8,128)(2,1)S(1)} %get-tuple-element.38), channel_id=1, source_target_pairs={{0,2},{2,0},{1,3},{3,1},{4,6},{6,4},{5,7},{7,5},{8,10},{10,8},{9,1... | collective-permute-start | bytes 98312 | tf_op jit(solution)/shard_map/ppermute | solution.py:41
  67.7 1.3 %collective-permute-start.17 = (bf16[4,2,8,512]{3,2,1,0:T(8,128)(2,1)S(1)}, bf16[4,2,8,512]{3,2,1,0:T(8,128)(2,1)S(1)}, u32[]{:S(2)}, u32[]{:S(2)}) collective-permute-start(bf16[4,2,8,512]{3,2,1,0:T(8,128)(2,1)S(1)} %dynamic-slice_bitcast_fusion), channel_id=1, source_target_pairs={{0,2},{2,0},{1,3},{3,1},{4,6},{6,4},{5,7},{7,5},{8,10},{10,8},{9,1... | collective-permute-start | bytes 196616 | tf_op jit(solution)/shard_map/ppermute | solution.py:41
  69.1 21.0 %collective-permute-start.20 = (bf16[48,512]{1,0:T(8,128)(2,1)S(1)}, bf16[48,512]{1,0:T(8,128)(2,1)S(1)}, u32[]{:S(2)}, u32[]{:S(2)}) collective-permute-start(bf16[48,512]{1,0:T(8,128)(2,1)S(1)} %get-tuple-element.33), channel_id=1, source_target_pairs={{0,4},{2,22},{4,0},{6,18},{8,12},{10,30},{12,8},{14,26},{16,20},{1... | collective-permute-start | bytes 147464 | tf_op jit(solution)/shard_map/ppermute | solution.py:320
  71.2 19.0 %collective-permute-start.21 = (bf16[48,512]{1,0:T(8,128)(2,1)S(1)}, bf16[48,512]{1,0:T(8,128)(2,1)S(1)}, u32[]{:S(2)}, u32[]{:S(2)}) collective-permute-start(bf16[48,512]{1,0:T(8,128)(2,1)S(1)} %get-tuple-element.34), channel_id=1, source_target_pairs={{0,8},{2,26},{4,12},{6,30},{8,0},{10,18},{12,4},{14,22},{16,24},{1... | collective-permute-start | bytes 147464 | tf_op jit(solution)/shard_map/ppermute | solution.py:320
  72.7 18.1 %collective-permute-start.22 = (bf16[48,512]{1,0:T(8,128)(2,1)S(1)}, bf16[48,512]{1,0:T(8,128)(2,1)S(1)}, u32[]{:S(2)}, u32[]{:S(2)}) collective-permute-start(bf16[48,512]{1,0:T(8,128)(2,1)S(1)} %get-tuple-element.31), channel_id=1, source_target_pairs={{0,12},{2,30},{4,8},{6,26},{8,4},{10,22},{12,0},{14,18},{16,28},{1... | collective-permute-start | bytes 147464 | tf_op jit(solution)/shard_map/ppermute | solution.py:320
  89.5 1.3 %collective-permute-start.19 = (bf16[48,512]{1,0:T(8,128)(2,1)S(1)}, bf16[48,512]{1,0:T(8,128)(2,1)S(1)}, u32[]{:S(2)}, u32[]{:S(2)}) collective-permute-start(bf16[48,512]{1,0:T(8,128)(2,1)S(1)} %get-tuple-element.19), channel_id=1, source_target_pairs={{2,18},{6,22},{10,26},{14,30},{18,2},{22,6},{26,10},{30,14},{3,19}... | collective-permute-start | bytes 147464 | tf_op jit(solution)/shard_map/ppermute | solution.py:320
  90.2 3.2 %collective-permute-start.24 = (bf16[48,512]{1,0:T(8,128)(2,1)S(1)}, bf16[48,512]{1,0:T(8,128)(2,1)S(1)}, u32[]{:S(2)}, u32[]{:S(2)}) collective-permute-start(bf16[48,512]{1,0:T(8,128)(2,1)S(1)} %collective-permute-done.20.refs_1_), channel_id=1, source_target_pairs={{0,2},{2,0},{1,3},{3,1},{4,6},{6,4},{5,7},{7,5},{8,10},{10,8},{9,1... | collective-permute-start | bytes 147464 | tf_op jit(solution)/shard_map/ppermute | solution.py:41
  90.3 3.1 %collective-permute-start.25 = (bf16[48,512]{1,0:T(8,128)(2,1)S(1)}, bf16[48,512]{1,0:T(8,128)(2,1)S(1)}, u32[]{:S(2)}, u32[]{:S(2)}) collective-permute-start(bf16[48,512]{1,0:T(8,128)(2,1)S(1)} %collective-permute-done.21.refs_2_), channel_id=1, source_target_pairs={{0,2},{2,0},{1,3},{3,1},{4,6},{6,4},{5,7},{7,5},{8,10},{10,8},{9,1... | collective-permute-start | bytes 147464 | tf_op jit(solution)/shard_map/ppermute | solution.py:41
  90.8 2.6 %collective-permute-start.26 = (bf16[48,512]{1,0:T(8,128)(2,1)S(1)}, bf16[48,512]{1,0:T(8,128)(2,1)S(1)}, u32[]{:S(2)}, u32[]{:S(2)}) collective-permute-start(bf16[48,512]{1,0:T(8,128)(2,1)S(1)} %collective-permute-done.22.refs_3_), channel_id=1, source_target_pairs={{0,2},{2,0},{1,3},{3,1},{4,6},{6,4},{5,7},{7,5},{8,10},{10,8},{9,1... | collective-permute-start | bytes 147464 | tf_op jit(solution)/shard_map/ppermute | solution.py:41
  90.9 2.5 %collective-permute-start.23 = (bf16[48,512]{1,0:T(8,128)(2,1)S(1)}, bf16[48,512]{1,0:T(8,128)(2,1)S(1)}, u32[]{:S(2)}, u32[]{:S(2)}) collective-permute-start(bf16[48,512]{1,0:T(8,128)(2,1)S(1)} %broadcast_select_fusion.refs_0_), channel_id=1, source_target_pairs={{0,2},{2,0},{1,3},{3,1},{4,6},{6,4},{5,7},{7,5},{8,10},{10,8},{9,1... | collective-permute-start | bytes 147464 | tf_op jit(solution)/shard_map/ppermute | solution.py:41

commit v9 on v7

--- a/solution.py
+++ b/solution.py
@@ -257,7 +257,7 @@
             [lax.dynamic_slice(normed, (0, j * part), (rows, part)), row_cot], axis=1
         )
     )
-    rows_there = [swap_core(piece) for piece in rows_here]
+    rows_there = [swap_core(piece) for piece in rows_here[::-1]][::-1]
     grad_part, gain_part, *key_parts = products(
         rows_here, rows_there, (weight_here, weight_there), core_keys, part, owned
     )

time: 94.4 us -> 94.4 us (level)
  no operation moved by 1% of the time
where the time goes in v9:
time: 94.4 us; the launch traced here: 94.1 us
  waiting for transfers between devices  50.3 us (53%)
  starting transfers between devices  32.1 us (34%)
  Pallas kernels  5.34 us (6%)
  other arithmetic  2.45 us (3%)
  between operations  1.65 us (2%)
  local copies, waits for them, and re-layouts  1.29 us (1%)
    ppermute x6, waiting for transfers between devices, swap_lo(): pieces.append(lax.ppermute(block(me ^ step), 'lo', pairs))  23 us
    all_to_all x1, waiting for transfers between devices, on_device(): lax.all_to_all(grad_part.reshape(halves * low, owned, part), ('hi', 'lo')...  16.8 us
    ppermute x6, starting transfers between devices, swap_lo(): pieces.append(lax.ppermute(block(me ^ step), 'lo', pairs))  7.11 us
    all_to_all x1, starting transfers between devices, on_device(): lax.all_to_all(cotangent[0], DP, split_axis=0, concat_axis=0, tiled=True)  5.94 us
    ppermute x2, waiting for transfers between devices, reduce_tensor(): return value + lax.ppermute(value, 'tensor', SWAP)  4.43 us
    ppermute x4, starting transfers between devices, on_device(): pieces[step] = lax.ppermute(pieces[step], DP, pairs)  4.27 us
    ppermute x11, waiting for transfers between devices, swap_core(): return lax.ppermute(value, 'core', SWAP)  3.84 us
    all_to_all x1, starting transfers between devices, on_device(): lax.all_to_all(grad_part.reshape(halves * low, owned, part), ('hi', 'lo')...  3.64 us
  transfers between devices with their start and end apart: 29, of which 9 were waited for; matrix products, arithmetic and copies ran while one was open for 3% of the time, Pallas kernels for 1%

profile of v9, /device:TPU:0, one launch (start us, length us, event | category | flops | bytes accessed | tf_op | source)
XLA Modules:
  0.0 94.1 jit_solution(5143117828304119750)
XLA Ops:
  0.7 1.6 %fusion = f32[64]{0:T(128)S(1)} fusion(bf16[64,8192]{1,0:T(8,128)(2,1)} %param.6), kind=kLoop, calls=%fused_computation.2 | loop fusion | flops 1572800 | bytes 1048832 | tf_op jit(solution)/shard_map/reduce_sum | solution.py:249
  2.3 3.0 %collective-permute-start = (f32[64]{0:T(128)S(1)}, f32[64]{0:T(128)S(1)}, u32[]{:S(2)}, u32[]{:S(2)}) collective-permute-start(f32[64]{0:T(128)S(1)} %fusion), channel_id=1, source_target_pairs={{0,1},{1,0},{2,3},{3,2},{4,5},{5,4},{6,7},{7,6},{8,9},{9,8},{10,11... | collective-permute-start | bytes 776 | tf_op jit(solution)/shard_map/ppermute | solution.py:36
  5.3 5.9 %all-to-all-start = ((bf16[16,8,512]{2,1,0:T(8,128)(2,1)}), bf16[16,8,512]{2,1,0:T(8,128)(2,1)S(1)}, u32[]{:S(2)}, u32[]{:S(2)}) async-start(bf16[16,8,512]{2,1,0:T(8,128)(2,1)} %bitcast.48), calls=%async_computation | async-start | bytes 262144 | tf_op jit(solution)/shard_map/all_to_all | solution.py:235
  11.3 1.1 %constant_dynamic-slice_fusion.3 = (bf16[32,2048]{1,0:T(8,128)(2,1)S(1)}, bf16[32,2048]{1,0:T(8,128)(2,1)S(1)}, bf16[32,2048]{1,0:T(8,128)(2,1)S(1)}, bf16[32,2048]{1,0:T(8,128)(2,1)S(1)}) fusion(bf16[32,8192]{1,0:T(8,128)(2,1)} %param.8, s32[]{:T(128)S(6)} %select_n.103, s32[]{:T(128)S(6)} %select_n.108, s32[]{:T(128)S(6)} %select_n.110, s32[]{:T(128)S(6)} %select_n.109), kind=kLoop, calls=%fused_computation.65 | loop fusion | bytes 1048592 | tf_op jit(solution)/shard_map/dynamic_slice | solution.py:230
  12.4 2.9 %collective-permute-start.10 = (bf16[32,2048]{1,0:T(8,128)(2,1)S(1)}, bf16[32,2048]{1,0:T(8,128)(2,1)S(1)}, u32[]{:S(2)}, u32[]{:S(2)}) collective-permute-start(bf16[32,2048]{1,0:T(8,128)(2,1)S(1)} %get-tuple-element.29), channel_id=1, source_target_pairs={{0,12},{4,8},{8,4},{12,0},{1,13},{5,9},{9,5},{13,1},{2,14},{6,10},... | collective-permute-start | bytes 393224 | tf_op jit(solution)/shard_map/ppermute | solution.py:50
  15.3 0.6 collective-permute-start.8
  15.8 0.2 collective-permute-start.9
  16.7 0.2 convert_reduce_fusion
  16.9 0.0 collective-permute-done
  16.9 0.4 fusion.3
  17.3 0.1 constant_dynamic-slice_fusion.4
  17.4 2.3 %all-to-all-done = bf16[16,8,512]{2,1,0:T(8,128)(2,1)S(1)} async-done(((bf16[16,8,512]{2,1,0:T(8,128)(2,1)}), bf16[16,8,512]{2,1,0:T(8,128)(2,1)S(1)}, u32[]{:S(2)}, u32[]{:S(2)}) %all-to-all-start) | async-done | bytes 131104 | tf_op jit(solution)/shard_map/all_to_all | solution.py:235
  19.7 0.4 convolution_convert_fusion.2
  20.1 0.1 pad_maximum_fusion
  20.2 0.1 collective-permute-start.1
  20.3 1.0 %collective-permute-start.2 = (bf16[64,2560]{1,0:T(8,128)(2,1)S(1)}, bf16[64,2560]{1,0:T(8,128)(2,1)S(1)}, u32[]{:S(2)}, u32[]{:S(2)}) collective-permute-start(bf16[64,2560]{1,0:T(8,128)(2,1)S(1)} %get-tuple-element.41), channel_id=1, source_target_pairs={{0,8},{4,12},{8,0},{12,4},{1,9},{5,13},{9,1},{13,5},{2,10},{6,14},... | collective-permute-start | bytes 983048 | tf_op jit(solution)/shard_map/ppermute | solution.py:50
  21.3 0.0 collective-permute-done.10
  21.3 2.5 %collective-permute-start.3 = (bf16[64,2560]{1,0:T(8,128)(2,1)S(1)}, bf16[64,2560]{1,0:T(8,128)(2,1)S(1)}, u32[]{:S(2)}, u32[]{:S(2)}) collective-permute-start(bf16[64,2560]{1,0:T(8,128)(2,1)S(1)} %get-tuple-element.39), channel_id=1, source_target_pairs={{0,12},{4,8},{8,4},{12,0},{1,13},{5,9},{9,5},{13,1},{2,14},{6,10},... | collective-permute-start | bytes 983048 | tf_op jit(solution)/shard_map/ppermute | solution.py:50
  23.8 0.0 collective-permute-done.8
  23.8 0.0 collective-permute-done.9
  23.8 1.7 %collective-permute-start.11 = (bf16[128,2048]{1,0:T(8,128)(2,1)S(1)}, bf16[128,2048]{1,0:T(8,128)(2,1)S(1)}, u32[]{:S(2)}, u32[]{:S(2)}) collective-permute-start(bf16[128,2048]{1,0:T(8,128)(2,1)S(1)} %pad_maximum_fusion.4.refs_8_), channel_id=1, source_target_pairs={{0,16},{16,0},{1,17},{17,1},{2,18},{18,2},{3,19},{19,3},{4,20},{20... | collective-permute-start | bytes 1572872 | tf_op jit(solution)/shard_map/ppermute | solution.py:233
  25.5 0.0 collective-permute-start.4
  25.5 4.5 %collective-permute-done.1.refs_1_ = bf16[64,2560]{1,0:T(8,128)(2,1)S(1)} collective-permute-done((bf16[64,2560]{1,0:T(8,128)(2,1)S(1)}, bf16[64,2560]{1,0:T(8,128)(2,1)S(1)}, u32[]{:S(2)}, u32[]{:S(2)}) %collective-permute-start.1) | collective-permute-done | bytes 327712 | tf_op jit(solution)/shard_map/ppermute | solution.py:50
  30.0 0.0 collective-permute-start.5
  30.0 12.3 %collective-permute-done.2.refs_2_ = bf16[64,2560]{1,0:T(8,128)(2,1)S(1)} collective-permute-done((bf16[64,2560]{1,0:T(8,128)(2,1)S(1)}, bf16[64,2560]{1,0:T(8,128)(2,1)S(1)}, u32[]{:S(2)}, u32[]{:S(2)}) %collective-permute-start.2) | collective-permute-done | bytes 327712 | tf_op jit(solution)/shard_map/ppermute | solution.py:50
  42.2 0.0 collective-permute-start.6
  42.2 6.2 %collective-permute-done.3.refs_3_ = bf16[64,2560]{1,0:T(8,128)(2,1)S(1)} collective-permute-done((bf16[64,2560]{1,0:T(8,128)(2,1)S(1)}, bf16[64,2560]{1,0:T(8,128)(2,1)S(1)}, u32[]{:S(2)}, u32[]{:S(2)}) %collective-permute-start.3) | collective-permute-done | bytes 327712 | tf_op jit(solution)/shard_map/ppermute | solution.py:50
  48.5 0.0 collective-permute-start.7
  48.5 0.0 collective-permute-done.4.refs_4_
  48.5 0.0 collective-permute-done.11.refs_9_
  48.5 0.0 collective-permute-done.5.refs_5_
  48.5 1.6 %collective-permute-done.7.refs_7_ = bf16[64,2560]{1,0:T(8,128)(2,1)S(1)} collective-permute-done((bf16[64,2560]{1,0:T(8,128)(2,1)S(1)}, bf16[64,2560]{1,0:T(8,128)(2,1)S(1)}, u32[]{:S(2)}, u32[]{:S(2)}) %collective-permute-start.7) | collective-permute-done | bytes 327712 | tf_op jit(solution)/shard_map/ppermute | solution.py:41
  50.1 3.5 %shard_map.85 = (bf16[256,2048]{1,0:T(8,128)(2,1)}, f32[1,2048]{1,0:T(1,128)S(1)}, bf16[2,64,256]{2,1,0:T(8,128)(2,1)S(1)}, bf16[2,64,256]{2,1,0:T(8,128)(2,1)S(...) custom-call(bf16[64,2560]{1,0:T(8,128)(2,1)S(1)} %get-tuple-element.42.refs_0_, ...), custom_call_target="tpu_custom_call" | custom-call | flops 1073741824 | bytes 6815744 | tf_op jit(solution)/shard_map/pallas_call | solution.py:131
  53.6 1.2 %collective-permute-start.12 = (bf16[2,64,256]{2,1,0:T(8,128)(2,1)S(1)}, bf16[2,64,256]{2,1,0:T(8,128)(2,1)S(1)}, u32[]{:S(2)}, u32[]{:S(2)}) collective-permute-start(bf16[2,64,256]{2,1,0:T(8,128)(2,1)S(1)} %get-tuple-element.14), channel_id=1, source_target_pairs={{0,4},{4,0},{8,12},{12,8},{1,5},{5,1},{9,13},{13,9},{2,6},{6,2},{1... | collective-permute-start | bytes 196616 | tf_op jit(solution)/shard_map/ppermute | solution.py:268
  54.8 0.0 collective-permute-start.13
  54.8 2.4 %collective-permute-start.14 = (bf16[2,64,256]{2,1,0:T(8,128)(2,1)S(1)}, bf16[2,64,256]{2,1,0:T(8,128)(2,1)S(1)}, u32[]{:S(2)}, u32[]{:S(2)}) collective-permute-start(bf16[2,64,256]{2,1,0:T(8,128)(2,1)S(1)} %get-tuple-element.16), channel_id=1, source_target_pairs={{0,12},{4,8},{8,4},{12,0},{1,13},{5,9},{9,5},{13,1},{2,14},{6,10},... | collective-permute-start | bytes 196616 | tf_op jit(solution)/shard_map/ppermute | solution.py:268
  57.2 3.6 %all-to-all-start.1 = ((bf16[8,32,2048]{2,1,0:T(8,128)(2,1)}), bf16[8,32,2048]{2,1,0:T(8,128)(2,1)S(1)}, u32[]{:S(2)}, u32[]{:S(2)}) async-start(bf16[8,32,2048]{2,1,0:T(8,128)(2,1)} %bitcast.14), calls=%async_computation.1 | async-start | bytes 2097152 | tf_op jit(solution)/shard_map/all_to_all | solution.py:275
  60.8 0.0 collective-permute-done.13
  60.9 0.6 collective-permute-start.15
  61.5 0.0 collective-permute-start.18
  61.5 4.4 %collective-permute-done.15 = f32[2,64,256]{2,1,0:T(8,128)S(1)} collective-permute-done((f32[2,64,256]{2,1,0:T(8,128)S(1)}, f32[2,64,256]{2,1,0:T(8,128)S(1)}, u32[]{:S(2)}, u32[]{:S(2)}) %collective-permute-start.15) | collective-permute-done | bytes 131104 | tf_op jit(solution)/shard_map/ppermute | solution.py:36
  66.0 0.1 collective-permute-start.16
  66.0 0.0 collective-permute-done.18
  66.1 1.2 %collective-permute-done.16 = bf16[64,256]{1,0:T(8,128)(2,1)S(1)} collective-permute-done((bf16[64,256]{1,0:T(8,128)(2,1)S(1)}, bf16[64,256]{1,0:T(8,128)(2,1)S(1)}, u32[]{:S(2)}, u32[]{:S(2)}) %collective-permute-start.16) | collective-permute-done | bytes 32800 | tf_op jit(solution)/shard_map/ppermute | solution.py:41
  67.2 0.5 convolution_convert_fusion
  67.7 0.2 collective-permute-start.17
  68.0 1.1 %collective-permute-done.17 = bf16[4,2,8,512]{3,2,1,0:T(8,128)(2,1)S(1)} collective-permute-done((bf16[4,2,8,512]{3,2,1,0:T(8,128)(2,1)S(1)}, bf16[4,2,8,512]{3,2,1,0:T(8,128)(2,1)S(1)}, u32[]{:S(2)}, u32[]{:S(2)}) %collective-permute-start.17) | collective-permute-done | bytes 65568 | tf_op jit(solution)/shard_map/ppermute | solution.py:41
  69.1 2.1 %collective-permute-start.20 = (bf16[48,512]{1,0:T(8,128)(2,1)S(1)}, bf16[48,512]{1,0:T(8,128)(2,1)S(1)}, u32[]{:S(2)}, u32[]{:S(2)}) collective-permute-start(bf16[48,512]{1,0:T(8,128)(2,1)S(1)} %get-tuple-element.33), channel_id=1, source_target_pairs={{0,4},{2,22},{4,0},{6,18},{8,12},{10,30},{12,8},{14,26},{16,20},{1... | collective-permute-start | bytes 147464 | tf_op jit(solution)/shard_map/ppermute | solution.py:320
  71.2 1.5 %collective-permute-start.21 = (bf16[48,512]{1,0:T(8,128)(2,1)S(1)}, bf16[48,512]{1,0:T(8,128)(2,1)S(1)}, u32[]{:S(2)}, u32[]{:S(2)}) collective-permute-start(bf16[48,512]{1,0:T(8,128)(2,1)S(1)} %get-tuple-element.34), channel_id=1, source_target_pairs={{0,8},{2,26},{4,12},{6,30},{8,0},{10,18},{12,4},{14,22},{16,24},{1... | collective-permute-start | bytes 147464 | tf_op jit(solution)/shard_map/ppermute | solution.py:320
  72.7 0.1 collective-permute-start.22
  72.8 16.8 %all-to-all-done.1 = bf16[8,32,2048]{2,1,0:T(8,128)(2,1)S(1)} async-done(((bf16[8,32,2048]{2,1,0:T(8,128)(2,1)}), bf16[8,32,2048]{2,1,0:T(8,128)(2,1)S(1)}, u32[]{:S(2)}, u32[]{:S(2)}) %all-to-all-start.1) | async-done | bytes 1048608 | tf_op jit(solution)/shard_map/all_to_all | solution.py:275
  89.5 0.7 collective-permute-start.19
  90.2 0.0 collective-permute-done.20.refs_1_
  90.2 0.1 collective-permute-start.24
  90.3 0.0 collective-permute-done.21.refs_2_
  90.3 0.5 collective-permute-start.25
  90.8 0.1 collective-permute-start.26
  90.8 0.0 collective-permute-done.19
  90.9 1.4 %collective-permute-start.23 = (bf16[48,512]{1,0:T(8,128)(2,1)S(1)}, bf16[48,512]{1,0:T(8,128)(2,1)S(1)}, u32[]{:S(2)}, u32[]{:S(2)}) collective-permute-start(bf16[48,512]{1,0:T(8,128)(2,1)S(1)} %broadcast_select_fusion.refs_0_), channel_id=1, source_target_pairs={{0,2},{2,0},{1,3},{3,1},{4,6},{6,4},{5,7},{7,5},{8,10},{10,8},{9,1... | collective-permute-start | bytes 147464 | tf_op jit(solution)/shard_map/ppermute | solution.py:41
  92.2 1.1 %shard_map.87 = f32[32,8192]{1,0:T(8,128)} custom-call(bf16[2,4,32,2048]{3,2,1,0:T(8,128)(2,1)S(1)} %bitcast.43), custom_call_target="tpu_custom_call" | custom-call | flops 1048576 | bytes 2097152 | tf_op jit(solution)/shard_map/pallas_call | solution.py:168
  93.3 0.0 collective-permute-done.24.refs_5_
  93.3 0.0 collective-permute-done.25.refs_6_
  93.3 0.0 collective-permute-done.23.refs_4_
  93.3 0.7 shard_map.86
  (28 shorter events, 0.3 us)
Async XLA Ops:
  0.6 16.2 %copy-start.1 = (bf16[64,8192]{1,0:T(8,128)(2,1)S(1)}, bf16[64,8192]{1,0:T(8,128)(2,1)}, u32[]{:S(2)}) copy-start(bf16[64,8192]{1,0:T(8,128)(2,1)} %param.6) | copy-start | bytes 3145732
  0.6 16.0 %copy-start.2 = (s32[64]{0:T(128)S(1)}, s32[64]{0:T(128)}, u32[]{:S(2)}) copy-start(s32[64]{0:T(128)} %param.11) | copy-start | bytes 772
  0.7 16.2 %copy-start = (f32[8192]{0:T(1024)S(1)}, f32[8192]{0:T(1024)}, u32[]{:S(2)}) copy-start(f32[8192]{0:T(1024)} %param.7) | copy-start | bytes 98308
  2.3 14.6 %collective-permute-start = (f32[64]{0:T(128)S(1)}, f32[64]{0:T(128)S(1)}, u32[]{:S(2)}, u32[]{:S(2)}) collective-permute-start(f32[64]{0:T(128)S(1)} %fusion), channel_id=1, source_target_pairs={{0,1},{1,0},{2,3},{3,2},{4,5},{5,4},{6,7},{7,6},{8,9},{9,8},{10,11... | collective-permute-start | bytes 776 | tf_op jit(solution)/shard_map/ppermute | solution.py:36
  5.3 14.4 %all-to-all-start = ((bf16[16,8,512]{2,1,0:T(8,128)(2,1)}), bf16[16,8,512]{2,1,0:T(8,128)(2,1)S(1)}, u32[]{:S(2)}, u32[]{:S(2)}) async-start(bf16[16,8,512]{2,1,0:T(8,128)(2,1)} %bitcast.48), calls=%async_computation | async-start | bytes 262144 | tf_op jit(solution)/shard_map/all_to_all | solution.py:235
  12.4 8.9 %collective-permute-start.10 = (bf16[32,2048]{1,0:T(8,128)(2,1)S(1)}, bf16[32,2048]{1,0:T(8,128)(2,1)S(1)}, u32[]{:S(2)}, u32[]{:S(2)}) collective-permute-start(bf16[32,2048]{1,0:T(8,128)(2,1)S(1)} %get-tuple-element.29), channel_id=1, source_target_pairs={{0,12},{4,8},{8,4},{12,0},{1,13},{5,9},{9,5},{13,1},{2,14},{6,10},... | collective-permute-start | bytes 393224 | tf_op jit(solution)/shard_map/ppermute | solution.py:50
  15.3 8.5 %collective-permute-start.8 = (bf16[32,2048]{1,0:T(8,128)(2,1)S(1)}, bf16[32,2048]{1,0:T(8,128)(2,1)S(1)}, u32[]{:S(2)}, u32[]{:S(2)}) collective-permute-start(bf16[32,2048]{1,0:T(8,128)(2,1)S(1)} %get-tuple-element.28), channel_id=1, source_target_pairs={{0,4},{4,0},{8,12},{12,8},{1,5},{5,1},{9,13},{13,9},{2,6},{6,2},{1... | collective-permute-start | bytes 393224 | tf_op jit(solution)/shard_map/ppermute | solution.py:50
  15.8 8.0 %collective-permute-start.9 = (bf16[32,2048]{1,0:T(8,128)(2,1)S(1)}, bf16[32,2048]{1,0:T(8,128)(2,1)S(1)}, u32[]{:S(2)}, u32[]{:S(2)}) collective-permute-start(bf16[32,2048]{1,0:T(8,128)(2,1)S(1)} %get-tuple-element.30), channel_id=1, source_target_pairs={{0,8},{4,12},{8,0},{12,4},{1,9},{5,13},{9,1},{13,5},{2,10},{6,14},... | collective-permute-start | bytes 393224 | tf_op jit(solution)/shard_map/ppermute | solution.py:50
  20.2 9.8 %collective-permute-start.1 = (bf16[64,2560]{1,0:T(8,128)(2,1)S(1)}, bf16[64,2560]{1,0:T(8,128)(2,1)S(1)}, u32[]{:S(2)}, u32[]{:S(2)}) collective-permute-start(bf16[64,2560]{1,0:T(8,128)(2,1)S(1)} %get-tuple-element.40), channel_id=1, source_target_pairs={{0,4},{4,0},{8,12},{12,8},{1,5},{5,1},{9,13},{13,9},{2,6},{6,2},{1... | collective-permute-start | bytes 983048 | tf_op jit(solution)/shard_map/ppermute | solution.py:50
  20.3 21.9 %collective-permute-start.2 = (bf16[64,2560]{1,0:T(8,128)(2,1)S(1)}, bf16[64,2560]{1,0:T(8,128)(2,1)S(1)}, u32[]{:S(2)}, u32[]{:S(2)}) collective-permute-start(bf16[64,2560]{1,0:T(8,128)(2,1)S(1)} %get-tuple-element.41), channel_id=1, source_target_pairs={{0,8},{4,12},{8,0},{12,4},{1,9},{5,13},{9,1},{13,5},{2,10},{6,14},... | collective-permute-start | bytes 983048 | tf_op jit(solution)/shard_map/ppermute | solution.py:50
  21.3 27.2 %collective-permute-start.3 = (bf16[64,2560]{1,0:T(8,128)(2,1)S(1)}, bf16[64,2560]{1,0:T(8,128)(2,1)S(1)}, u32[]{:S(2)}, u32[]{:S(2)}) collective-permute-start(bf16[64,2560]{1,0:T(8,128)(2,1)S(1)} %get-tuple-element.39), channel_id=1, source_target_pairs={{0,12},{4,8},{8,4},{12,0},{1,13},{5,9},{9,5},{13,1},{2,14},{6,10},... | collective-permute-start | bytes 983048 | tf_op jit(solution)/shard_map/ppermute | solution.py:50
  23.8 24.6 %collective-permute-start.11 = (bf16[128,2048]{1,0:T(8,128)(2,1)S(1)}, bf16[128,2048]{1,0:T(8,128)(2,1)S(1)}, u32[]{:S(2)}, u32[]{:S(2)}) collective-permute-start(bf16[128,2048]{1,0:T(8,128)(2,1)S(1)} %pad_maximum_fusion.4.refs_8_), channel_id=1, source_target_pairs={{0,16},{16,0},{1,17},{17,1},{2,18},{18,2},{3,19},{19,3},{4,20},{20... | collective-permute-start | bytes 1572872 | tf_op jit(solution)/shard_map/ppermute | solution.py:233
  25.5 23.0 %collective-permute-start.4 = (bf16[64,2560]{1,0:T(8,128)(2,1)S(1)}, bf16[64,2560]{1,0:T(8,128)(2,1)S(1)}, u32[]{:S(2)}, u32[]{:S(2)}) collective-permute-start(bf16[64,2560]{1,0:T(8,128)(2,1)S(1)} %get-tuple-element.42.refs_0_), channel_id=1, source_target_pairs={{0,2},{2,0},{1,3},{3,1},{4,6},{6,4},{5,7},{7,5},{8,10},{10,8},{9,1... | collective-permute-start | bytes 983048 | tf_op jit(solution)/shard_map/ppermute | solution.py:41
  30.0 18.5 %collective-permute-start.5 = (bf16[64,2560]{1,0:T(8,128)(2,1)S(1)}, bf16[64,2560]{1,0:T(8,128)(2,1)S(1)}, u32[]{:S(2)}, u32[]{:S(2)}) collective-permute-start(bf16[64,2560]{1,0:T(8,128)(2,1)S(1)} %collective-permute-done.1.refs_1_), channel_id=1, source_target_pairs={{0,2},{2,0},{1,3},{3,1},{4,6},{6,4},{5,7},{7,5},{8,10},{10,8},{9,1... | collective-permute-start | bytes 983048 | tf_op jit(solution)/shard_map/ppermute | solution.py:41
  42.2 6.2 %collective-permute-start.6 = (bf16[64,2560]{1,0:T(8,128)(2,1)S(1)}, bf16[64,2560]{1,0:T(8,128)(2,1)S(1)}, u32[]{:S(2)}, u32[]{:S(2)}) collective-permute-start(bf16[64,2560]{1,0:T(8,128)(2,1)S(1)} %collective-permute-done.2.refs_2_), channel_id=1, source_target_pairs={{0,2},{2,0},{1,3},{3,1},{4,6},{6,4},{5,7},{7,5},{8,10},{10,8},{9,1... | collective-permute-start | bytes 983048 | tf_op jit(solution)/shard_map/ppermute | solution.py:41
  48.5 1.6 %collective-permute-start.7 = (bf16[64,2560]{1,0:T(8,128)(2,1)S(1)}, bf16[64,2560]{1,0:T(8,128)(2,1)S(1)}, u32[]{:S(2)}, u32[]{:S(2)}) collective-permute-start(bf16[64,2560]{1,0:T(8,128)(2,1)S(1)} %collective-permute-done.3.refs_3_), channel_id=1, source_target_pairs={{0,2},{2,0},{1,3},{3,1},{4,6},{6,4},{5,7},{7,5},{8,10},{10,8},{9,1... | collective-permute-start | bytes 983048 | tf_op jit(solution)/shard_map/ppermute | solution.py:41
  53.6 7.2 %collective-permute-start.12 = (bf16[2,64,256]{2,1,0:T(8,128)(2,1)S(1)}, bf16[2,64,256]{2,1,0:T(8,128)(2,1)S(1)}, u32[]{:S(2)}, u32[]{:S(2)}) collective-permute-start(bf16[2,64,256]{2,1,0:T(8,128)(2,1)S(1)} %get-tuple-element.14), channel_id=1, source_target_pairs={{0,4},{4,0},{8,12},{12,8},{1,5},{5,1},{9,13},{13,9},{2,6},{6,2},{1... | collective-permute-start | bytes 196616 | tf_op jit(solution)/shard_map/ppermute | solution.py:268
  54.8 6.0 %collective-permute-start.13 = (bf16[2,64,256]{2,1,0:T(8,128)(2,1)S(1)}, bf16[2,64,256]{2,1,0:T(8,128)(2,1)S(1)}, u32[]{:S(2)}, u32[]{:S(2)}) collective-permute-start(bf16[2,64,256]{2,1,0:T(8,128)(2,1)S(1)} %get-tuple-element.15), channel_id=1, source_target_pairs={{0,8},{4,12},{8,0},{12,4},{1,9},{5,13},{9,1},{13,5},{2,10},{6,14},... | collective-permute-start | bytes 196616 | tf_op jit(solution)/shard_map/ppermute | solution.py:268
  54.8 6.0 %collective-permute-start.14 = (bf16[2,64,256]{2,1,0:T(8,128)(2,1)S(1)}, bf16[2,64,256]{2,1,0:T(8,128)(2,1)S(1)}, u32[]{:S(2)}, u32[]{:S(2)}) collective-permute-start(bf16[2,64,256]{2,1,0:T(8,128)(2,1)S(1)} %get-tuple-element.16), channel_id=1, source_target_pairs={{0,12},{4,8},{8,4},{12,0},{1,13},{5,9},{9,5},{13,1},{2,14},{6,10},... | collective-permute-start | bytes 196616 | tf_op jit(solution)/shard_map/ppermute | solution.py:268
  57.2 32.3 %all-to-all-start.1 = ((bf16[8,32,2048]{2,1,0:T(8,128)(2,1)}), bf16[8,32,2048]{2,1,0:T(8,128)(2,1)S(1)}, u32[]{:S(2)}, u32[]{:S(2)}) async-start(bf16[8,32,2048]{2,1,0:T(8,128)(2,1)} %bitcast.14), calls=%async_computation.1 | async-start | bytes 2097152 | tf_op jit(solution)/shard_map/all_to_all | solution.py:275
  60.9 5.0 %collective-permute-start.15 = (f32[2,64,256]{2,1,0:T(8,128)S(1)}, f32[2,64,256]{2,1,0:T(8,128)S(1)}, u32[]{:S(2)}, u32[]{:S(2)}) collective-permute-start(f32[2,64,256]{2,1,0:T(8,128)S(1)} %convert_add_fusion), channel_id=1, source_target_pairs={{0,1},{1,0},{2,3},{3,2},{4,5},{5,4},{6,7},{7,6},{8,9},{9,8},{10,11... | collective-permute-start | bytes 393224 | tf_op jit(solution)/shard_map/ppermute | solution.py:36
  61.5 4.5 %collective-permute-start.18 = (f32[2048]{0:T(1024)S(1)}, f32[2048]{0:T(1024)S(1)}, u32[]{:S(2)}, u32[]{:S(2)}) collective-permute-start(f32[2048]{0:T(1024)S(1)} %bitcast.45), channel_id=1, source_target_pairs={{0,2},{2,0},{1,3},{3,1},{4,6},{6,4},{5,7},{7,5},{8,10},{10,8},{9,1... | collective-permute-start | bytes 24584 | tf_op jit(solution)/shard_map/ppermute | solution.py:41
  66.0 1.3 %collective-permute-start.16 = (bf16[64,256]{1,0:T(8,128)(2,1)S(1)}, bf16[64,256]{1,0:T(8,128)(2,1)S(1)}, u32[]{:S(2)}, u32[]{:S(2)}) collective-permute-start(bf16[64,256]{1,0:T(8,128)(2,1)S(1)} %get-tuple-element.38), channel_id=1, source_target_pairs={{0,2},{2,0},{1,3},{3,1},{4,6},{6,4},{5,7},{7,5},{8,10},{10,8},{9,1... | collective-permute-start | bytes 98312 | tf_op jit(solution)/shard_map/ppermute | solution.py:41
  67.7 1.3 %collective-permute-start.17 = (bf16[4,2,8,512]{3,2,1,0:T(8,128)(2,1)S(1)}, bf16[4,2,8,512]{3,2,1,0:T(8,128)(2,1)S(1)}, u32[]{:S(2)}, u32[]{:S(2)}) collective-permute-start(bf16[4,2,8,512]{3,2,1,0:T(8,128)(2,1)S(1)} %dynamic-slice_bitcast_fusion), channel_id=1, source_target_pairs={{0,2},{2,0},{1,3},{3,1},{4,6},{6,4},{5,7},{7,5},{8,10},{10,8},{9,1... | collective-permute-start | bytes 196616 | tf_op jit(solution)/shard_map/ppermute | solution.py:41
  69.1 21.0 %collective-permute-start.20 = (bf16[48,512]{1,0:T(8,128)(2,1)S(1)}, bf16[48,512]{1,0:T(8,128)(2,1)S(1)}, u32[]{:S(2)}, u32[]{:S(2)}) collective-permute-start(bf16[48,512]{1,0:T(8,128)(2,1)S(1)} %get-tuple-element.33), channel_id=1, source_target_pairs={{0,4},{2,22},{4,0},{6,18},{8,12},{10,30},{12,8},{14,26},{16,20},{1... | collective-permute-start | bytes 147464 | tf_op jit(solution)/shard_map/ppermute | solution.py:320
  71.2 19.0 %collective-permute-start.21 = (bf16[48,512]{1,0:T(8,128)(2,1)S(1)}, bf16[48,512]{1,0:T(8,128)(2,1)S(1)}, u32[]{:S(2)}, u32[]{:S(2)}) collective-permute-start(bf16[48,512]{1,0:T(8,128)(2,1)S(1)} %get-tuple-element.34), channel_id=1, source_target_pairs={{0,8},{2,26},{4,12},{6,30},{8,0},{10,18},{12,4},{14,22},{16,24},{1... | collective-permute-start | bytes 147464 | tf_op jit(solution)/shard_map/ppermute | solution.py:320
  72.7 18.1 %collective-permute-start.22 = (bf16[48,512]{1,0:T(8,128)(2,1)S(1)}, bf16[48,512]{1,0:T(8,128)(2,1)S(1)}, u32[]{:S(2)}, u32[]{:S(2)}) collective-permute-start(bf16[48,512]{1,0:T(8,128)(2,1)S(1)} %get-tuple-element.31), channel_id=1, source_target_pairs={{0,12},{2,30},{4,8},{6,26},{8,4},{10,22},{12,0},{14,18},{16,28},{1... | collective-permute-start | bytes 147464 | tf_op jit(solution)/shard_map/ppermute | solution.py:320
  89.5 1.3 %collective-permute-start.19 = (bf16[48,512]{1,0:T(8,128)(2,1)S(1)}, bf16[48,512]{1,0:T(8,128)(2,1)S(1)}, u32[]{:S(2)}, u32[]{:S(2)}) collective-permute-start(bf16[48,512]{1,0:T(8,128)(2,1)S(1)} %get-tuple-element.19), channel_id=1, source_target_pairs={{2,18},{6,22},{10,26},{14,30},{18,2},{22,6},{26,10},{30,14},{3,19}... | collective-permute-start | bytes 147464 | tf_op jit(solution)/shard_map/ppermute | solution.py:320
  90.2 3.2 %collective-permute-start.24 = (bf16[48,512]{1,0:T(8,128)(2,1)S(1)}, bf16[48,512]{1,0:T(8,128)(2,1)S(1)}, u32[]{:S(2)}, u32[]{:S(2)}) collective-permute-start(bf16[48,512]{1,0:T(8,128)(2,1)S(1)} %collective-permute-done.20.refs_1_), channel_id=1, source_target_pairs={{0,2},{2,0},{1,3},{3,1},{4,6},{6,4},{5,7},{7,5},{8,10},{10,8},{9,1... | collective-permute-start | bytes 147464 | tf_op jit(solution)/shard_map/ppermute | solution.py:41
  90.3 3.1 %collective-permute-start.25 = (bf16[48,512]{1,0:T(8,128)(2,1)S(1)}, bf16[48,512]{1,0:T(8,128)(2,1)S(1)}, u32[]{:S(2)}, u32[]{:S(2)}) collective-permute-start(bf16[48,512]{1,0:T(8,128)(2,1)S(1)} %collective-permute-done.21.refs_2_), channel_id=1, source_target_pairs={{0,2},{2,0},{1,3},{3,1},{4,6},{6,4},{5,7},{7,5},{8,10},{10,8},{9,1... | collective-permute-start | bytes 147464 | tf_op jit(solution)/shard_map/ppermute | solution.py:41
  90.8 2.6 %collective-permute-start.26 = (bf16[48,512]{1,0:T(8,128)(2,1)S(1)}, bf16[48,512]{1,0:T(8,128)(2,1)S(1)}, u32[]{:S(2)}, u32[]{:S(2)}) collective-permute-start(bf16[48,512]{1,0:T(8,128)(2,1)S(1)} %collective-permute-done.22.refs_3_), channel_id=1, source_target_pairs={{0,2},{2,0},{1,3},{3,1},{4,6},{6,4},{5,7},{7,5},{8,10},{10,8},{9,1... | collective-permute-start | bytes 147464 | tf_op jit(solution)/shard_map/ppermute | solution.py:41
  90.9 2.5 %collective-permute-start.23 = (bf16[48,512]{1,0:T(8,128)(2,1)S(1)}, bf16[48,512]{1,0:T(8,128)(2,1)S(1)}, u32[]{:S(2)}, u32[]{:S(2)}) collective-permute-start(bf16[48,512]{1,0:T(8,128)(2,1)S(1)} %broadcast_select_fusion.refs_0_), channel_id=1, source_target_pairs={{0,2},{2,0},{1,3},{3,1},{4,6},{6,4},{5,7},{7,5},{8,10},{10,8},{9,1... | collective-permute-start | bytes 147464 | tf_op jit(solution)/shard_map/ppermute | solution.py:41
